TPU v7x, 32 devices: a whole 2x2x4 slice. The times are simulated.
32 devices in a mesh: section: 2 (over y), dp: 16 (over z, x, core).
Axes of the slice: x: 2, y: 2, z: 4, core: 2. Of those that a mesh axis runs over, the one named last changes fastest.
Arguments:
- inputs: bfloat16 [8192, 1024], P('dp'), may hold values from -6 to 6
- out_grad: bfloat16 [8192, 1024], P('dp'), may hold values from -6 to 6
- doc_ids: int32 [32, 256], P('dp'), may hold values from 0 to 3, never falling along the last dimension, each value on 1 to 128 neighbouring positions
- row_live: int32 [32], P('dp'), may hold values from 64 to 256, as said below
- pre_gain: float32 [2, 1024], P('section'), may hold values from 0.5 to 1.5
- mlp_gain: float32 [2, 1024], P('section'), may hold values from 0.5 to 1.5
- mixer_gain: float32 [2, 1536], P('section'), may hold values from 0.5 to 1.5
- conv_weight: float32 [2, 4, 1792], P('section'), may hold values from -0.5 to 0.5
- conv_bias: float32 [2, 1792], P('section'), may hold values from -0.5 to 0.5
- step_bias: float32 [2, 24], P('section'), may hold values from -4 to -1
- decay_log: float32 [2, 24], P('section'), may hold values from -4 to 1
- skip_scale: float32 [2, 24], P('section'), may hold values from 0.5 to 1.5
- mixer_in_weight: bfloat16 [2, 1024, 3352], P('section', 'dp'), may hold values from -0.1875 to 0.1875
- mixer_out_weight: bfloat16 [2, 1536, 1024], P('section', None, 'dp'), may hold values from -0.15625 to 0.15625
- query_weight: bfloat16 [2, 1024, 512], P('section', 'dp'), may hold values from -0.1875 to 0.1875
- key_weight: bfloat16 [2, 1024, 128], P('section', 'dp'), may hold values from -0.1875 to 0.1875
- value_weight: bfloat16 [2, 1024, 128], P('section', 'dp'), may hold values from -0.1875 to 0.1875
- attend_weight: bfloat16 [2, 512, 1024], P('section', None, 'dp'), may hold values from -0.75 to 0.75
- gate_up_weight: bfloat16 [2, 1024, 4096], P('section', 'dp'), may hold values from -0.1875 to 0.1875
- down_weight: bfloat16 [2, 2048, 1024], P('section', None, 'dp'), may hold values from -0.125 to 0.125
Outputs:
- section_out: bfloat16 [2, 8192, 1024], P('section', 'dp')
- section_in_grad: float32 [2, 8192, 1024], P('section', 'dp')
- pre_gain_grad: float32 [2, 1024], P('section')
- mlp_gain_grad: float32 [2, 1024], P('section')
- mixer_gain_grad: float32 [2, 1536], P('section')
- conv_weight_grad: float32 [2, 4, 1792], P('section')
- conv_bias_grad: float32 [2, 1792], P('section')
- step_bias_grad: float32 [2, 24], P('section')
- decay_log_grad: float32 [2, 24], P('section')
- skip_scale_grad: float32 [2, 24], P('section')
- mixer_in_grad: float32 [2, 1024, 3352], P('section', 'dp')
- mixer_out_grad: float32 [2, 1536, 1024], P('section', None, 'dp')
- query_grad: float32 [2, 1024, 512], P('section', 'dp')
- key_grad: float32 [2, 1024, 128], P('section', 'dp')
- value_grad: float32 [2, 1024, 128], P('section', 'dp')
- attend_grad: float32 [2, 512, 1024], P('section', None, 'dp')
- gate_up_grad: float32 [2, 1024, 4096], P('section', 'dp')
- down_grad: float32 [2, 2048, 1024], P('section', None, 'dp')
Inputs may be any that keep to these rules, and one draw needn't show every extreme that they name: `doc_ids`: each row of 256 positions holds 4 documents in order, numbered from 0, each at most 128 positions long. The loss counts the first row_live positions of each row; some row is counted in full.
All inputs are finite; a program needn't handle non-finite values.
Results may differ from a plain program's by a relative error of at most 0.02.
Values may be sent and summed in bfloat16 or wider, within the bound.
No kernel may reach another device: no remote copies, remote signals or barrier semaphores. Data moves between devices by JAX's collectives and lax.ppermute only.
A program may use at most 320 MiB of HBM per device.

v0:
```python
import functools
import math

import jax
import jax.numpy as jnp
from jax import lax
from jax.experimental import pallas as pl
from jax.experimental.pallas import tpu as pltpu
from jax.sharding import Mesh
from jax.sharding import PartitionSpec as P

D = 1024
FF = 2048
MH = 24
MP = 64
NS = 128
AH = 8
KVH = 2
HD = 64
MB = 2
TOK = 256
E = 1536
CH = 1792
HALF = TOK // 2
PAIRS = MH // 2
LANES = 128
SIDE = D // 2
MIB = 2**20
FF_VMEM = 22
FB_VMEM = 20

AT_W = E
AT_Q = E + CH
AT_K = AT_Q + AH * HD
AT_V = AT_K + KVH * HD
AT_DT = AT_V + KVH * HD
WIDE_A = AT_DT + LANES
CUT_A = 16 * LANES
MIXED = E + AH * HD
AT_GU = MIXED
AT_DN = AT_GU + 2 * FF
WIDE_B = AT_DN + FF

highest = lax.Precision.HIGHEST
epsilon = 1e-05
rope_base = 100000000000.0
bf16 = jnp.bfloat16
f32 = jnp.float32


def dot_nn(left, right):
    return lax.dot_general(left, right, (((1,), (0,)), ((), ())), preferred_element_type=f32)


def dot_nt(left, right):
    return lax.dot_general(left, right, (((1,), (1,)), ((), ())), preferred_element_type=f32)


def dot_tn(left, right):
    return lax.dot_general(left, right, (((0,), (0,)), ((), ())), preferred_element_type=f32)


def dot_exact(left, right):
    return lax.dot_general(
        left, right, (((1,), (0,)), ((), ())), precision=highest, preferred_element_type=f32
    )


def softplus(value):
    return jnp.maximum(value, 0.0) + jnp.log1p(jnp.exp(-jnp.abs(value)))


def lane_low(rows):
    return lax.broadcasted_iota(jnp.int32, (rows, LANES), 1) < HD


def rope_halves(rows):
    return (lax.broadcasted_iota(jnp.int32, (rows, LANES), 1) & (HD - 1)) < HD // 2


def rope_turn(tile, cosine, sine):
    swapped = jnp.where(
        rope_halves(tile.shape[0]),
        -pltpu.roll(tile, LANES - HD // 2, 1),
        pltpu.roll(tile, HD // 2, 1),
    )
    return tile * cosine + swapped * sine


def rope_back(tile, cosine, sine):
    swapped = jnp.where(
        rope_halves(tile.shape[0]),
        pltpu.roll(tile, LANES - HD // 2, 1),
        -pltpu.roll(tile, HD // 2, 1),
    )
    return tile * cosine + swapped * sine


def both_halves(tile):
    swapped = pltpu.roll(tile, HD, 1)
    low = lane_low(tile.shape[0])
    return (jnp.where(low, tile, swapped), jnp.where(low, swapped, tile))


def tile_at(index):
    return pl.ds(pl.multiple_of(index * LANES, LANES), LANES)


def tile_from(start, index):
    return pl.ds(pl.multiple_of(start + index * LANES, LANES), LANES)


def allowed_pairs(doc_col_ref, doc_row_ref):
    later = lax.broadcasted_iota(jnp.int32, (TOK, TOK), 0)
    early = lax.broadcasted_iota(jnp.int32, (TOK, TOK), 1)
    same = doc_col_ref[:, 0:1] == doc_row_ref[0:1, :]
    return (later >= early) & same


def pair_rows(tile):
    low = lane_low(tile.shape[0])
    zero = jnp.zeros_like(tile)
    return jnp.concatenate([jnp.where(low, tile, zero), jnp.where(low, zero, tile)], axis=0)


def pair_lanes(rows):
    half = rows.shape[0] // 2
    return jnp.where(lane_low(half), rows[:half], rows[half:])


def core_forward_kernel(
    held, pm_ref, pq_ref, pd_ref, rope_ref, mask_ref, doc_col_ref, doc_row_ref,
    taps_ref, head_ref, wide_ref, *refs,
):
    xb_ref, pre_ref, yns_ref, conv_s, cb_s, bias_s, sum_s = refs[3:] if held else refs

    def conv_tile(index, carry):
        rows = pm_ref[:, tile_from(AT_W, index)].astype(f32)
        at = tile_at(index)
        total = taps_ref[4:5, at] + taps_ref[3:4, at] * rows
        for shift in (1, 2, 3):
            moved = mask_ref[:, (shift - 1) * LANES : shift * LANES] * pltpu.roll(rows, shift, 0)
            total = total + taps_ref[3 - shift : 4 - shift, at] * moved
        total = total.astype(bf16)
        pre_ref[:, at] = total
        total = total.astype(f32)
        conv_s[:, at] = total * jax.nn.sigmoid(total)
        return carry

    lax.fori_loop(0, CH // LANES, conv_tile, 0)

    allowed = allowed_pairs(doc_col_ref, doc_row_ref)
    bias_s[...] = jnp.where(allowed, 0.0, -1e30)
    steps = softplus(pd_ref[...] + head_ref[0:1, :])
    rates = -steps * head_ref[1:2, :]
    totals = dot_exact(jnp.where(allowed, 1.0, 0.0), rates)
    totals_t = totals.T
    inward = conv_s[:, E : E + NS].astype(bf16)
    outward = conv_s[:, E + NS :].astype(bf16)
    cb_s[...] = jnp.where(allowed, dot_nt(outward, inward), 0.0)
    low = lane_low(TOK)
    for pair in range(PAIRS):
        lanes = slice(pair * LANES, (pair + 1) * LANES)
        first = 2 * pair
        step_pair = jnp.where(low, steps[:, first : first + 1], steps[:, first + 1 : first + 2])
        scaled = (conv_s[:, lanes] * step_pair).astype(bf16)
        mixes = []
        for head in (first, first + 1):
            apart = totals[:, head : head + 1] - totals_t[head : head + 1, :]
            mixes.append((jnp.exp(jnp.minimum(apart, 0.0)) * cb_s[...]).astype(bf16))
        yns_ref[:, lanes] = pair_lanes(dot_nn(jnp.concatenate(mixes, axis=0), scaled))

    sum_s[...] = jnp.zeros((TOK, LANES), f32)

    def gate_tile(index, carry):
        at = tile_at(index)
        gate = pm_ref[:, at].astype(f32)
        rows = yns_ref[:, at] + wide_ref[0:1, at] * conv_s[:, at]
        gated = rows * (gate * jax.nn.sigmoid(gate))
        sum_s[...] += gated * gated
        conv_s[:, at] = gated
        return carry

    lax.fori_loop(0, E // LANES, gate_tile, 0)
    scale = lax.rsqrt(jnp.sum(sum_s[...], axis=1, keepdims=True) * (1.0 / E) + epsilon)

    def norm_tile(index, carry):
        at = tile_at(index)
        xb_ref[:, at] = (conv_s[:, at] * scale * wide_ref[1:2, at]).astype(bf16)
        return carry

    lax.fori_loop(0, E // LANES, norm_tile, 0)

    cosine = rope_ref[:, :LANES]
    sine = rope_ref[:, LANES:]
    keys = both_halves(rope_turn(pq_ref[:, AH * HD : AH * HD + LANES].astype(f32), cosine, sine))
    values = both_halves(pq_ref[:, AH * HD + LANES :].astype(f32))
    keys = tuple(part.astype(bf16) for part in keys)
    values = tuple(part.astype(bf16) for part in values)
    for pair in range(AH // 2):
        group = pair // (AH // (2 * KVH))
        at = pair * LANES
        turned = rope_turn(pq_ref[:, at : at + LANES].astype(f32), cosine, sine)
        scores = dot_nt(pair_rows((turned * (1.0 / math.sqrt(HD))).astype(bf16)), keys[group])
        weights = []
        shares = []
        for part in (scores[:TOK], scores[TOK:]):
            part = part + bias_s[...]
            part = jnp.exp(part - jnp.max(part, axis=1, keepdims=True))
            shares.append(1.0 / jnp.sum(part, axis=1, keepdims=True))
            weights.append(part.astype(bf16))
        out = pair_lanes(dot_nn(jnp.concatenate(weights, axis=0), values[group]))
        out = out * jnp.where(low, shares[0], shares[1])
        xb_ref[:, E + pair * LANES : E + (pair + 1) * LANES] = out.astype(bf16)


def silu_slope(value, gate):
    return gate * (1.0 + value * (1.0 - gate))


def attend_back_kernel(
    pick_ref, pq_ref, dxb_ref, rope_ref, doc_col_ref, doc_row_ref, pg_ref, bias_s
):
    later = lax.broadcasted_iota(jnp.int32, (TOK, TOK), 1)
    early = lax.broadcasted_iota(jnp.int32, (TOK, TOK), 0)
    allowed_t = (later >= early) & (doc_col_ref[:, 0:1] == doc_row_ref[0:1, :])
    bias_s[...] = jnp.where(allowed_t, 0.0, -1e30)
    low = lane_low(TOK)
    cosine = rope_ref[:, :LANES]
    sine = rope_ref[:, LANES:]
    keys = both_halves(rope_turn(pq_ref[:, AH * HD : AH * HD + LANES].astype(f32), cosine, sine))
    values = both_halves(pq_ref[:, AH * HD + LANES :].astype(f32))
    root = 1.0 / math.sqrt(HD)
    d_keys = []
    d_values = []
    for group in range(KVH):
        key = keys[group].astype(bf16)
        key_rows = pair_rows(key)
        value_rows = pair_rows(values[group].astype(bf16))
        d_key = jnp.zeros((TOK, LANES), f32)
        d_value = jnp.zeros((TOK, LANES), f32)
        for pair in range(group * (AH // (2 * KVH)), (group + 1) * (AH // (2 * KVH))):
            at = pair * LANES
            turned = rope_turn(pq_ref[:, at : at + LANES].astype(f32), cosine, sine) * root
            query = turned.astype(bf16)
            d_out = dxb_ref[:, E + at : E + at + LANES].astype(bf16)
            scores = dot_nt(key_rows, query)
            d_weights = dot_nt(value_rows, d_out)
            weights = []
            d_scores = []
            for part in (slice(0, TOK), slice(TOK, 2 * TOK)):
                score = scores[part] + bias_s[...]
                weight = jnp.exp(score - jnp.max(score, axis=0, keepdims=True))
                weight = weight * (1.0 / jnp.sum(weight, axis=0, keepdims=True))
                d_weight = d_weights[part]
                offset = jnp.sum(weight * d_weight, axis=0, keepdims=True)
                weights.append(weight.astype(bf16))
                d_scores.append((weight * (d_weight - offset)).astype(bf16))
            d_value = d_value + pair_lanes(dot_nn(jnp.concatenate(weights, axis=0), d_out))
            d_key = d_key + pair_lanes(dot_nn(jnp.concatenate(d_scores, axis=0), query))
            d_query = pair_lanes(dot_tn(jnp.concatenate(d_scores, axis=1), key))
            pg_ref[:, at : at + LANES] = rope_back(d_query * root, cosine, sine).astype(bf16)
        d_keys.append(d_key + pltpu.roll(d_key, HD, 1))
        d_values.append(d_value + pltpu.roll(d_value, HD, 1))
    d_key = rope_back(jnp.where(low, d_keys[0], d_keys[1]), cosine, sine)
    pg_ref[:, AH * HD : AH * HD + LANES] = d_key.astype(bf16)
    pg_ref[:, AH * HD + LANES :] = jnp.where(low, d_values[0], d_values[1]).astype(bf16)


def mixer_back_kernel(
    pick_ref, pm_ref, pd_ref, pre_ref, yns_ref, dxb_ref, attend_ref, mask_ref, doc_col_ref,
    doc_row_ref, taps_ref, head_ref, wide_ref,
    pg_ref, small_ref,
    x_s, dx_s, dyb_s, cbt_s, dcbt_s, sum_s, ssum_s,
):
    small_ref[...] = jnp.zeros_like(small_ref)
    pg_ref[:, AT_Q:AT_DT] = attend_ref[...]
    sum_s[...] = jnp.zeros((TOK, LANES), f32)
    ssum_s[...] = jnp.zeros((TOK, LANES), f32)

    def start_tile(index, carry):
        at = tile_at(index)
        pre = pre_ref[:, at].astype(f32)
        heads_in = pre * jax.nn.sigmoid(pre)
        x_s[:, at] = heads_in
        gate = pm_ref[:, at].astype(f32)
        rows = yns_ref[:, at] + wide_ref[0:1, at] * heads_in
        gated = rows * (gate * jax.nn.sigmoid(gate))
        sum_s[...] += gated * gated
        ssum_s[...] += dxb_ref[:, at] * wide_ref[1:2, at] * gated
        return carry

    lax.fori_loop(0, E // LANES, start_tile, 0)
    scale = lax.rsqrt(jnp.sum(sum_s[...], axis=1, keepdims=True) * (1.0 / E) + epsilon)
    pull = jnp.sum(ssum_s[...], axis=1, keepdims=True) * (1.0 / E) * scale * scale * scale

    def gate_tile(index, carry):
        at = tile_at(index)
        heads_in = x_s[:, at]
        skip = wide_ref[0:1, at]
        gate = pm_ref[:, at].astype(f32)
        opened = jax.nn.sigmoid(gate)
        rows = yns_ref[:, at] + skip * heads_in
        gated = rows * (gate * opened)
        arrived = dxb_ref[:, at]
        d_gated = scale * (arrived * wide_ref[1:2, at]) - gated * pull
        small_ref[5:6, at] = jnp.sum(arrived * gated * scale, axis=0, keepdims=True)
        d_rows = d_gated * (gate * opened)
        pg_ref[:, at] = (d_gated * rows * silu_slope(gate, opened)).astype(bf16)
        small_ref[6:7, at] = jnp.sum(d_rows * heads_in, axis=0, keepdims=True)
        dyb_s[:, at] = d_rows.astype(bf16)
        dx_s[:, at] = skip * d_rows
        return carry

    lax.fori_loop(0, E // LANES, gate_tile, 0)

    def state_tile(index, carry):
        at = tile_from(E, index)
        pre = pre_ref[:, at].astype(f32)
        x_s[:, at] = pre * jax.nn.sigmoid(pre)
        return carry

    lax.fori_loop(0, 2, state_tile, 0)

    later = lax.broadcasted_iota(jnp.int32, (TOK, TOK), 1)
    early = lax.broadcasted_iota(jnp.int32, (TOK, TOK), 0)
    allowed_t = (later >= early) & (doc_col_ref[:, 0:1] == doc_row_ref[0:1, :])
    allowed = allowed_pairs(doc_col_ref, doc_row_ref)
    raw = pd_ref[...] + head_ref[0:1, :]
    steps = softplus(raw)
    decay = head_ref[1:2, :]
    rates = -steps * decay
    totals = dot_exact(jnp.where(allowed, 1.0, 0.0), rates)
    totals_t = totals.T
    inward = x_s[:, E : E + NS].astype(bf16)
    outward = x_s[:, E + NS :].astype(bf16)
    cbt_s[...] = jnp.where(allowed_t, dot_nt(inward, outward), 0.0)
    dcbt_s[...] = jnp.zeros((TOK, TOK), f32)
    low = lane_low(TOK)
    spread_row = lax.broadcasted_iota(jnp.int32, (2 * LANES, LANES), 0) // HD
    spread_col = lax.broadcasted_iota(jnp.int32, (2 * LANES, LANES), 1)
    sum_s[...] = jnp.zeros((TOK, LANES), f32)
    ssum_s[...] = jnp.zeros((TOK, LANES), f32)
    waiting = None
    for pair in range(PAIRS):
        lanes = slice(pair * LANES, (pair + 1) * LANES)
        first = 2 * pair
        step_pair = jnp.where(low, steps[:, first : first + 1], steps[:, first + 1 : first + 2])
        heads_in = x_s[:, lanes]
        scaled = (heads_in * step_pair).astype(bf16)
        d_rows = dyb_s[:, lanes]
        d_mix = dot_nt(pair_rows(scaled), d_rows)
        mixes = []
        d_pairs = None
        for side, head in enumerate((first, first + 1)):
            apart = totals_t[head : head + 1, :] - totals[:, head : head + 1]
            decays = jnp.exp(jnp.minimum(apart, 0.0))
            mixes.append((decays * cbt_s[...]).astype(bf16))
            part = d_mix[side * TOK : (side + 1) * TOK] * decays
            d_pairs = part if d_pairs is None else d_pairs + part
        dcbt_s[...] += d_pairs
        d_scaled = pair_lanes(dot_nn(jnp.concatenate(mixes, axis=0), d_rows))
        dx_s[:, lanes] += d_scaled * step_pair
        value = d_rows.astype(f32) * yns_ref[:, lanes] - scaled.astype(f32) * d_scaled
        coarse = value.astype(bf16)
        fine = (value - coarse.astype(f32)).astype(bf16)
        spread = (spread_col == first + (spread_row & 1)).astype(bf16)
        ssum_s[...] += dot_nn(jnp.concatenate([coarse, fine], axis=1), spread)
        value = (d_scaled * heads_in).astype(bf16)
        if pair % 2 == 0:
            waiting = value
        else:
            spread = (spread_col == first - 2 + spread_row).astype(bf16)
            sum_s[...] += dot_nn(jnp.concatenate([waiting, value], axis=1), spread)

    d_rates = dot_exact(jnp.where(allowed_t, 1.0, 0.0), ssum_s[...])
    d_steps = sum_s[...] - decay * d_rates
    d_raw = d_steps * jax.nn.sigmoid(raw)
    pg_ref[:, AT_DT:] = d_raw.astype(bf16)
    small_ref[7:8, :LANES] = jnp.sum(d_raw, axis=0, keepdims=True)
    small_ref[7:8, LANES : 2 * LANES] = jnp.sum(d_rates * rates, axis=0, keepdims=True)
    d_pairs = jnp.where(allowed_t, dcbt_s[...], 0.0).astype(bf16)
    dx_s[:, E : E + NS] = dot_nn(d_pairs, outward)
    dx_s[:, E + NS :] = dot_tn(d_pairs, inward)

    def conv_tile(index, carry):
        at = tile_at(index)
        pre = pre_ref[:, at].astype(f32)
        d_pre = dx_s[:, at] * silu_slope(pre, jax.nn.sigmoid(pre))
        rows = pm_ref[:, tile_from(AT_W, index)].astype(f32)
        small_ref[4:5, at] = jnp.sum(d_pre, axis=0, keepdims=True)
        small_ref[3:4, at] = jnp.sum(d_pre * rows, axis=0, keepdims=True)
        back = taps_ref[3:4, at] * d_pre
        for shift in (1, 2, 3):
            held = mask_ref[:, (shift - 1) * LANES : shift * LANES] * d_pre
            small_ref[3 - shift : 4 - shift, at] = jnp.sum(
                held * pltpu.roll(rows, shift, 0), axis=0, keepdims=True
            )
            back = back + taps_ref[3 - shift : 4 - shift, at] * pltpu.roll(held, TOK - shift, 0)
        pg_ref[:, tile_from(AT_W, index)] = back.astype(bf16)
        return carry

    lax.fori_loop(0, CH // LANES, conv_tile, 0)


def whole_block(shape):
    return pl.BlockSpec(shape, lambda *steps: (0,) * len(shape))


def once(shape, place):
    return pl.BlockSpec(shape, place, pipeline_mode=pl.Buffered(1))


def core_forward(row, projected, layout, params, held=()):
    operands = (*projected, *layout)

    def block(array):
        return once((None,) + array.shape[1:], lambda step: (row, 0, 0))

    outs = [
        jax.ShapeDtypeStruct((MB, TOK, MIXED), bf16),
        jax.ShapeDtypeStruct((MB, TOK, CH), bf16),
        jax.ShapeDtypeStruct((MB, TOK, E), f32),
    ]
    return pl.pallas_call(
        functools.partial(core_forward_kernel, bool(held)),
        grid=(1,),
        in_specs=[block(array) for array in operands]
        + [once(array.shape, lambda step: (0, 0)) for array in params]
        + [pl.BlockSpec(memory_space=pl.ANY)] * len(held),
        out_specs=[block(array) for array in outs],
        out_shape=outs,
        scratch_shapes=[
            pltpu.VMEM((TOK, CH), f32),
            pltpu.VMEM((TOK, TOK), f32),
            pltpu.VMEM((TOK, TOK), f32),
            pltpu.VMEM((TOK, LANES), f32),
        ],
        input_output_aliases={10: 0, 11: 1, 12: 2} if held else {},
        compiler_params=pltpu.CompilerParams(vmem_limit_bytes=12 * MIB),
        cost_estimate=pl.CostEstimate(
            flops=4 * 10**8, bytes_accessed=12 * 2**20, transcendentals=10**6
        ),
        name="core_forward",
    )(*operands, *params, *held)


def core_back_specs(by_row, plain):
    return [
        once((None,) + array.shape[1:], lambda step, pick: (pick[0], 0, 0)) if chosen
        else once(array.shape, lambda step, pick: (0, 0))
        for chosen, arrays in ((True, by_row), (False, plain))
        for array in arrays
    ]


def attend_back(row, projected, d_mixed, layout):
    rope, masks, doc_cols, doc_rows = layout
    return pl.pallas_call(
        attend_back_kernel,
        grid_spec=pltpu.PrefetchScalarGridSpec(
            num_scalar_prefetch=1,
            grid=(1,),
            in_specs=core_back_specs([projected[1]], [d_mixed])
            + core_back_specs([rope, doc_cols, doc_rows], []),
            out_specs=once((TOK, AT_DT - AT_Q), lambda step, pick: (0, 0)),
            scratch_shapes=[pltpu.VMEM((TOK, TOK), f32)],
        ),
        out_shape=jax.ShapeDtypeStruct((TOK, AT_DT - AT_Q), bf16),
        compiler_params=pltpu.CompilerParams(vmem_limit_bytes=6 * MIB),
        cost_estimate=pl.CostEstimate(
            flops=3 * 10**8, bytes_accessed=4 * 2**20, transcendentals=6 * 10**5
        ),
        name="attend_back",
    )(row, projected[1], d_mixed, rope, doc_cols, doc_rows)


def mixer_back(row, projected, pre, yns, d_mixed, attended, layout, params):
    rope, masks, doc_cols, doc_rows = layout
    return pl.pallas_call(
        mixer_back_kernel,
        grid_spec=pltpu.PrefetchScalarGridSpec(
            num_scalar_prefetch=1,
            grid=(1,),
            in_specs=core_back_specs(
                [projected[0], projected[2], pre, yns], [d_mixed, attended]
            )
            + core_back_specs([masks, doc_cols, doc_rows], params),
            out_specs=[
                once((TOK, WIDE_A), lambda step, pick: (0, 0)),
                once((8, CH), lambda step, pick: (0, 0)),
            ],
            scratch_shapes=[
                pltpu.VMEM((TOK, CH), f32),
                pltpu.VMEM((TOK, CH), f32),
                pltpu.VMEM((TOK, E), bf16),
                pltpu.VMEM((TOK, TOK), f32),
                pltpu.VMEM((TOK, TOK), f32),
                pltpu.VMEM((TOK, LANES), f32),
                pltpu.VMEM((TOK, LANES), f32),
            ],
        ),
        out_shape=[
            jax.ShapeDtypeStruct((TOK, WIDE_A), bf16),
            jax.ShapeDtypeStruct((8, CH), f32),
        ],
        compiler_params=pltpu.CompilerParams(vmem_limit_bytes=15 * MIB),
        cost_estimate=pl.CostEstimate(
            flops=7 * 10**8, bytes_accessed=10 * 2**20, transcendentals=15 * 10**5
        ),
        name="mixer_back",
    )(
        row, projected[0], projected[2], pre, yns, d_mixed, attended, masks, doc_cols, doc_rows,
        *params,
    )


def passed_along(value, axis, steps):
    count = lax.axis_size(axis)
    leading, last = (max(0, -steps), min(count, count - steps))
    return lax.ppermute(value, axis, [(source, source + steps) for source in range(leading, last)])


def norm_rows(values):
    return lax.rsqrt(jnp.mean(values * values, axis=-1, keepdims=True) + epsilon)


def norm_back(values, gain, arrived):
    scale = norm_rows(values)
    weighted = arrived * gain
    pull = jnp.mean(weighted * values, axis=-1, keepdims=True) * scale * scale * scale
    gain_grad = jnp.sum(arrived * values * scale, axis=0, keepdims=True)
    return (weighted * scale - values * pull, gain_grad)


def project_kernel(rows_ref, gain_ref, own_ref, other_ref, *refs):
    normed_ref, pm_ref, pq_ref, pd_ref = refs[-4:]
    step = pl.program_id(0)

    @pl.when(step == 0)
    def _():
        rows = rows_ref[...].astype(f32)
        normed_ref[...] = (rows * norm_rows(rows) * gain_ref[...]).astype(bf16)

    out = dot_nn(normed_ref[:, :SIDE], own_ref[...]) + dot_nn(normed_ref[:, SIDE:], other_ref[...])
    tile = WIDE_A // 3
    for index in range(2):
        @pl.when(step == index)
        def _(index=index):
            pm_ref[:, index * tile : (index + 1) * tile] = out.astype(bf16)

    @pl.when(step == 2)
    def _():
        pm_ref[:, 2 * tile :] = out[:, : AT_Q - 2 * tile].astype(bf16)
        pq_ref[...] = out[:, AT_Q - 2 * tile : AT_DT - 2 * tile].astype(bf16)
        pd_ref[...] = out[:, AT_DT - 2 * tile :]


def project(rows, gain, own, other, row=None, held=()):
    count = rows.shape[0]
    tile = WIDE_A // 3
    weight = pl.BlockSpec((SIDE, tile), lambda step: (0, step))
    at = row or 0
    total = count if row is None else MB * TOK
    widths = ((D, bf16), (AT_Q, bf16), (AT_DT - AT_Q, bf16), (LANES, f32))
    return pl.pallas_call(
        project_kernel,
        grid=(3,),
        in_specs=[whole_block((count, D)), whole_block((1, D)), weight, weight]
        + [pl.BlockSpec(memory_space=pl.ANY)] * len(held),
        out_specs=[pl.BlockSpec((count, width), lambda step: (at, 0)) for width, _ in widths],
        out_shape=[jax.ShapeDtypeStruct((total, width), kind) for width, kind in widths],
        input_output_aliases={4 + index: index for index in range(len(held))},
        compiler_params=pltpu.CompilerParams(vmem_limit_bytes=15 * MIB),
        cost_estimate=pl.CostEstimate(
            flops=2 * count * D * WIDE_A,
            bytes_accessed=2 * D * WIDE_A + 2 * count * WIDE_A,
            transcendentals=0,
        ),
        name="project",
    )(rows, gain, own, other, *held)


def by_row(projected):
    return tuple(array.reshape(MB, TOK, -1) for array in projected[1:])


def feed_forward_kernel(
    keep, rows_ref, mixed_ref, gain_ref,
    out_own, out_other, gate_own, gate_other, up_own, up_other, down_own, down_other,
    *refs,
):
    if keep:
        low_ref, middle_ref, normed_ref, gate_ref, up_ref, act_ref, total_s = refs[-7:]
    else:
        low_ref, middle_ref, normed_ref, total_s = refs
    step = pl.program_id(0)

    @pl.when(step == 0)
    def _():
        middle_ref[...] = rows_ref[...].astype(f32)

    @pl.when(step < 4)
    def _():
        mixed = mixed_ref[...]
        middle_ref[:, :SIDE] += dot_nt(mixed, out_own[...])
        middle_ref[:, SIDE:] += dot_nt(mixed, out_other[...])

    @pl.when(step == 3)
    def _():
        middle = middle_ref[...]
        normed_ref[...] = (middle * norm_rows(middle) * gain_ref[...]).astype(bf16)
        total_s[...] = middle

    @pl.when(step >= 4)
    def _():
        left = normed_ref[:, :SIDE]
        right = normed_ref[:, SIDE:]
        gate = dot_nn(left, gate_own[...]) + dot_nn(right, gate_other[...])
        up = dot_nn(left, up_own[...]) + dot_nn(right, up_other[...])
        act = (gate * jax.nn.sigmoid(gate) * up).astype(bf16)
        if keep:
            gate_ref[...] = gate.astype(bf16)
            up_ref[...] = up.astype(bf16)
            act_ref[...] = act
        total_s[:, :SIDE] += dot_nt(act, down_own[...])
        total_s[:, SIDE:] += dot_nt(act, down_other[...])

    @pl.when(step == 7)
    def _():
        low_ref[...] = total_s[...].astype(bf16)


def pinned(own, other):
    return [
        pltpu.with_memory_space_constraint(own, pltpu.VMEM),
        pltpu.with_memory_space_constraint(other, pltpu.HBM),
    ]


def b_block(start, skipped):
    return pl.BlockSpec(
        (SIDE, 512), lambda step, *pick: (0, start + jnp.clip(step - skipped, 0, 3))
    )


def b_blocks(parts):
    return [b_block(start, skipped) for start, skipped in parts for _ in range(2)]


def feed_forward(row, rows, mixed, gain, own, other, held=None):
    keep = held is not None
    at = row if rows.shape[0] > TOK else 0

    def late(step):
        return (row, jnp.clip(step - 4, 0, 3))

    wide = pl.BlockSpec((TOK, 512), late)
    full = pl.BlockSpec((TOK, D), lambda step: (row, 0))
    scratch = [pltpu.VMEM((TOK, D), f32)]
    if keep:
        out_specs = [full, full, full, wide, wide, wide]
        out_shape = [
            jax.ShapeDtypeStruct((MB * TOK, width), kind)
            for width, kind in ((D, bf16), (D, f32), (D, bf16), (FF, bf16), (FF, bf16), (FF, bf16))
        ]
    else:
        out_specs = [whole_block((TOK, D))]
        out_shape = [jax.ShapeDtypeStruct((TOK, D), bf16)]
        scratch = [pltpu.VMEM((TOK, D), f32), pltpu.VMEM((TOK, D), bf16)] + scratch
    held = tuple(held or ())
    return pl.pallas_call(
        functools.partial(feed_forward_kernel, keep),
        grid=(8,),
        in_specs=[
            pl.BlockSpec((TOK, D), lambda step: (at, 0)),
            pl.BlockSpec((TOK, 512), lambda step: (row, jnp.clip(step, 0, 3))),
            whole_block((1, D)),
        ]
        + b_blocks(((0, 0), (4, 4), (8, 4), (12, 4)))
        + [pl.BlockSpec(memory_space=pl.ANY)] * len(held),
        out_specs=out_specs,
        out_shape=out_shape,
        scratch_shapes=scratch,
        input_output_aliases={11 + index: index for index in range(len(held))},
        compiler_params=pltpu.CompilerParams(vmem_limit_bytes=(FF_VMEM if keep else 18) * MIB),
        cost_estimate=pl.CostEstimate(
            flops=2 * TOK * D * WIDE_B, bytes_accessed=2 * D * WIDE_B, transcendentals=0
        ),
        name="feed_forward",
    )(rows, mixed, gain, *((pinned(own, other) if keep else [own, other]) * 4), *held)


def feed_back_kernel(
    pick_ref, cot_ref, gate_ref, up_ref, middle_ref, gain_ref,
    down_own, down_other, gate_own, gate_other, up_own, up_other, out_own, out_other,
    d_gate_ref, d_up_ref, d_middle_ref, low_ref, d_mixed_ref, gain_grad_ref,
    total_s,
):
    step = pl.program_id(0)

    @pl.when(step == 0)
    def _():
        total_s[...] = jnp.zeros_like(total_s)

    @pl.when(step < 4)
    def _():
        arrived = dot_nn(cot_ref[:, :SIDE], down_own[...]) + dot_nn(
            cot_ref[:, SIDE:], down_other[...]
        )
        gate = gate_ref[...].astype(f32)
        opened = jax.nn.sigmoid(gate)
        d_gate = (arrived * up_ref[...].astype(f32) * silu_slope(gate, opened)).astype(bf16)
        d_up = (arrived * (gate * opened)).astype(bf16)
        d_gate_ref[...] = d_gate
        d_up_ref[...] = d_up
        total_s[:, :SIDE] += dot_nt(d_gate, gate_own[...]) + dot_nt(d_up, up_own[...])
        total_s[:, SIDE:] += dot_nt(d_gate, gate_other[...]) + dot_nt(d_up, up_other[...])

    @pl.when(step == 3)
    def _():
        d_norm, gain_grad = norm_back(middle_ref[...], gain_ref[...], total_s[...])
        d_middle = cot_ref[...].astype(f32) + d_norm
        d_middle_ref[...] = d_middle
        low_ref[...] = d_middle.astype(bf16)
        gain_grad_ref[...] = gain_grad

    @pl.when(step >= 4)
    def _():
        d_mixed_ref[...] = dot_nn(low_ref[:, :SIDE], out_own[...]) + dot_nn(
            low_ref[:, SIDE:], out_other[...]
        )


def feed_back(row, cotangent, gate, up, middle, gain, own, other):
    saved = pl.BlockSpec((TOK, 512), lambda step, pick: (pick[0], jnp.clip(step, 0, 3)))
    early = pl.BlockSpec((TOK, 512), lambda step, pick: (0, jnp.clip(step, 0, 3)))
    late = pl.BlockSpec((TOK, 512), lambda step, pick: (0, jnp.clip(step - 4, 0, 3)))
    full = pl.BlockSpec((TOK, D), lambda step, pick: (0, 0))
    gain_block = pl.BlockSpec((1, D), lambda step, pick: (0, 0))
    return pl.pallas_call(
        feed_back_kernel,
        grid_spec=pltpu.PrefetchScalarGridSpec(
            num_scalar_prefetch=1,
            grid=(8,),
            in_specs=[
                full,
                saved,
                saved,
                pl.BlockSpec((TOK, D), lambda step, pick: (pick[0], 0)),
                gain_block,
            ]
            + b_blocks(((12, 0), (4, 0), (8, 0), (0, 4))),
            out_specs=[early, early, full, full, late, gain_block],
            scratch_shapes=[pltpu.VMEM((TOK, D), f32)],
        ),
        out_shape=[
            jax.ShapeDtypeStruct((TOK, FF), bf16),
            jax.ShapeDtypeStruct((TOK, FF), bf16),
            jax.ShapeDtypeStruct((TOK, D), f32),
            jax.ShapeDtypeStruct((TOK, D), bf16),
            jax.ShapeDtypeStruct((TOK, MIXED), f32),
            jax.ShapeDtypeStruct((1, D), f32),
        ],
        compiler_params=pltpu.CompilerParams(vmem_limit_bytes=FB_VMEM * MIB),
        cost_estimate=pl.CostEstimate(
            flops=2 * TOK * D * WIDE_B, bytes_accessed=2 * D * WIDE_B, transcendentals=0
        ),
        name="feed_back",
    )(
        row, cotangent, *(pltpu.with_memory_space_constraint(one, pltpu.HBM) for one in (gate, up)),
        middle, gain, *(pinned(own, other) * 4),
    )


def project_back_kernel(
    pick_ref, grad_ref, rows_ref, d_middle_ref, gain_ref, own_ref, other_ref,
    d_rows_ref, low_ref, gain_grad_ref, total_s,
):
    step = pl.program_id(0)

    @pl.when(step == 0)
    def _():
        total_s[...] = jnp.zeros_like(total_s)

    total_s[:, :SIDE] += dot_nt(grad_ref[...], own_ref[...])
    total_s[:, SIDE:] += dot_nt(grad_ref[...], other_ref[...])

    @pl.when(step == 2)
    def _():
        d_norm, gain_grad = norm_back(rows_ref[...].astype(f32), gain_ref[...], total_s[...])
        d_rows = d_middle_ref[...] + d_norm
        d_rows_ref[...] = d_rows
        low_ref[...] = d_rows.astype(bf16)
        gain_grad_ref[...] = gain_grad


def project_back(row, proj_low, start_rows, d_middle, gain, own, other):
    tile = WIDE_A // 3
    weight = pl.BlockSpec((SIDE, tile), lambda step, pick: (0, step))
    full = pl.BlockSpec((TOK, D), lambda step, pick: (0, 0))
    gain_block = pl.BlockSpec((1, D), lambda step, pick: (0, 0))
    return pl.pallas_call(
        project_back_kernel,
        grid_spec=pltpu.PrefetchScalarGridSpec(
            num_scalar_prefetch=1,
            grid=(3,),
            in_specs=[
                pl.BlockSpec((TOK, tile), lambda step, pick: (0, step)),
                pl.BlockSpec((TOK, D), lambda step, pick: (pick[0], 0)),
                full,
                gain_block,
                weight,
                weight,
            ],
            out_specs=[full, full, gain_block],
            scratch_shapes=[pltpu.VMEM((TOK, D), f32)],
        ),
        out_shape=[
            jax.ShapeDtypeStruct((TOK, D), f32),
            jax.ShapeDtypeStruct((TOK, D), bf16),
            jax.ShapeDtypeStruct((1, D), f32),
        ],
        compiler_params=pltpu.CompilerParams(vmem_limit_bytes=15 * MIB),
        cost_estimate=pl.CostEstimate(
            flops=2 * TOK * D * WIDE_A, bytes_accessed=2 * D * WIDE_A, transcendentals=0
        ),
        name="project_back",
    )(row, proj_low, start_rows, d_middle, gain, own, other)


def weight_grad_kernel(groups, pick_ref, *refs):
    lefts = refs[: 4 * len(groups)]
    rights = refs[4 * len(groups) : 8 * len(groups)]
    sum_ref, left_s = refs[8 * len(groups) :]
    step = pl.program_id(0)
    for index, (start, count) in enumerate(groups):
        four = lefts[4 * index : 4 * index + 4]
        blocks = rights[4 * index : 4 * index + 4]

        @pl.when(step == start)
        def _(four=four):
            for place, ref in enumerate(four):
                left_s[:, place * TOK : (place + 1) * TOK] = ref[...].astype(f32).T.astype(bf16)

        @pl.when((step >= start) & (step < start + count))
        def _(blocks=blocks):
            right = jnp.concatenate([ref[...] for ref in blocks], axis=0)
            sum_ref[...] = dot_nn(left_s[...], right).astype(bf16)


def weight_grad(picks, tile, groups):
    steps = []
    in_left = []
    in_right = []
    operands_left = []
    operands_right = []
    start = 0
    for left, right in groups:
        count = right[0][0].shape[1] // tile
        steps.append((start, count))
        for array, which, column in left:
            in_left.append(
                pl.BlockSpec(
                    (TOK, SIDE),
                    lambda step, pick, which=which, column=column: (
                        0 if which is None else pick[which],
                        column,
                    ),
                )
            )
            operands_left.append(array)
        for array, which in right:
            in_right.append(
                pl.BlockSpec(
                    (TOK, tile),
                    lambda step, pick, which=which, start=start, count=count: (
                        0 if which is None else pick[which],
                        jnp.clip(step - start, 0, count - 1),
                    ),
                )
            )
            operands_right.append(array)
        start += count
    return pl.pallas_call(
        functools.partial(weight_grad_kernel, tuple(steps)),
        grid_spec=pltpu.PrefetchScalarGridSpec(
            num_scalar_prefetch=1,
            grid=(start,),
            in_specs=in_left + in_right,
            out_specs=pl.BlockSpec((SIDE, tile), lambda step, pick: (0, step)),
            scratch_shapes=[pltpu.VMEM((SIDE, 4 * TOK), bf16)],
        ),
        out_shape=jax.ShapeDtypeStruct((SIDE, start * tile), bf16),
        compiler_params=pltpu.CompilerParams(vmem_limit_bytes=16 * MIB),
        cost_estimate=pl.CostEstimate(
            flops=8 * TOK * SIDE * start * tile,
            bytes_accessed=4 * SIDE * start * tile,
            transcendentals=0,
        ),
        name="weight_grad",
    )(picks, *operands_left, *operands_right)


def row_layout(doc_ids):
    rows = doc_ids.shape[0]
    positions = jnp.arange(TOK, dtype=jnp.int32)
    earlier = jnp.sum((doc_ids[:, None, :] < doc_ids[:, :, None]).astype(jnp.int32), axis=2)
    places = positions[None, :] - earlier
    half_dim = HD // 2
    inverse_freq = rope_base ** (-jnp.arange(half_dim, dtype=f32) / half_dim)
    angles = places.astype(f32)[:, :, None] * inverse_freq[None, None, :]
    repeats = LANES // half_dim
    rope = jnp.concatenate([jnp.cos(angles)] * repeats + [jnp.sin(angles)] * repeats, axis=-1)
    masks = jnp.concatenate(
        [
            jnp.broadcast_to((places >= shift).astype(f32)[:, :, None], (rows, TOK, LANES))
            for shift in (1, 2, 3)
        ],
        axis=-1,
    )
    doc_cols = jnp.broadcast_to(doc_ids[:, :, None], (rows, TOK, LANES))
    doc_rows = jnp.broadcast_to(doc_ids[:, None, :], (rows, 8, TOK))
    return (rope, masks, doc_cols, doc_rows)


def core_params(conv_weight, conv_bias, step_bias, decay_log, skip_scale, mixer_gain):
    taps = jnp.concatenate([conv_weight, conv_bias[None], jnp.zeros((3, CH), f32)], axis=0)
    heads = jnp.zeros((8, LANES), f32)
    heads = heads.at[0, :MH].set(step_bias).at[1, :MH].set(jnp.exp(decay_log))
    wide = jnp.concatenate(
        [jnp.repeat(skip_scale, MP)[None], mixer_gain[None], jnp.zeros((6, E), f32)], axis=0
    )
    return (taps, heads, wide)


def swapped(value):
    return lax.ppermute(value, "core", [(0, 1), (1, 0)])


def ring_order(chips):
    return [2 * step for step in range(chips // 2)] + [
        2 * step + 1 for step in reversed(range(chips // 2))
    ]


def ring_place(chip, chips):
    return jnp.where(chip % 2 == 0, chip // 2, chips - 1 - chip // 2)


def onward(value, steps):
    order = ring_order(lax.axis_size("chip"))
    chips = len(order)
    return lax.ppermute(
        value, "chip", [(order[at], order[(at + steps) % chips]) for at in range(chips)]
    )


def slot_offsets(chips):
    offsets = [0]
    for far in range(1, chips // 2):
        offsets += [-far, far]
    return offsets + [chips // 2]


def tied(*values):
    return lax.optimization_barrier(values)


class RingGather:
    def __init__(self, shard):
        self.slots = [shard]
        self.ahead = self.back = shard
        self.left = lax.axis_size("chip") // 2

    def operands(self):
        half = self.ahead.shape[0] // 2
        if self.left == 1:
            return self.ahead[:half], self.back[half:]
        return self.ahead, self.back

    def send(self, ahead, back):
        self.ahead, self.back = tied(onward(ahead, 1), onward(back, -1))
        self.slots += [self.ahead, self.back]
        self.left -= 1
        return self.ahead

    def step(self):
        return self.send(*self.operands())

    def last(self):
        while self.left > 1:
            self.step()

    def hold(self, value):
        self.ahead, self.back, _ = tied(self.ahead, self.back, value)
        self.slots[-2:] = [self.ahead, self.back]


class RingReduce:
    def __init__(self, sums):
        self.sums = sums
        self.chips = lax.axis_size("chip")
        self.size = sums.shape[0] // self.chips
        self.left = self.chips // 2
        self.ahead = self.back = None

    def slot(self, index, start=0, stop=None):
        stop = self.size if stop is None else stop
        return self.sums[index * self.size + start : index * self.size + stop]

    def operands(self):
        half = self.size // 2
        if self.ahead is None:
            last = self.chips - 1
            return self.slot(last, 0, half), self.slot(last, half)
        ahead, back = self.ahead.astype(f32), self.back.astype(f32)
        if self.left == self.chips // 2 - 1:
            ahead = jnp.pad(ahead, ((0, half), (0, 0)))
            back = jnp.pad(back, ((half, 0), (0, 0)))
        return (
            (self.slot(2 * self.left).astype(f32) + ahead).astype(bf16),
            (self.slot(2 * self.left - 1).astype(f32) + back).astype(bf16),
        )

    def send(self, ahead, back):
        self.ahead, self.back = tied(onward(ahead, 1), onward(back, -1))
        self.left -= 1
        return self.ahead

    def step(self):
        return self.send(*self.operands())

    def hold(self, value):
        self.ahead, self.back, _ = tied(self.ahead, self.back, value)

    def columns(self, start, stop):
        part = RingReduce(self.sums[:, start:stop])
        part.left = self.left
        part.ahead, part.back = self.ahead[:, start:stop], self.back[:, start:stop]
        return part

    def total(self):
        while self.left > 0:
            self.step()
        return self.slot(0).astype(f32) + self.ahead.astype(f32) + self.back.astype(f32)


def small_hops(chips):
    if chips & (chips - 1):
        return [lambda value: lax.psum(value, ("chip", "core")) - value]
    hops = [swapped]
    for bit in range(chips.bit_length() - 1):
        pairs = [(chip, chip ^ (1 << bit)) for chip in range(chips)]
        hops.append(lambda value, pairs=pairs: lax.ppermute(value, "chip", pairs))
    return hops


def ring_columns(core):
    chips = lax.axis_size("chip")
    place = ring_place(lax.axis_index("chip"), chips)
    own = []
    for offset in slot_offsets(chips):
        at = (place + offset) % chips
        own.append(jnp.where(at < chips // 2, 2 * at, 2 * (chips - 1 - at) + 1))
    own = jnp.stack(own)
    width = D // (2 * chips)
    starts = jnp.concatenate([2 * own + core, 2 * own + 1 - core]) * width
    wanted = (starts[:, None] + jnp.arange(width)[None, :]).reshape(D)
    return (jnp.arange(D)[:, None] == wanted[None, :]).astype(bf16)


def per_device(
    inputs, out_grad, doc_ids, row_live, pre_gain, mlp_gain, mixer_gain, conv_weight, conv_bias,
    step_bias, decay_log, skip_scale, mixer_in_weight, mixer_out_weight, query_weight, key_weight,
    value_weight, attend_weight, gate_up_weight, down_weight,
):
    is_first = lax.axis_index("section") == 0
    core = lax.axis_index("core")
    shard = mixer_in_weight.shape[1]
    packed_a = jnp.concatenate(
        [
            mixer_in_weight[0, :, :AT_Q],
            query_weight[0],
            key_weight[0],
            value_weight[0],
            mixer_in_weight[0, :, AT_Q:],
            jnp.zeros((shard, LANES - MH), bf16),
        ],
        axis=1,
    )
    packed_b = jnp.concatenate(
        [mixer_out_weight[0].T, attend_weight[0].T, gate_up_weight[0], down_weight[0].T], axis=1
    )

    layout = row_layout(doc_ids)
    params = core_params(
        conv_weight[0], conv_bias[0], step_bias[0], decay_log[0], skip_scale[0], mixer_gain[0]
    )
    turn = ring_columns(core)

    def own_order(values):
        if values.dtype == bf16:
            return dot_nn(values, turn).astype(bf16)
        return dot_exact(values, turn.astype(f32))

    def whole_order(values):
        if values.dtype == bf16:
            return dot_nt(values, turn).astype(bf16)
        return dot_exact(values, turn.astype(f32).T)

    pre_row = own_order(pre_gain)
    mlp_row = own_order(mlp_gain)
    first_rows = own_order(inputs)

    positions = jnp.arange(TOK, dtype=jnp.int32)
    live = (positions[None, :] < row_live[:, None]).reshape(MB * TOK, 1)
    from_loss = own_order(jnp.where(live, out_grad, jnp.zeros_like(out_grad)))
    first_rows, from_loss = tied(first_rows, from_loss)

    ring_a = RingGather(packed_a)
    ring_b = RingGather(packed_b)
    ring_a.step()
    ring_b.step()
    ring_a.last()
    now_a, now_b = tied(ring_a.operands(), ring_b.operands())
    ring_a.send(*now_a)
    ring_b.send(*now_b)
    own_a = jnp.concatenate(ring_a.slots, axis=0)
    pair_a = (own_a, swapped(own_a))
    now_b, gain_now, pair_a = tied(ring_b.operands(), pre_row, pair_a)
    ring_b.send(*now_b)
    projected = by_row(project(first_rows, gain_now, *pair_a))
    mixed = core_forward(0, projected, layout, params)
    ring_b.hold(mixed)
    now_b, mixed = tied(ring_b.operands(), mixed)
    ring_b.send(*now_b)
    mixed, _, _ = core_forward(1, projected, layout, params, held=mixed)
    ring_b.hold(mixed)
    while ring_b.left:
        ring_b.step()
    pair_b = (
        jnp.concatenate(ring_b.slots, axis=0),
        jnp.concatenate([swapped(slot) for slot in ring_b.slots], axis=0),
    )
    mixed = mixed.reshape(MB * TOK, MIXED)
    received = {}
    for row in (1, 0):
        (handed,) = feed_forward(row, first_rows, mixed, mlp_row, *pair_b)
        received[row] = passed_along(handed, "section", 1)

    def second_pass(row, projects=(), cores=(), forwards=()):
        start = jnp.where(is_first, first_rows[row * TOK : (row + 1) * TOK], received[row])
        projects = project(start, pre_row, *pair_a, row=row, held=projects)
        cores = core_forward(row, by_row(projects), layout, params, held=cores)
        mixed = cores[0].reshape(MB * TOK, MIXED)
        forwards = feed_forward(row, start, mixed, mlp_row, *pair_b, held=forwards)
        return start, projects, cores, forwards

    arrived = jnp.zeros((TOK, D), bf16)
    lefts = []
    rights = []
    rows = []
    picks = jnp.where(is_first, jnp.array([1, 0]), jnp.array([0, 1])).astype(jnp.int32)

    def tick_left(which):
        return [(lefts[1][which], None, 0), (lefts[2][which], None, 0)] + [
            (lefts[1][which + 2], None, 0), (lefts[2][which + 2], None, 0)
        ]

    def tick_right(which):
        return [(rights[tick][which + far], None) for far in (0, 2) for tick in (1, 2)]

    def saved_left(own, their):
        return [(own, 0, 0), (own, 1, 0), (their, 0, 0), (their, 1, 0)]

    def saved_right(own, their):
        return [(own, 0), (own, 1), (their, 0), (their, 1)]

    start, projects, cores, forwards = second_pass(1)
    starts = {1: start}
    start_rows = jnp.concatenate([start, start], axis=0)
    for tick in range(3):
        if tick == 1:
            (projects, cores, forwards), received[0], _ = tied(
                (projects, cores, forwards), received[0], d_low
            )
            starts[0], projects, cores, forwards = second_pass(0, projects, cores, forwards)
            start_rows = jnp.concatenate([starts[0], starts[1]], axis=0)
            arrived, forwards = tied(arrived, forwards)
        normed, projected = projects[0], by_row(projects)
        mixed, pre, yns = cores[0].reshape(MB * TOK, MIXED), cores[1], cores[2]
        result, middle, normed_two, gate, up, act = forwards
        row = jnp.where(is_first, (1, 1, 0)[tick], (1, 0, 1)[tick]).astype(jnp.int32).reshape(1)
        if tick == 2:
            row, lefts[1], rights[1], rows[1] = tied(row, lefts[1], rights[1], rows[1])
        loss_row = (1, 0, 1)[tick]
        cotangent = jnp.where(
            is_first, arrived, from_loss[loss_row * TOK : (loss_row + 1) * TOK]
        )
        if tick == 1:
            cotangent, swaps = tied(
                cotangent, (mixed, act, normed[:, SIDE:], normed_two[:, SIDE:])
            )
            their_mixed, their_act, their_normed, their_normed_two = map(swapped, swaps)
        d_gate, d_up, d_middle, middle_low, d_mixed, mlp_grad = feed_back(
            row, cotangent, gate, up, middle, mlp_row, *pair_b
        )
        lefts.append(
            (cotangent, middle_low, swapped(cotangent[:, SIDE:]), swapped(middle_low[:, SIDE:]))
        )
        rights.append((d_gate, d_up, swapped(d_gate), swapped(d_up)))
        if tick < 2:
            attended = attend_back(row, projected, d_mixed, layout)
            if tick == 1:
                row, their_mixed, their_act, their_normed, their_normed_two = tied(
                    row, their_mixed, their_act, their_normed, their_normed_two
                )
            proj_low, small = mixer_back(
                row, projected, pre, yns, d_mixed, attended, layout, params
            )
            their_low = swapped(proj_low)
        else:
            sum_c = weight_grad(
                picks,
                1024,
                [
                    (tick_left(1), saved_right(mixed, their_mixed)),
                    (tick_left(0), saved_right(act, their_act)),
                ],
            )
            ring_c = RingReduce(sum_c)
            now_c, row = tied(ring_c.operands(), row)
            ring_c.send(*now_c)
            attended = attend_back(row, projected, d_mixed, layout)
            ring_c.hold(attended)
            picks_now, now_c, rights[2] = tied(picks, ring_c.operands(), rights[2])
            ring_c.send(*now_c)
            sum_b = weight_grad(
                picks_now,
                1024,
                [
                    (saved_left(normed_two, their_normed_two), tick_right(0)),
                    (saved_left(normed_two, their_normed_two), tick_right(1)),
                ],
            )
            ring_b = RingReduce(sum_b)
            ring_c.hold(sum_b)
            now_b, now_c, row, attended = tied(
                ring_b.operands(), ring_c.operands(), row, attended
            )
            ring_c.send(*now_c)
            ring_b.send(*now_b)
            proj_low, small = mixer_back(
                row, projected, pre, yns, d_mixed, attended, layout, params
            )
            proj_low, ring_b.ahead, ring_b.back, ring_c.ahead, ring_c.back = tied(
                proj_low, ring_b.ahead, ring_b.back, ring_c.ahead, ring_c.back
            )
            their_low = swapped(proj_low)
            now_b, row = tied(ring_b.operands(), row)
            ring_b.send(*now_b)
            d_rows, d_low, pre_grad = project_back(
                row, proj_low, start_rows, d_middle, pre_row, *pair_a
            )
            now_c, their_low, d_rows, pre_grad = tied(
                ring_c.operands(), their_low, d_rows, pre_grad
            )
            ring_c.send(*now_c)
            picks_now, now_c = tied(picks, now_c)
            (p_one, their_one), (p_two, their_two) = rows[1][1], (proj_low, their_low)
            sum_a = weight_grad(
                picks_now,
                WIDE_A // 3,
                [
                    (
                        saved_left(normed, their_normed),
                        [(p_one, None), (p_two, None), (their_one, None), (their_two, None)],
                    )
                ],
            )
            ring_b.hold(sum_a)
            ring_a = RingReduce(sum_a)
            ring_c.hold(sum_a)
            now_a, now_b, ring_c.ahead, ring_c.back = tied(
                ring_a.operands(), ring_b.operands(), ring_c.ahead, ring_c.back
            )
            ring_b.send(*now_b)
            ring_a.send(*now_a)
        if tick < 2:
            d_rows, d_low, pre_grad = project_back(
                row, proj_low, start_rows, d_middle, pre_row, *pair_a
            )
        rows.append((d_rows, (proj_low, their_low), pre_grad, mlp_grad, small))
        if tick < 2:
            arrived = passed_along(d_low, "section", -1)

    pre_sum, mlp_sum, small = (one + two for one, two in zip(rows[1][2:], rows[2][2:]))
    gain_sums = whole_order(jnp.concatenate([pre_sum, mlp_sum], axis=0))
    small = jnp.concatenate([small, jnp.pad(gain_sums, ((0, 6), (0, CH - D)))], axis=0)

    hops = small_hops(lax.axis_size("chip"))

    def hop_beside(small, ring):
        if not hops:
            return small
        small, moved, _ = tied(small, hops.pop(0)(small), ring.ahead)
        return small + moved

    small = hop_beside(small, ring_a)
    ring_b.step()
    ring_a.step()
    small = hop_beside(small, ring_a)
    while ring_a.left > 2:
        ring_a.step()
    d_last = tied(rows[2][0], ring_a.ahead)[0]
    rings_a = [ring_a.columns(0, CUT_A), ring_a.columns(CUT_A, WIDE_A)]
    while rings_a[0].left:
        for ring in rings_a:
            ring.step()
        small = hop_beside(small, rings_a[0])
    for hop in hops:
        small = small + hop(small)
    share_c = ring_c.total()
    share_b = ring_b.total()
    share_a = jnp.concatenate([ring.total() for ring in rings_a], axis=1)

    start_grad = jnp.concatenate(
        [
            jnp.where(is_first, d_last, rows[1][0]),
            jnp.where(is_first, rows[1][0], d_last),
        ],
        axis=0,
    )
    skip_sum = jnp.sum(small[6, :E].reshape(MH, MP), axis=1)
    mixer_in_grad = jnp.concatenate([share_a[:, :AT_Q], share_a[:, AT_DT : AT_DT + MH]], axis=1)
    return (
        whole_order(result)[None],
        whole_order(start_grad)[None],
        small[8:9, :D],
        small[9:10, :D],
        small[5:6, :E],
        small[None, :4],
        small[4:5],
        small[7:8, :MH],
        small[7:8, LANES : LANES + MH],
        skip_sum[None],
        mixer_in_grad[None],
        share_c[:, :E].T[None],
        share_a[:, AT_Q:AT_K][None],
        share_a[:, AT_K:AT_V][None],
        share_a[:, AT_V:AT_DT][None],
        share_c[:, E:MIXED].T[None],
        share_b[None],
        share_c[:, MIXED:].T[None],
    )


def solution(mesh):
    dp = mesh.shape["dp"]
    devices = mesh.devices.reshape(mesh.shape["section"], dp // 2, 2)
    paired = Mesh(devices, ("section", "chip", "core"))
    over = ("chip", "core")
    rows = P(over, None)
    small = P("section", None)
    by_row = P("section", over, None)
    by_col = P("section", None, over)
    small_specs = (small, small, small, P("section", None, None), small, small, small, small)
    big_specs = (by_row, by_col, by_row, by_row, by_row, by_col, by_row, by_col)
    in_specs = (rows, rows, rows, P(over)) + small_specs + big_specs
    out_specs = (by_row, by_row) + small_specs + big_specs
    return jax.shard_map(
        per_device, mesh=paired, in_specs=in_specs, out_specs=out_specs, check_vma=False
    )
```

profile of v0, /device:TPU:0, one launch (start us, length us, event | category | flops | bytes accessed | tf_op | source)
XLA Modules:
  0.0 502.7 jit_solution(1599965950041821928)
XLA Ops:
  27.9 14.3 %collective-permute-done.6 = bf16[64,8192]{1,0:T(8,128)(2,1)} collective-permute-done((bf16[64,8192]{1,0:T(8,128)(2,1)S(1)}, bf16[64,8192]{1,0:T(8,128)(2,1)}, u32[]{:S(2)}, u32[]{:S(2)}) %collective-permute-start.6) | collective-permute-done | bytes 1048608 | tf_op jit(solution)/shard_map/ppermute | solution.py:954
  56.5 10.7 %collective-permute-done.4 = bf16[64,4224]{1,0:T(8,128)(2,1)S(1)} collective-permute-done((bf16[64,4224]{1,0:T(8,128)(2,1)S(1)}, bf16[64,4224]{1,0:T(8,128)(2,1)S(1)}, u32[]{:S(2)}, u32[]{:S(2)}) %collective-permute-start.4) | collective-permute-done | bytes 540704 | tf_op jit(solution)/shard_map/ppermute | solution.py:954
  79.5 17.4 %collective-permute-done.8 = bf16[64,8192]{1,0:T(8,128)(2,1)S(1)} collective-permute-done((bf16[64,8192]{1,0:T(8,128)(2,1)}, bf16[64,8192]{1,0:T(8,128)(2,1)S(1)}, u32[]{:S(2)}, u32[]{:S(2)}) %collective-permute-start.8) | collective-permute-done | bytes 1048608 | tf_op jit(solution)/shard_map/ppermute | solution.py:954
  104.2 7.9 %project.3 = (bf16[512,1024]{1,0:T(8,128)(2,1)}, bf16[512,3328]{1,0:T(8,128)(2,1)S(1)}, bf16[512,768]{1,0:T(8,128)(2,1)S(1)}, f32[512,128]{1,0:T(8,128)S(1)}) custom-call(bf16[512,1024]{1,0:T(8,128)(2,1)S(1)} %copy-done.44, f32[1,1024]{1,0:T(1,128)S(1)} %fusion.4.gain_ref, bf16[512,4224]{1,0:T(8,128)(2,1)S(1)} %constant_dynamic-update-slice_fusion.own_ref, ...), custom_call_target="tpu_custom_call" | custom-call | flops 4429185024 | bytes 12976128 | tf_op jit(solution)/shard_map/project/pallas_call | solution.py:566
  112.2 6.9 %core_forward.4 = (bf16[2,256,2048]{2,1,0:T(8,128)(2,1)S(1)}, bf16[2,256,1792]{2,1,0:T(8,128)(2,1)S(1)}, f32[2,256,1536]{2,1,0:T(8,128)S(1)}) custom-call(bf16[2,256,3328]{2,1,0:T(8,128)(2,1)S(1)} %bitcast.106, bf16[2,256,768]{2,1,0:T(8,128)(2,1)S(1)} %bitcast.113, f32[2,256,128]{2,1,0:T(8,128)S(1)} %bitcast.115, f32[2,256,256]{2,1,0:T(8,128)S(1)} %concatenate.67.rope_ref, ...), custom_call_target="tpu_custom_call" | custom-call | flops 400000000 | bytes 12582912 | tf_op jit(solution)/shard_map/core_forward/pallas_call | solution.py:425
  119.1 8.0 %collective-permute-done.13 = bf16[64,8192]{1,0:T(8,128)(2,1)S(1)} collective-permute-done((bf16[64,8192]{1,0:T(8,128)(2,1)S(1)}, bf16[64,8192]{1,0:T(8,128)(2,1)S(1)}, u32[]{:S(2)}, u32[]{:S(2)}) %collective-permute-start.13) | collective-permute-done | bytes 1048608 | tf_op jit(solution)/shard_map/ppermute | solution.py:954
  131.5 6.9 %core_forward.5 = (bf16[2,256,2048]{2,1,0:T(8,128)(2,1)S(1)}, bf16[2,256,1792]{2,1,0:T(8,128)(2,1)S(1)}, f32[2,256,1536]{2,1,0:T(8,128)S(1)}) custom-call(bf16[2,256,3328]{2,1,0:T(8,128)(2,1)S(1)} %bitcast.107, bf16[2,256,768]{2,1,0:T(8,128)(2,1)S(1)} %bitcast.114, ...), custom_call_target="tpu_custom_call", output_to_operand_aliasing={{0}: (10, {}), {1}: (11, {}), {2}: (12, {})} | custom-call | flops 400000000 | bytes 12582912 | tf_op jit(solution)/shard_map/core_forward/pallas_call | solution.py:425
  146.3 8.6 %feed_forward.4 = bf16[256,1024]{1,0:T(8,128)(2,1)S(1)} custom-call(bf16[512,1024]{1,0:T(8,128)(2,1)S(1)} %copy-done.44, bf16[512,2048]{1,0:T(8,128)(2,1)S(1)} %bitcast.104, f32[1,1024]{1,0:T(1,128)S(1)} %fusion.3.gain_ref, bf16[512,8192]{1,0:T(8,128)(2,1)S(1)} %constant_dynamic-update-slice_fusion.9.out_own.gate_own.up_own.down_own, ...), custom_call_target="tpu_custom_call" | custom-call | flops 4294967296 | bytes 16777216 | tf_op jit(solution)/shard_map/feed_forward/pallas_call | solution.py:672
  158.4 8.6 %feed_forward.6 = bf16[256,1024]{1,0:T(8,128)(2,1)S(1)} custom-call(bf16[512,1024]{1,0:T(8,128)(2,1)S(1)} %copy-done.44, bf16[512,2048]{1,0:T(8,128)(2,1)S(1)} %bitcast.105, f32[1,1024]{1,0:T(1,128)S(1)} %fusion.3.gain_ref, bf16[512,8192]{1,0:T(8,128)(2,1)S(1)} %constant_dynamic-update-slice_fusion.9.out_own.gate_own.up_own.down_own, ...), custom_call_target="tpu_custom_call" | custom-call | flops 4294967296 | bytes 16777216 | tf_op jit(solution)/shard_map/feed_forward/pallas_call | solution.py:672
  174.8 7.9 %core_forward.6 = (bf16[2,256,2048]{2,1,0:T(8,128)(2,1)}, bf16[2,256,1792]{2,1,0:T(8,128)(2,1)S(1)}, f32[2,256,1536]{2,1,0:T(8,128)S(1)}) custom-call(bf16[2,256,3328]{2,1,0:T(8,128)(2,1)S(1)} %bitcast.84, bf16[2,256,768]{2,1,0:T(8,128)(2,1)S(1)} %bitcast.99, f32[2,256,128]{2,1,0:T(8,128)S(1)} %bitcast.108, f32[2,256,256]{2,1,0:T(8,128)S(1)} %concatenate.67.rope_ref, ...), custom_call_target="tpu_custom_call" | custom-call | flops 400000000 | bytes 12582912 | tf_op jit(solution)/shard_map/core_forward/pallas_call | solution.py:425
  182.6 12.6 %feed_forward.5 = (bf16[512,1024]{1,0:T(8,128)(2,1)S(1)}, f32[512,1024]{1,0:T(8,128)S(1)}, bf16[512,1024]{1,0:T(8,128)(2,1)S(1)}, bf16[512,2048]{1,0:T(8,128)(2,...) custom-call(bf16[256,1024]{1,0:T(8,128)(2,1)S(1)} %slice_select_fusion.2.rows_ref, ...), custom_call_target="tpu_custom_call" | custom-call | flops 4294967296 | bytes 16777216 | tf_op jit(solution)/shard_map/feed_forward/pallas_call | solution.py:672
  197.9 13.3 %feed_back.3 = (bf16[256,2048]{1,0:T(8,128)(2,1)}, bf16[256,2048]{1,0:T(8,128)(2,1)}, f32[256,1024]{1,0:T(8,128)S(1)}, bf16[256,1024]{1,0:T(8,128)(2,1)}, f32[256,2048]{1,0:T(8,128)S(1)}, /*index=5*/f32[1,1024]{1,0:T(1,128)}) custom-call(s32[1]{0:T(128)} %constant.150.clone.1.pick_ref, bf16[256,1024]{1,0:T(8,128)(2,1)S(1)} %broadcast_select_fusion.3.cot_ref, ...), custom_call_target="tpu_custom_call" | custom-call | flops 4294967296 | bytes 16777216 | tf_op jit(solution)/shard_map/feed_back/pallas_call | solution.py:741
  215.0 12.0 %mixer_back.3 = (bf16[256,4224]{1,0:T(8,128)(2,1)S(1)}, f32[8,1792]{1,0:T(8,128)}) custom-call(s32[1]{0:T(128)} %constant.150.clone.1.pick_ref, bf16[2,256,3328]{2,1,0:T(8,128)(2,1)S(1)} %bitcast.85, f32[2,256,128]{2,1,0:T(8,128)S(1)} %bitcast.109, bf16[2,256,1792]{2,1,0:T(8,128)(2,1)S(1)} %get-tuple-element.332.pre_ref.refs_1_, ...), custom_call_target="tpu_custom_call" | custom-call | flops 700000000 | bytes 10485760 | tf_op jit(solution)/shard_map/mixer_back/pallas_call | solution.py:480
  239.4 7.9 %core_forward.7 = (bf16[2,256,2048]{2,1,0:T(8,128)(2,1)}, bf16[2,256,1792]{2,1,0:T(8,128)(2,1)S(1)}, f32[2,256,1536]{2,1,0:T(8,128)S(1)}) custom-call(bf16[2,256,3328]{2,1,0:T(8,128)(2,1)S(1)} %bitcast.86, bf16[2,256,768]{2,1,0:T(8,128)(2,1)S(1)} %bitcast.101, ...), custom_call_target="tpu_custom_call", output_to_operand_aliasing={{0}: (10, {}), {1}: (11, {}), {2}: (12, {})} | custom-call | flops 400000000 | bytes 12582912 | tf_op jit(solution)/shard_map/core_forward/pallas_call | solution.py:425
  250.2 10.9 %feed_forward.7 = (bf16[512,1024]{1,0:T(8,128)(2,1)S(1)}, f32[512,1024]{1,0:T(8,128)S(1)}, bf16[512,1024]{1,0:T(8,128)(2,1)S(1)}, bf16[512,2048]{1,0:T(8,128)(2,...) custom-call(bf16[256,1024]{1,0:T(8,128)(2,1)S(1)} %slice_select_fusi, ...), custom_call_target="tpu_custom_call", output_to_operand_aliasing={{0}: (11, {}), {1}: (12, {}), {2}: (13, {}), {3}: (14, {}),... | custom-call | flops 4294967296 | bytes 16777216 | tf_op jit(solution)/shard_map/feed_forward/pallas_call | solution.py:672
  272.9 12.4 %feed_back.4 = (bf16[256,2048]{1,0:T(8,128)(2,1)}, bf16[256,2048]{1,0:T(8,128)(2,1)}, f32[256,1024]{1,0:T(8,128)S(1)}, bf16[256,1024]{1,0:T(8,128)(2,1)S(1)}, f3...) custom-call(s32[1]{0:T(128)} %bitcast.43.pick_ref, bf16[256,1024]{1,0:T(8,128)(2,1)S(1)} %slice_select_fusion.cot_ref.refs_4_, ...), custom_call_target="tpu_custom_call" | custom-call | flops 4294967296 | bytes 16777216 | tf_op jit(solution)/shard_map/feed_back/pallas_call | solution.py:741
  288.1 12.8 %mixer_back.4 = (bf16[256,4224]{1,0:T(8,128)(2,1)}, f32[8,1792]{1,0:T(8,128)S(1)}) custom-call(s32[1]{0:T(128)} %bitcast.43.pick_ref, bf16[2,256,3328]{2,1,0:T(8,128)(2,1)S(1)} %bitcast.87, f32[2,256,128]{2,1,0:T(8,128)S(1)} %bitcast.111, bf16[2,256,1792]{2,1,0:T(8,128)(2,1)S(1)} %copy-done.36, f32[2,256,1536]{2,1,0:T(8,128)S(1)} %copy-done.15, ...), custom_call_target="tpu_custom_call" | custom-call | flops 700000000 | bytes 10485760 | tf_op jit(solution)/shard_map/mixer_back/pallas_call | solution.py:480
  311.2 14.9 %collective-permute-done.38 = bf16[256,1024]{1,0:T(8,128)(2,1)} collective-permute-done((bf16[256,1024]{1,0:T(8,128)(2,1)}, bf16[256,1024]{1,0:T(8,128)(2,1)}, u32[]{:S(2)}, u32[]{:S(2)}) %collective-permute-start.38) | collective-permute-done | bytes 524320 | tf_op jit(solution)/shard_map/ppermute | solution.py:521
  333.0 11.6 %feed_back.5 = (bf16[256,2048]{1,0:T(8,128)(2,1)S(1)}, bf16[256,2048]{1,0:T(8,128)(2,1)S(1)}, f32[256,1024]{1,0:T(8,128)S(1)}, bf16[256,1024]{1,0:T(8,128)(2,1)S...) custom-call(s32[1]{0:T(128)} %bitcast.42.pick_ref, bf16[256,1024]{1,0:T(8,128)(2,1)S(1)} %broadcast_select_fusion.2.cot_ref.refs_5_, ...), custom_call_target="tpu_custom_call" | custom-call | flops 4294967296 | bytes 16777216 | tf_op jit(solution)/shard_map/feed_back/pallas_call | solution.py:741
  346.3 9.4 %weight_grad.3 = bf16[512,4096]{1,0:T(8,128)(2,1)S(1)} custom-call(s32[2]{0:T(128)S(1)} %broadcast_select_fusion.4.pick_ref, bf16[256,1024]{1,0:T(8,128)(2,1)S(1)} %get-tuple-element.373.refs_0_, bf16[256,1024]{1,0:T(8,128)(2,1)S(1)} %get-tuple-element.376.refs_1_, bf16[256,512]{1,0:T(8,128)(2,1)S(1)} %collective-permute-done.30.refs_2_, ...), custom_call_target="tpu_custom_call" | custom-call | flops 4294967296 | bytes 8388608 | tf_op jit(solution)/shard_map/weight_grad/pallas_call | solution.py:885
  366.5 9.3 %weight_grad.4 = bf16[512,4096]{1,0:T(8,128)(2,1)S(1)} custom-call(s32[2]{0:T(128)S(1)} %broadcast_select_fusion.4.pick_ref, bf16[512,1024]{1,0:T(8,128)(2,1)S(1)} %copy-done.32, bf16[512,1024]{1,0:T(8,128)(2,1)S(1)} %copy-done.32, bf16[512,512]{1,0:T(8,128)(2,1)} %collective-permute-done.36.refs_2_.refs_3_.refs_6_.refs_7_, ...), custom_call_target="tpu_custom_call" | custom-call | flops 4294967296 | bytes 8388608 | tf_op jit(solution)/shard_map/weight_grad/pallas_call | solution.py:885
  382.0 11.6 %mixer_back.5 = (bf16[256,4224]{1,0:T(8,128)(2,1)S(1)}, f32[8,1792]{1,0:T(8,128)S(1)}) custom-call(s32[1]{0:T(128)} %bitcast.42.pick_ref, bf16[2,256,3328]{2,1,0:T(8,128)(2,1)S(1)} %bitcast.88, f32[2,256,128]{2,1,0:T(8,128)S(1)} %bitcast.112, bf16[2,256,1792]{2,1,0:T(8,128)(2,1)S(1)} %copy-done.37, f32[2,256,1536]{2,1,0:T(8,128)S(1)} %copy-done.16, ...), custom_call_target="tpu_custom_call" | custom-call | flops 700000000 | bytes 10485760 | tf_op jit(solution)/shard_map/mixer_back/pallas_call | solution.py:480
  413.5 8.6 %weight_grad.5 = bf16[512,4224]{1,0:T(8,128)(2,1)S(1)} custom-call(s32[2]{0:T(128)S(1)} %broadcast_select_fusion.4.pick_ref, bf16[512,1024]{1,0:T(8,128)(2,1)S(1)} %copy-done.55, bf16[512,1024]{1,0:T(8,128)(2,1)S(1)} %copy-done.55, bf16[512,512]{1,0:T(8,128)(2,1)} %collective-permute-done.35.refs_2_.refs_3_, ...), custom_call_target="tpu_custom_call" | custom-call | flops 4429185024 | bytes 8650752 | tf_op jit(solution)/shard_map/weight_grad/pallas_call | solution.py:885
  451.6 7.7 %collective-permute-done.58 = bf16[64,4224]{1,0:T(8,128)(2,1)S(1)} collective-permute-done((bf16[64,4224]{1,0:T(8,128)(2,1)S(1)}, bf16[64,4224]{1,0:T(8,128)(2,1)S(1)}, u32[]{:S(2)}, u32[]{:S(2)}) %collective-permute-start.58) | collective-permute-done | bytes 540704 | tf_op jit(solution)/shard_map/ppermute | solution.py:954
  (457 shorter events, 248.2 us)
Async XLA Ops:
  9.0 33.2 %collective-permute-start.6 = (bf16[64,8192]{1,0:T(8,128)(2,1)S(1)}, bf16[64,8192]{1,0:T(8,128)(2,1)}, u32[]{:S(2)}, u32[]{:S(2)}) collective-permute-start(bf16[64,8192]{1,0:T(8,128)(2,1)S(1)} %get-tuple-element.515), channel_id=1, source_target_pairs={{0,4},{4,8},{8,12},{12,14},{14,10},{10,6},{6,2},{2,0},{1,5},{5,9},... | collective-permute-start | bytes 3145736 | tf_op jit(solution)/shard_map/ppermute | solution.py:954
  11.0 33.4 %collective-permute-start.7 = (bf16[64,8192]{1,0:T(8,128)(2,1)S(1)}, bf16[64,8192]{1,0:T(8,128)(2,1)}, u32[]{:S(2)}, u32[]{:S(2)}) collective-permute-start(bf16[64,8192]{1,0:T(8,128)(2,1)S(1)} %get-tuple-element.515), channel_id=1, source_target_pairs={{0,2},{4,0},{8,4},{12,8},{14,12},{10,14},{6,10},{2,6},{1,3},{5,1},... | collective-permute-start | bytes 3145736 | tf_op jit(solution)/shard_map/ppermute | solution.py:954
  11.0 38.4 %collective-permute-start.17 = (bf16[64,8192]{1,0:T(8,128)(2,1)S(1)}, bf16[64,8192]{1,0:T(8,128)(2,1)}, u32[]{:S(2)}, u32[]{:S(2)}) collective-permute-start(bf16[64,8192]{1,0:T(8,128)(2,1)S(1)} %get-tuple-element.515), channel_id=1, source_target_pairs={{0,1},{1,0},{2,3},{3,2},{4,5},{5,4},{6,7},{7,6},{8,9},{9,8},{10,11... | collective-permute-start | bytes 3145736 | tf_op jit(solution)/shard_map/ppermute | solution.py:938
  23.6 29.3 %collective-permute-start.2 = (bf16[64,4224]{1,0:T(8,128)(2,1)}, bf16[64,4224]{1,0:T(8,128)(2,1)S(1)}, u32[]{:S(2)}, u32[]{:S(2)}) collective-permute-start(bf16[64,4224]{1,0:T(8,128)(2,1)} %collective-permute-done), channel_id=1, source_target_pairs={{0,4},{4,8},{8,12},{12,14},{14,10},{10,6},{6,2},{2,0},{1,5},{5,9},... | collective-permute-start | bytes 1622024 | tf_op jit(solution)/shard_map/ppermute | solution.py:954
  25.6 28.8 %collective-permute-start.3 = (bf16[64,4224]{1,0:T(8,128)(2,1)}, bf16[64,4224]{1,0:T(8,128)(2,1)S(1)}, u32[]{:S(2)}, u32[]{:S(2)}) collective-permute-start(bf16[64,4224]{1,0:T(8,128)(2,1)} %collective-permute-done.1), channel_id=1, source_target_pairs={{0,2},{4,0},{8,4},{12,8},{14,12},{10,14},{6,10},{2,6},{1,3},{5,1},... | collective-permute-start | bytes 1622024 | tf_op jit(solution)/shard_map/ppermute | solution.py:954
  44.4 35.0 %collective-permute-start.18 = (bf16[64,8192]{1,0:T(8,128)(2,1)}, bf16[64,8192]{1,0:T(8,128)(2,1)S(1)}, u32[]{:S(2)}, u32[]{:S(2)}) collective-permute-start(bf16[64,8192]{1,0:T(8,128)(2,1)} %collective-permute-done.6), channel_id=1, source_target_pairs={{0,1},{1,0},{2,3},{3,2},{4,5},{5,4},{6,7},{7,6},{8,9},{9,8},{10,11... | collective-permute-start | bytes 3145736 | tf_op jit(solution)/shard_map/ppermute | solution.py:938
  44.4 35.1 %collective-permute-start.19 = (bf16[64,8192]{1,0:T(8,128)(2,1)}, bf16[64,8192]{1,0:T(8,128)(2,1)S(1)}, u32[]{:S(2)}, u32[]{:S(2)}) collective-permute-start(bf16[64,8192]{1,0:T(8,128)(2,1)} %collective-permute-done.7), channel_id=1, source_target_pairs={{0,1},{1,0},{2,3},{3,2},{4,5},{5,4},{6,7},{7,6},{8,9},{9,8},{10,11... | collective-permute-start | bytes 3145736 | tf_op jit(solution)/shard_map/ppermute | solution.py:938
  70.7 26.2 %collective-permute-start.8 = (bf16[64,8192]{1,0:T(8,128)(2,1)}, bf16[64,8192]{1,0:T(8,128)(2,1)S(1)}, u32[]{:S(2)}, u32[]{:S(2)}) collective-permute-start(bf16[64,8192]{1,0:T(8,128)(2,1)} %collective-permute-done.6), channel_id=1, source_target_pairs={{0,4},{4,8},{8,12},{12,14},{14,10},{10,6},{6,2},{2,0},{1,5},{5,9},... | collective-permute-start | bytes 3145736 | tf_op jit(solution)/shard_map/ppermute | solution.py:954
  79.3 22.6 %collective-permute-start.12 = (bf16[512,4224]{1,0:T(8,128)(2,1)S(1)}, bf16[512,4224]{1,0:T(8,128)(2,1)S(1)}, u32[]{:S(2)}, u32[]{:S(2)}) collective-permute-start(bf16[512,4224]{1,0:T(8,128)(2,1)S(1)} %constant_dynamic-update-slice_fusion.own_ref), channel_id=1, source_target_pairs={{0,1},{1,0},{2,3},{3,2},{4,5},{5,4},{6,7},{7,6},{8,9},{9,8},{10,11... | collective-permute-start | bytes 12976136 | tf_op jit(solution)/shard_map/ppermute | solution.py:938
  101.9 25.3 %collective-permute-start.13 = (bf16[64,8192]{1,0:T(8,128)(2,1)S(1)}, bf16[64,8192]{1,0:T(8,128)(2,1)S(1)}, u32[]{:S(2)}, u32[]{:S(2)}) collective-permute-start(bf16[64,8192]{1,0:T(8,128)(2,1)S(1)} %collective-permute-done.8), channel_id=1, source_target_pairs={{0,4},{4,8},{8,12},{12,14},{14,10},{10,6},{6,2},{2,0},{1,5},{5,9},... | collective-permute-start | bytes 3145736 | tf_op jit(solution)/shard_map/ppermute | solution.py:954
  103.4 25.1 %collective-permute-start.14 = (bf16[64,8192]{1,0:T(8,128)(2,1)S(1)}, bf16[64,8192]{1,0:T(8,128)(2,1)S(1)}, u32[]{:S(2)}, u32[]{:S(2)}) collective-permute-start(bf16[64,8192]{1,0:T(8,128)(2,1)S(1)} %collective-permute-done.9), channel_id=1, source_target_pairs={{0,2},{4,0},{8,4},{12,8},{14,12},{10,14},{6,10},{2,6},{1,3},{5,1},... | collective-permute-start | bytes 3145736 | tf_op jit(solution)/shard_map/ppermute | solution.py:954
  167.0 67.0 %collective-permute-start.28 = (bf16[256,1024]{1,0:T(8,128)(2,1)S(1)}, bf16[256,1024]{1,0:T(8,128)(2,1)S(1)}, u32[]{:S(2)}, u32[]{:S(2)}) collective-permute-start(bf16[256,1024]{1,0:T(8,128)(2,1)S(1)} %feed_forward.6), channel_id=1, source_target_pairs={{0,16},{1,17},{2,18},{3,19},{4,20},{5,21},{6,22},{7,23},{8,24},{9,... | collective-permute-start | bytes 1572872 | tf_op jit(solution)/shard_map/ppermute | solution.py:521
  232.7 32.4 %collective-permute-start.27 = (bf16[256,1024]{1,0:T(8,128)(2,1)S(1)}, bf16[256,1024]{1,0:T(8,128)(2,1)S(1)}, u32[]{:S(2)}, u32[]{:S(2)}) collective-permute-start(bf16[256,1024]{1,0:T(8,128)(2,1)S(1)} %get-tuple-element.318), channel_id=1, source_target_pairs={{16,0},{17,1},{18,2},{19,3},{20,4},{21,5},{22,6},{23,7},{24,8},{25... | collective-permute-start | bytes 1572872 | tf_op jit(solution)/shard_map/ppermute | solution.py:521
  266.8 21.1 %collective-permute-start.33 = (bf16[512,2048]{1,0:T(8,128)(2,1)}, bf16[512,2048]{1,0:T(8,128)(2,1)}, u32[]{:S(2)}, u32[]{:S(2)}) collective-permute-start(bf16[512,2048]{1,0:T(8,128)(2,1)} %bitcast.40.mixed_ref.refs_8_.refs_9_), channel_id=1, source_target_pairs={{0,1},{1,0},{2,3},{3,2},{4,5},{5,4},{6,7},{7,6},{8,9},{9,8},{10,11... | collective-permute-start | bytes 6291464 | tf_op jit(solution)/shard_map/ppermute | solution.py:938
  266.8 21.1 %collective-permute-start.34 = (bf16[512,2048]{1,0:T(8,128)(2,1)}, bf16[512,2048]{1,0:T(8,128)(2,1)}, u32[]{:S(2)}, u32[]{:S(2)}) collective-permute-start(bf16[512,2048]{1,0:T(8,128)(2,1)} %get-tuple-element.360.refs_12_.refs_13_), channel_id=1, source_target_pairs={{0,1},{1,0},{2,3},{3,2},{4,5},{5,4},{6,7},{7,6},{8,9},{9,8},{10,11... | collective-permute-start | bytes 6291464 | tf_op jit(solution)/shard_map/ppermute | solution.py:938
  301.4 26.6 %collective-permute-start.37 = (bf16[256,4224]{1,0:T(8,128)(2,1)}, bf16[256,4224]{1,0:T(8,128)(2,1)}, u32[]{:S(2)}, u32[]{:S(2)}) collective-permute-start(bf16[256,4224]{1,0:T(8,128)(2,1)} %get-tuple-element.433.grad_ref.refs_4_), channel_id=1, source_target_pairs={{0,1},{1,0},{2,3},{3,2},{4,5},{5,4},{6,7},{7,6},{8,9},{9,8},{10,11... | collective-permute-start | bytes 6488072 | tf_op jit(solution)/shard_map/ppermute | solution.py:938
  301.5 26.6 %collective-permute-start.31 = (bf16[256,2048]{1,0:T(8,128)(2,1)}, bf16[256,2048]{1,0:T(8,128)(2,1)}, u32[]{:S(2)}, u32[]{:S(2)}) collective-permute-start(bf16[256,2048]{1,0:T(8,128)(2,1)} %get-tuple-element.394.refs_8_), channel_id=1, source_target_pairs={{0,1},{1,0},{2,3},{3,2},{4,5},{5,4},{6,7},{7,6},{8,9},{9,8},{10,11... | collective-permute-start | bytes 3145736 | tf_op jit(solution)/shard_map/ppermute | solution.py:938
  302.0 26.0 %collective-permute-start.32 = (bf16[256,2048]{1,0:T(8,128)(2,1)}, bf16[256,2048]{1,0:T(8,128)(2,1)}, u32[]{:S(2)}, u32[]{:S(2)}) collective-permute-start(bf16[256,2048]{1,0:T(8,128)(2,1)} %get-tuple-element.398.refs_12_), channel_id=1, source_target_pairs={{0,1},{1,0},{2,3},{3,2},{4,5},{5,4},{6,7},{7,6},{8,9},{9,8},{10,11... | collective-permute-start | bytes 3145736 | tf_op jit(solution)/shard_map/ppermute | solution.py:938
  438.1 21.1 %collective-permute-start.58 = (bf16[64,4224]{1,0:T(8,128)(2,1)S(1)}, bf16[64,4224]{1,0:T(8,128)(2,1)S(1)}, u32[]{:S(2)}, u32[]{:S(2)}) collective-permute-start(bf16[64,4224]{1,0:T(8,128)(2,1)S(1)} %get-tuple-element.493), channel_id=1, source_target_pairs={{0,4},{4,8},{8,12},{12,14},{14,10},{10,6},{6,2},{2,0},{1,5},{5,9},... | collective-permute-start | bytes 1622024 | tf_op jit(solution)/shard_map/ppermute | solution.py:954
  439.7 21.1 %collective-permute-start.59 = (bf16[64,4224]{1,0:T(8,128)(2,1)S(1)}, bf16[64,4224]{1,0:T(8,128)(2,1)S(1)}, u32[]{:S(2)}, u32[]{:S(2)}) collective-permute-start(bf16[64,4224]{1,0:T(8,128)(2,1)S(1)} %get-tuple-element.492), channel_id=1, source_target_pairs={{0,2},{4,0},{8,4},{12,8},{14,12},{10,14},{6,10},{2,6},{1,3},{5,1},... | collective-permute-start | bytes 1622024 | tf_op jit(solution)/shard_map/ppermute | solution.py:954
  440.2 22.9 %collective-permute-start.61 = (f32[16,1792]{1,0:T(8,128)S(1)}, f32[16,1792]{1,0:T(8,128)S(1)}, u32[]{:S(2)}, u32[]{:S(2)}) collective-permute-start(f32[16,1792]{1,0:T(8,128)S(1)} %add.284), channel_id=1, source_target_pairs={{0,2},{2,0},{4,6},{6,4},{8,10},{10,8},{12,14},{14,12},{1,3},{3,1},... | collective-permute-start | bytes 344072 | tf_op jit(solution)/shard_map/ppermute | solution.py:1055
  449.5 23.5 %collective-permute-start.74 = (bf16[64,4096]{1,0:T(8,128)(2,1)S(1)}, bf16[64,4096]{1,0:T(8,128)(2,1)S(1)}, u32[]{:S(2)}, u32[]{:S(2)}) collective-permute-start(bf16[64,4096]{1,0:T(8,128)(2,1)S(1)} %get-tuple-element.497), channel_id=1, source_target_pairs={{0,4},{4,8},{8,12},{12,14},{14,10},{10,6},{6,2},{2,0},{1,5},{5,9},... | collective-permute-start | bytes 1572872 | tf_op jit(solution)/shard_map/ppermute | solution.py:954
  451.0 21.9 %collective-permute-start.75 = (bf16[64,4096]{1,0:T(8,128)(2,1)S(1)}, bf16[64,4096]{1,0:T(8,128)(2,1)S(1)}, u32[]{:S(2)}, u32[]{:S(2)}) collective-permute-start(bf16[64,4096]{1,0:T(8,128)(2,1)S(1)} %get-tuple-element.496), channel_id=1, source_target_pairs={{0,2},{4,0},{8,4},{12,8},{14,12},{10,14},{6,10},{2,6},{1,3},{5,1},... | collective-permute-start | bytes 1572872 | tf_op jit(solution)/shard_map/ppermute | solution.py:954
  463.2 24.5 %collective-permute-start.68 = (bf16[64,2176]{1,0:T(8,128)(2,1)S(1)}, bf16[64,2176]{1,0:T(8,128)(2,1)S(1)}, u32[]{:S(2)}, u32[]{:S(2)}) collective-permute-start(bf16[64,2176]{1,0:T(8,128)(2,1)S(1)} %get-tuple-element.487), channel_id=1, source_target_pairs={{0,4},{4,8},{8,12},{12,14},{14,10},{10,6},{6,2},{2,0},{1,5},{5,9},... | collective-permute-start | bytes 835592 | tf_op jit(solution)/shard_map/ppermute | solution.py:954
  (138 other events, 2009.7 us)
where the time goes:
time: 512 us; the launch traced here: 503 us
  Pallas kernels  212 us (41%)
  waiting for transfers between devices  148 us (29%)
  starting transfers between devices  63.5 us (12%)
  local copies, waits for them, and re-layouts  46.4 us (9%)
  matrix products  16.6 us (3%)
  other arithmetic  12.9 us (3%)
    ppermute x44, waiting for transfers between devices, onward(): lax.ppermute(value, 'chip', [(order[at], order[(at + steps) % chips]) for...  119 us
    ppermute x44, starting transfers between devices, onward(): lax.ppermute(value, 'chip', [(order[at], order[(at + steps) % chips]) for...  46.2 us
    pallas_call x4, Pallas kernels, feed_forward(): pl.pallas_call(functools.partial(feed_forward_kernel, keep), grid=(8,), i...  40.6 us
    pallas_call x3, Pallas kernels, feed_back(): pl.pallas_call(feed_back_kernel, grid_spec=pltpu.PrefetchScalarGridSpec(n...  37.3 us
    pallas_call x3, Pallas kernels, mixer_back(): pl.pallas_call(mixer_back_kernel, grid_spec=pltpu.PrefetchScalarGridSpec(...  36.3 us
    unnamed x195, local copies, waits for them, and re-layouts  32.4 us
    pallas_call x4, Pallas kernels, core_forward(): pl.pallas_call(functools.partial(core_forward_kernel, bool(held)), grid=(...  29.6 us
    pallas_call x3, Pallas kernels, weight_grad(): pl.pallas_call(functools.partial(weight_grad_kernel, tuple(steps)), grid_...  27.3 us
  transfers between devices with their start and end apart: 76, of which 41 were waited for; matrix products, arithmetic and copies ran while one was open for 9% of the time, Pallas kernels for 36%

commit v1 on v0

--- a/solution.py
+++ b/solution.py
@@ -661,14 +661,14 @@
     if keep:
         out_specs = [full, full, full, wide, wide, wide]
         out_shape = [
-            jax.ShapeDtypeStruct((MB * TOK, width), kind)
+            pltpu.HBM((MB * TOK, width), kind)
             for width, kind in ((D, bf16), (D, f32), (D, bf16), (FF, bf16), (FF, bf16), (FF, bf16))
         ]
     else:
         out_specs = [whole_block((TOK, D))]
         out_shape = [jax.ShapeDtypeStruct((TOK, D), bf16)]
         scratch = [pltpu.VMEM((TOK, D), f32), pltpu.VMEM((TOK, D), bf16)] + scratch
-    held = tuple(held or ())
+    held = tuple(pltpu.with_memory_space_constraint(one, pltpu.HBM) for one in held or ())
     return pl.pallas_call(
         functools.partial(feed_forward_kernel, keep),
         grid=(8,),
@@ -769,7 +769,7 @@
         name="feed_back",
     )(
         row, cotangent, *(pltpu.with_memory_space_constraint(one, pltpu.HBM) for one in (gate, up)),
-        middle, gain, *(pinned(own, other) * 4),
+        pltpu.with_memory_space_constraint(middle, pltpu.HBM), gain, *(pinned(own, other) * 4),
     )
 
 
@@ -1194,6 +1194,8 @@
         row = jnp.where(is_first, (1, 1, 0)[tick], (1, 0, 1)[tick]).astype(jnp.int32).reshape(1)
         if tick == 2:
             row, lefts[1], rights[1], rows[1] = tied(row, lefts[1], rights[1], rows[1])
+            section_out = whole_order(result)
+            row, section_out = tied(row, section_out)
         loss_row = (1, 0, 1)[tick]
         cotangent = jnp.where(
             is_first, arrived, from_loss[loss_row * TOK : (loss_row + 1) * TOK]
@@ -1267,7 +1269,13 @@
                 ring_c.operands(), their_low, d_rows, pre_grad
             )
             ring_c.send(*now_c)
-            picks_now, now_c = tied(picks, now_c)
+            small_two = (pre_grad, mlp_grad, small)
+            pre_sum, mlp_sum, small_sum = (one + two for one, two in zip(rows[1][2:], small_two))
+            gain_sums = whole_order(jnp.concatenate([pre_sum, mlp_sum], axis=0))
+            small_sum = jnp.concatenate(
+                [small_sum, jnp.pad(gain_sums, ((0, 6), (0, CH - D)))], axis=0
+            )
+            picks_now, now_c, small_sum = tied(picks, now_c, small_sum)
             (p_one, their_one), (p_two, their_two) = rows[1][1], (proj_low, their_low)
             sum_a = weight_grad(
                 picks_now,
@@ -1295,10 +1303,6 @@
         if tick < 2:
             arrived = passed_along(d_low, "section", -1)
 
-    pre_sum, mlp_sum, small = (one + two for one, two in zip(rows[1][2:], rows[2][2:]))
-    gain_sums = whole_order(jnp.concatenate([pre_sum, mlp_sum], axis=0))
-    small = jnp.concatenate([small, jnp.pad(gain_sums, ((0, 6), (0, CH - D)))], axis=0)
-
     hops = small_hops(lax.axis_size("chip"))
 
     def hop_beside(small, ring):
@@ -1307,9 +1311,10 @@
         small, moved, _ = tied(small, hops.pop(0)(small), ring.ahead)
         return small + moved
 
-    small = hop_beside(small, ring_a)
+    small = hop_beside(small_sum, ring_a)
     ring_b.step()
     ring_a.step()
+    ring_c.hold(ring_a.ahead)
     small = hop_beside(small, ring_a)
     while ring_a.left > 2:
         ring_a.step()
@@ -1335,7 +1340,7 @@
     skip_sum = jnp.sum(small[6, :E].reshape(MH, MP), axis=1)
     mixer_in_grad = jnp.concatenate([share_a[:, :AT_Q], share_a[:, AT_DT : AT_DT + MH]], axis=1)
     return (
-        whole_order(result)[None],
+        section_out[None],
         whole_order(start_grad)[None],
         small[8:9, :D],
         small[9:10, :D],

time: 512 us -> 499 us (0.975)
  local copies, waits for them, and re-layouts: 46.4 us -> 36.7 us
    unnamed x195 -> x185, local copies, waits for them, and re-layouts: 32.4 us -> 20.4 us
  transfers between devices with their start and end apart: 76 -> 76, of which waited for: 41 -> 42; matrix products, arithmetic and copies ran while one was open for 9% -> 10% of each run, Pallas kernels for 36% -> 37%
where the time goes in v1:
time: 499 us; the launch traced here: 490 us
  Pallas kernels  213 us (43%)
  waiting for transfers between devices  144 us (29%)
  starting transfers between devices  63.9 us (13%)
  local copies, waits for them, and re-layouts  36.7 us (7%)
  matrix products  16.9 us (3%)
  other arithmetic  13.3 us (3%)
    ppermute x44, waiting for transfers between devices, onward(): lax.ppermute(value, 'chip', [(order[at], order[(at + steps) % chips]) for...  119 us
    ppermute x44, starting transfers between devices, onward(): lax.ppermute(value, 'chip', [(order[at], order[(at + steps) % chips]) for...  46.8 us
    pallas_call x4, Pallas kernels, feed_forward(): pl.pallas_call(functools.partial(feed_forward_kernel, keep), grid=(8,), i...  42.3 us
    pallas_call x3, Pallas kernels, feed_back(): pl.pallas_call(feed_back_kernel, grid_spec=pltpu.PrefetchScalarGridSpec(n...  37.9 us
    pallas_call x3, Pallas kernels, mixer_back(): pl.pallas_call(mixer_back_kernel, grid_spec=pltpu.PrefetchScalarGridSpec(...  36.9 us
    pallas_call x4, Pallas kernels, core_forward(): pl.pallas_call(functools.partial(core_forward_kernel, bool(held)), grid=(...  27.6 us
    pallas_call x3, Pallas kernels, weight_grad(): pl.pallas_call(functools.partial(weight_grad_kernel, tuple(steps)), grid_...  26.5 us
    unnamed x185, local copies, waits for them, and re-layouts  20.4 us
  transfers between devices with their start and end apart: 76, of which 42 were waited for; matrix products, arithmetic and copies ran while one was open for 10% of the time, Pallas kernels for 37%

profile of v1, /device:TPU:0, one launch (start us, length us, event | category | flops | bytes accessed | tf_op | source)
XLA Modules:
  0.0 490.0 jit_solution(1046782789556007669)
XLA Ops:
  27.9 15.1 %collective-permute-done.6 = bf16[64,8192]{1,0:T(8,128)(2,1)} collective-permute-done((bf16[64,8192]{1,0:T(8,128)(2,1)}, bf16[64,8192]{1,0:T(8,128)(2,1)}, u32[]{:S(2)}, u32[]{:S(2)}) %collective-permute-start.6) | collective-permute-done | bytes 1048608 | tf_op jit(solution)/shard_map/ppermute | solution.py:954
  57.4 10.7 %collective-permute-done.4 = bf16[64,4224]{1,0:T(8,128)(2,1)S(1)} collective-permute-done((bf16[64,4224]{1,0:T(8,128)(2,1)S(1)}, bf16[64,4224]{1,0:T(8,128)(2,1)S(1)}, u32[]{:S(2)}, u32[]{:S(2)}) %collective-permute-start.4) | collective-permute-done | bytes 540704 | tf_op jit(solution)/shard_map/ppermute | solution.py:954
  80.4 17.4 %collective-permute-done.8 = bf16[64,8192]{1,0:T(8,128)(2,1)S(1)} collective-permute-done((bf16[64,8192]{1,0:T(8,128)(2,1)}, bf16[64,8192]{1,0:T(8,128)(2,1)S(1)}, u32[]{:S(2)}, u32[]{:S(2)}) %collective-permute-start.8) | collective-permute-done | bytes 1048608 | tf_op jit(solution)/shard_map/ppermute | solution.py:954
  105.1 7.9 %project.3 = (bf16[512,1024]{1,0:T(8,128)(2,1)}, bf16[512,3328]{1,0:T(8,128)(2,1)S(1)}, bf16[512,768]{1,0:T(8,128)(2,1)S(1)}, f32[512,128]{1,0:T(8,128)S(1)}) custom-call(bf16[512,1024]{1,0:T(8,128)(2,1)S(1)} %fusion.23.rows_ref, f32[1,1024]{1,0:T(1,128)S(1)} %fusion.4.gain_ref, bf16[512,4224]{1,0:T(8,128)(2,1)S(1)} %constant_dynamic-update-slice_fusion.own_ref, ...), custom_call_target="tpu_custom_call" | custom-call | flops 4429185024 | bytes 12976128 | tf_op jit(solution)/shard_map/project/pallas_call | solution.py:566
  113.2 6.9 %core_forward.4 = (bf16[2,256,2048]{2,1,0:T(8,128)(2,1)S(1)}, bf16[2,256,1792]{2,1,0:T(8,128)(2,1)S(1)}, f32[2,256,1536]{2,1,0:T(8,128)S(1)}) custom-call(bf16[2,256,3328]{2,1,0:T(8,128)(2,1)S(1)} %bitcast.108, bf16[2,256,768]{2,1,0:T(8,128)(2,1)S(1)} %bitcast.115, f32[2,256,128]{2,1,0:T(8,128)S(1)} %bitcast.117, f32[2,256,256]{2,1,0:T(8,128)S(1)} %concatenate.67.rope_ref, ...), custom_call_target="tpu_custom_call" | custom-call | flops 400000000 | bytes 12582912 | tf_op jit(solution)/shard_map/core_forward/pallas_call | solution.py:425
  120.1 7.9 %collective-permute-done.13 = bf16[64,8192]{1,0:T(8,128)(2,1)S(1)} collective-permute-done((bf16[64,8192]{1,0:T(8,128)(2,1)S(1)}, bf16[64,8192]{1,0:T(8,128)(2,1)S(1)}, u32[]{:S(2)}, u32[]{:S(2)}) %collective-permute-start.13) | collective-permute-done | bytes 1048608 | tf_op jit(solution)/shard_map/ppermute | solution.py:954
  132.8 6.9 %core_forward.5 = (bf16[2,256,2048]{2,1,0:T(8,128)(2,1)S(1)}, bf16[2,256,1792]{2,1,0:T(8,128)(2,1)S(1)}, f32[2,256,1536]{2,1,0:T(8,128)S(1)}) custom-call(bf16[2,256,3328]{2,1,0:T(8,128)(2,1)S(1)} %bitcast.109, bf16[2,256,768]{2,1,0:T(8,128)(2,1)S(1)} %bitcast.116, ...), custom_call_target="tpu_custom_call", output_to_operand_aliasing={{0}: (10, {}), {1}: (11, {}), {2}: (12, {})} | custom-call | flops 400000000 | bytes 12582912 | tf_op jit(solution)/shard_map/core_forward/pallas_call | solution.py:425
  147.6 8.6 %feed_forward.4 = bf16[256,1024]{1,0:T(8,128)(2,1)S(1)} custom-call(bf16[512,1024]{1,0:T(8,128)(2,1)S(1)} %fusion.23.rows_ref, bf16[512,2048]{1,0:T(8,128)(2,1)S(1)} %bitcast.106, f32[1,1024]{1,0:T(1,128)S(1)} %fusion.3.gain_ref, bf16[512,8192]{1,0:T(8,128)(2,1)S(1)} %constant_dynamic-update-slice_fusion.9.out_own.gate_own.up_own.down_own, ...), custom_call_target="tpu_custom_call" | custom-call | flops 4294967296 | bytes 16777216 | tf_op jit(solution)/shard_map/feed_forward/pallas_call | solution.py:672
  159.7 8.6 %feed_forward.6 = bf16[256,1024]{1,0:T(8,128)(2,1)S(1)} custom-call(bf16[512,1024]{1,0:T(8,128)(2,1)S(1)} %fusion.23.rows_ref, bf16[512,2048]{1,0:T(8,128)(2,1)S(1)} %bitcast.107, f32[1,1024]{1,0:T(1,128)S(1)} %fusion.3.gain_ref, bf16[512,8192]{1,0:T(8,128)(2,1)S(1)} %constant_dynamic-update-slice_fusion.9.out_own.gate_own.up_own.down_own, ...), custom_call_target="tpu_custom_call" | custom-call | flops 4294967296 | bytes 16777216 | tf_op jit(solution)/shard_map/feed_forward/pallas_call | solution.py:672
  176.0 6.9 %core_forward.6 = (bf16[2,256,2048]{2,1,0:T(8,128)(2,1)S(1)}, bf16[2,256,1792]{2,1,0:T(8,128)(2,1)S(1)}, f32[2,256,1536]{2,1,0:T(8,128)S(1)}) custom-call(bf16[2,256,3328]{2,1,0:T(8,128)(2,1)S(1)} %bitcast.83, bf16[2,256,768]{2,1,0:T(8,128)(2,1)S(1)} %bitcast.101, f32[2,256,128]{2,1,0:T(8,128)S(1)} %bitcast.110, f32[2,256,256]{2,1,0:T(8,128)S(1)} %copy-done.20, ...), custom_call_target="tpu_custom_call" | custom-call | flops 400000000 | bytes 12582912 | tf_op jit(solution)/shard_map/core_forward/pallas_call | solution.py:425
  183.0 11.8 %feed_forward.5 = (bf16[512,1024]{1,0:T(8,128)(2,1)}, f32[512,1024]{1,0:T(8,128)}, bf16[512,1024]{1,0:T(8,128)(2,1)}, bf16[512,2048]{1,0:T(8,128)(2,1)}, bf16[51...) custom-call(bf16[256,1024]{1,0:T(8,128)(2,1)S(1)} %slice_select_fusion.2.rows_ref, bf16[512,2048]{1,0:T(8,128)(2,1)S(1)} %bitcast.96, ...), custom_call_target="tpu_custom_call" | custom-call | flops 4294967296 | bytes 16777216 | tf_op jit(solution)/shard_map/feed_forward/pallas_call | solution.py:672
  194.8 12.9 %feed_back.3 = (bf16[256,2048]{1,0:T(8,128)(2,1)}, bf16[256,2048]{1,0:T(8,128)(2,1)}, f32[256,1024]{1,0:T(8,128)S(1)}, bf16[256,1024]{1,0:T(8,128)(2,1)}, f32[256,2048]{1,0:T(8,128)S(1)}, /*index=5*/f32[1,1024]{1,0:T(1,128)}) custom-call(s32[1]{0:T(128)} %constant.154.clone.1.pick_ref, bf16[256,1024]{1,0:T(8,128)(2,1)S(1)} %broadcast_select_fusion.3.cot_ref, ...), custom_call_target="tpu_custom_call" | custom-call | flops 4294967296 | bytes 16777216 | tf_op jit(solution)/shard_map/feed_back/pallas_call | solution.py:741
  211.3 12.1 %mixer_back.3 = (bf16[256,4224]{1,0:T(8,128)(2,1)S(1)}, f32[8,1792]{1,0:T(8,128)}) custom-call(s32[1]{0:T(128)} %constant.154.clone.1.pick_ref, bf16[2,256,3328]{2,1,0:T(8,128)(2,1)S(1)} %bitcast.84, f32[2,256,128]{2,1,0:T(8,128)S(1)} %bitcast.111, bf16[2,256,1792]{2,1,0:T(8,128)(2,1)S(1)} %get-tuple-element.337.pre_ref.refs_1_, ...), custom_call_target="tpu_custom_call" | custom-call | flops 700000000 | bytes 10485760 | tf_op jit(solution)/shard_map/mixer_back/pallas_call | solution.py:480
  235.9 6.9 %core_forward.7 = (bf16[2,256,2048]{2,1,0:T(8,128)(2,1)S(1)}, bf16[2,256,1792]{2,1,0:T(8,128)(2,1)S(1)}, f32[2,256,1536]{2,1,0:T(8,128)S(1)}) custom-call(bf16[2,256,3328]{2,1,0:T(8,128)(2,1)S(1)} %bitcast.85, bf16[2,256,768]{2,1,0:T(8,128)(2,1)S(1)} %bitcast.103, ...), custom_call_target="tpu_custom_call", output_to_operand_aliasing={{0}: (10, {}), {1}: (11, {}), {2}: (12, {})} | custom-call | flops 400000000 | bytes 12582912 | tf_op jit(solution)/shard_map/core_forward/pallas_call | solution.py:425
  242.9 13.4 %feed_forward.7 = (bf16[512,1024]{1,0:T(8,128)(2,1)}, f32[512,1024]{1,0:T(8,128)}, bf16[512,1024]{1,0:T(8,128)(2,1)}, bf16[512,2048]{1,0:T(8,128)(2,1)}, bf16[51...) custom-call(bf16[256,1024]{1,0:T(8,128)(2,1)S(1)} %slice_select_fusi, ...), custom_call_target="tpu_custom_call", output_to_operand_aliasing={{0}: (11, {}), {1}: (12, {}), {2}: (13, {}), {3}: (14, {}),... | custom-call | flops 4294967296 | bytes 16777216 | tf_op jit(solution)/shard_map/feed_forward/pallas_call | solution.py:672
  264.6 13.0 %feed_back.4 = (bf16[256,2048]{1,0:T(8,128)(2,1)}, bf16[256,2048]{1,0:T(8,128)(2,1)}, f32[256,1024]{1,0:T(8,128)S(1)}, bf16[256,1024]{1,0:T(8,128)(2,1)S(1)}, f3...) custom-call(s32[1]{0:T(128)} %bitcast.42.pick_ref, bf16[256,1024]{1,0:T(8,128)(2,1)S(1)} %copy-done.47, ...), custom_call_target="tpu_custom_call" | custom-call | flops 4294967296 | bytes 16777216 | tf_op jit(solution)/shard_map/feed_back/pallas_call | solution.py:741
  280.5 12.8 %mixer_back.4 = (bf16[256,4224]{1,0:T(8,128)(2,1)}, f32[8,1792]{1,0:T(8,128)S(1)}) custom-call(s32[1]{0:T(128)} %bitcast.42.pick_ref, bf16[2,256,3328]{2,1,0:T(8,128)(2,1)S(1)} %bitcast.86, f32[2,256,128]{2,1,0:T(8,128)S(1)} %bitcast.113, bf16[2,256,1792]{2,1,0:T(8,128)(2,1)S(1)} %copy-done.30, f32[2,256,1536]{2,1,0:T(8,128)S(1)} %copy-done.13, ...), custom_call_target="tpu_custom_call" | custom-call | flops 700000000 | bytes 10485760 | tf_op jit(solution)/shard_map/mixer_back/pallas_call | solution.py:480
  307.8 10.3 %collective-permute-done.38 = bf16[256,1024]{1,0:T(8,128)(2,1)} collective-permute-done((bf16[256,1024]{1,0:T(8,128)(2,1)}, bf16[256,1024]{1,0:T(8,128)(2,1)}, u32[]{:S(2)}, u32[]{:S(2)}) %collective-permute-start.38) | collective-permute-done | bytes 524320 | tf_op jit(solution)/shard_map/ppermute | solution.py:521
  323.2 12.1 %feed_back.5 = (bf16[256,2048]{1,0:T(8,128)(2,1)S(1)}, bf16[256,2048]{1,0:T(8,128)(2,1)S(1)}, f32[256,1024]{1,0:T(8,128)S(1)}, bf16[256,1024]{1,0:T(8,128)(2,1)S...) custom-call(s32[1]{0:T(128)} %bitcast.pick_ref, bf16[256,1024]{1,0:T(8,128)(2,1)S(1)} %broadcast_select_fusion.2.cot_ref.refs_5_, ...), custom_call_target="tpu_custom_call" | custom-call | flops 4294967296 | bytes 16777216 | tf_op jit(solution)/shard_map/feed_back/pallas_call | solution.py:741
  337.0 8.8 %weight_grad.3 = bf16[512,4096]{1,0:T(8,128)(2,1)S(1)} custom-call(s32[2]{0:T(128)S(1)} %broadcast_select_fusion.4.pick_ref, bf16[256,1024]{1,0:T(8,128)(2,1)S(1)} %copy-done.54, bf16[256,1024]{1,0:T(8,128)(2,1)S(1)} %get-tuple-element.383.refs_1_, bf16[256,512]{1,0:T(8,128)(2,1)S(1)} %collective-permute-done.30.refs_2_, ...), custom_call_target="tpu_custom_call" | custom-call | flops 4294967296 | bytes 8388608 | tf_op jit(solution)/shard_map/weight_grad/pallas_call | solution.py:885
  356.7 9.3 %weight_grad.4 = bf16[512,4096]{1,0:T(8,128)(2,1)S(1)} custom-call(s32[2]{0:T(128)S(1)} %broadcast_select_fusion.4.pick_ref, bf16[512,1024]{1,0:T(8,128)(2,1)S(1)} %copy-done.28, bf16[512,1024]{1,0:T(8,128)(2,1)S(1)} %copy-done.28, bf16[512,512]{1,0:T(8,128)(2,1)} %collective-permute-done.36.refs_2_.refs_3_.refs_6_.refs_7_, ...), custom_call_target="tpu_custom_call" | custom-call | flops 4294967296 | bytes 8388608 | tf_op jit(solution)/shard_map/weight_grad/pallas_call | solution.py:885
  372.2 11.9 %mixer_back.5 = (bf16[256,4224]{1,0:T(8,128)(2,1)S(1)}, f32[8,1792]{1,0:T(8,128)S(1)}) custom-call(s32[1]{0:T(128)} %bitcast.pick_ref, bf16[2,256,3328]{2,1,0:T(8,128)(2,1)S(1)} %bitcast.87, f32[2,256,128]{2,1,0:T(8,128)S(1)} %bitcast.114, bf16[2,256,1792]{2,1,0:T(8,128)(2,1)S(1)} %copy-done.31, f32[2,256,1536]{2,1,0:T(8,128)S(1)} %copy-done.14, ...), custom_call_target="tpu_custom_call" | custom-call | flops 700000000 | bytes 10485760 | tf_op jit(solution)/shard_map/mixer_back/pallas_call | solution.py:480
  405.5 8.4 %weight_grad.5 = bf16[512,4224]{1,0:T(8,128)(2,1)S(1)} custom-call(s32[2]{0:T(128)S(1)} %broadcast_select_fusion.4.pick_ref, bf16[512,1024]{1,0:T(8,128)(2,1)S(1)} %copy-done.51, bf16[512,1024]{1,0:T(8,128)(2,1)S(1)} %copy-done.51, bf16[512,512]{1,0:T(8,128)(2,1)} %collective-permute-done.35.refs_2_.refs_3_, ...), custom_call_target="tpu_custom_call" | custom-call | flops 4429185024 | bytes 8650752 | tf_op jit(solution)/shard_map/weight_grad/pallas_call | solution.py:885
  439.3 7.6 %collective-permute-done.58 = bf16[64,4224]{1,0:T(8,128)(2,1)S(1)} collective-permute-done((bf16[64,4224]{1,0:T(8,128)(2,1)S(1)}, bf16[64,4224]{1,0:T(8,128)(2,1)S(1)}, u32[]{:S(2)}, u32[]{:S(2)}) %collective-permute-start.58) | collective-permute-done | bytes 540704 | tf_op jit(solution)/shard_map/ppermute | solution.py:954
  (446 shorter events, 239.2 us)
Async XLA Ops:
  10.0 33.1 %collective-permute-start.6 = (bf16[64,8192]{1,0:T(8,128)(2,1)}, bf16[64,8192]{1,0:T(8,128)(2,1)}, u32[]{:S(2)}, u32[]{:S(2)}) collective-permute-start(bf16[64,8192]{1,0:T(8,128)(2,1)} %get-tuple-element.525), channel_id=1, source_target_pairs={{0,4},{4,8},{8,12},{12,14},{14,10},{10,6},{6,2},{2,0},{1,5},{5,9},... | collective-permute-start | bytes 3145736 | tf_op jit(solution)/shard_map/ppermute | solution.py:954
  12.0 33.2 %collective-permute-start.7 = (bf16[64,8192]{1,0:T(8,128)(2,1)}, bf16[64,8192]{1,0:T(8,128)(2,1)}, u32[]{:S(2)}, u32[]{:S(2)}) collective-permute-start(bf16[64,8192]{1,0:T(8,128)(2,1)} %get-tuple-element.525), channel_id=1, source_target_pairs={{0,2},{4,0},{8,4},{12,8},{14,12},{10,14},{6,10},{2,6},{1,3},{5,1},... | collective-permute-start | bytes 3145736 | tf_op jit(solution)/shard_map/ppermute | solution.py:954
  12.0 38.3 %collective-permute-start.17 = (bf16[64,8192]{1,0:T(8,128)(2,1)}, bf16[64,8192]{1,0:T(8,128)(2,1)}, u32[]{:S(2)}, u32[]{:S(2)}) collective-permute-start(bf16[64,8192]{1,0:T(8,128)(2,1)} %get-tuple-element.525), channel_id=1, source_target_pairs={{0,1},{1,0},{2,3},{3,2},{4,5},{5,4},{6,7},{7,6},{8,9},{9,8},{10,11... | collective-permute-start | bytes 3145736 | tf_op jit(solution)/shard_map/ppermute | solution.py:938
  23.6 30.1 %collective-permute-start.2 = (bf16[64,4224]{1,0:T(8,128)(2,1)}, bf16[64,4224]{1,0:T(8,128)(2,1)S(1)}, u32[]{:S(2)}, u32[]{:S(2)}) collective-permute-start(bf16[64,4224]{1,0:T(8,128)(2,1)} %collective-permute-done), channel_id=1, source_target_pairs={{0,4},{4,8},{8,12},{12,14},{14,10},{10,6},{6,2},{2,0},{1,5},{5,9},... | collective-permute-start | bytes 1622024 | tf_op jit(solution)/shard_map/ppermute | solution.py:954
  25.7 29.6 %collective-permute-start.3 = (bf16[64,4224]{1,0:T(8,128)(2,1)}, bf16[64,4224]{1,0:T(8,128)(2,1)S(1)}, u32[]{:S(2)}, u32[]{:S(2)}) collective-permute-start(bf16[64,4224]{1,0:T(8,128)(2,1)} %collective-permute-done.1), channel_id=1, source_target_pairs={{0,2},{4,0},{8,4},{12,8},{14,12},{10,14},{6,10},{2,6},{1,3},{5,1},... | collective-permute-start | bytes 1622024 | tf_op jit(solution)/shard_map/ppermute | solution.py:954
  45.2 35.0 %collective-permute-start.18 = (bf16[64,8192]{1,0:T(8,128)(2,1)}, bf16[64,8192]{1,0:T(8,128)(2,1)S(1)}, u32[]{:S(2)}, u32[]{:S(2)}) collective-permute-start(bf16[64,8192]{1,0:T(8,128)(2,1)} %collective-permute-done.6), channel_id=1, source_target_pairs={{0,1},{1,0},{2,3},{3,2},{4,5},{5,4},{6,7},{7,6},{8,9},{9,8},{10,11... | collective-permute-start | bytes 3145736 | tf_op jit(solution)/shard_map/ppermute | solution.py:938
  45.2 35.1 %collective-permute-start.19 = (bf16[64,8192]{1,0:T(8,128)(2,1)}, bf16[64,8192]{1,0:T(8,128)(2,1)S(1)}, u32[]{:S(2)}, u32[]{:S(2)}) collective-permute-start(bf16[64,8192]{1,0:T(8,128)(2,1)} %collective-permute-done.7), channel_id=1, source_target_pairs={{0,1},{1,0},{2,3},{3,2},{4,5},{5,4},{6,7},{7,6},{8,9},{9,8},{10,11... | collective-permute-start | bytes 3145736 | tf_op jit(solution)/shard_map/ppermute | solution.py:938
  71.6 26.2 %collective-permute-start.8 = (bf16[64,8192]{1,0:T(8,128)(2,1)}, bf16[64,8192]{1,0:T(8,128)(2,1)S(1)}, u32[]{:S(2)}, u32[]{:S(2)}) collective-permute-start(bf16[64,8192]{1,0:T(8,128)(2,1)} %collective-permute-done.6), channel_id=1, source_target_pairs={{0,4},{4,8},{8,12},{12,14},{14,10},{10,6},{6,2},{2,0},{1,5},{5,9},... | collective-permute-start | bytes 3145736 | tf_op jit(solution)/shard_map/ppermute | solution.py:954
  78.9 21.1 %collective-permute-start.9 = (bf16[64,8192]{1,0:T(8,128)(2,1)}, bf16[64,8192]{1,0:T(8,128)(2,1)S(1)}, u32[]{:S(2)}, u32[]{:S(2)}) collective-permute-start(bf16[64,8192]{1,0:T(8,128)(2,1)} %collective-permute-done.7), channel_id=1, source_target_pairs={{0,2},{4,0},{8,4},{12,8},{14,12},{10,14},{6,10},{2,6},{1,3},{5,1},... | collective-permute-start | bytes 3145736 | tf_op jit(solution)/shard_map/ppermute | solution.py:954
  80.1 22.6 %collective-permute-start.12 = (bf16[512,4224]{1,0:T(8,128)(2,1)S(1)}, bf16[512,4224]{1,0:T(8,128)(2,1)S(1)}, u32[]{:S(2)}, u32[]{:S(2)}) collective-permute-start(bf16[512,4224]{1,0:T(8,128)(2,1)S(1)} %constant_dynamic-update-slice_fusion.own_ref), channel_id=1, source_target_pairs={{0,1},{1,0},{2,3},{3,2},{4,5},{5,4},{6,7},{7,6},{8,9},{9,8},{10,11... | collective-permute-start | bytes 12976136 | tf_op jit(solution)/shard_map/ppermute | solution.py:938
  102.7 25.3 %collective-permute-start.13 = (bf16[64,8192]{1,0:T(8,128)(2,1)S(1)}, bf16[64,8192]{1,0:T(8,128)(2,1)S(1)}, u32[]{:S(2)}, u32[]{:S(2)}) collective-permute-start(bf16[64,8192]{1,0:T(8,128)(2,1)S(1)} %collective-permute-done.8), channel_id=1, source_target_pairs={{0,4},{4,8},{8,12},{12,14},{14,10},{10,6},{6,2},{2,0},{1,5},{5,9},... | collective-permute-start | bytes 3145736 | tf_op jit(solution)/shard_map/ppermute | solution.py:954
  104.3 25.2 %collective-permute-start.14 = (bf16[64,8192]{1,0:T(8,128)(2,1)S(1)}, bf16[64,8192]{1,0:T(8,128)(2,1)S(1)}, u32[]{:S(2)}, u32[]{:S(2)}) collective-permute-start(bf16[64,8192]{1,0:T(8,128)(2,1)S(1)} %collective-permute-done.9), channel_id=1, source_target_pairs={{0,2},{4,0},{8,4},{12,8},{14,12},{10,14},{6,10},{2,6},{1,3},{5,1},... | collective-permute-start | bytes 3145736 | tf_op jit(solution)/shard_map/ppermute | solution.py:954
  168.2 62.1 %collective-permute-start.28 = (bf16[256,1024]{1,0:T(8,128)(2,1)S(1)}, bf16[256,1024]{1,0:T(8,128)(2,1)S(1)}, u32[]{:S(2)}, u32[]{:S(2)}) collective-permute-start(bf16[256,1024]{1,0:T(8,128)(2,1)S(1)} %feed_forward.6), channel_id=1, source_target_pairs={{0,16},{1,17},{2,18},{3,19},{4,20},{5,21},{6,22},{7,23},{8,24},{9,... | collective-permute-start | bytes 1572872 | tf_op jit(solution)/shard_map/ppermute | solution.py:521
  229.0 27.3 %collective-permute-start.27 = (bf16[256,1024]{1,0:T(8,128)(2,1)S(1)}, bf16[256,1024]{1,0:T(8,128)(2,1)S(1)}, u32[]{:S(2)}, u32[]{:S(2)}) collective-permute-start(bf16[256,1024]{1,0:T(8,128)(2,1)S(1)} %get-tuple-element.323), channel_id=1, source_target_pairs={{16,0},{17,1},{18,2},{19,3},{20,4},{21,5},{22,6},{23,7},{24,8},{25... | collective-permute-start | bytes 1572872 | tf_op jit(solution)/shard_map/ppermute | solution.py:521
  259.1 21.3 %collective-permute-start.33 = (bf16[512,2048]{1,0:T(8,128)(2,1)S(1)}, bf16[512,2048]{1,0:T(8,128)(2,1)}, u32[]{:S(2)}, u32[]{:S(2)}) collective-permute-start(bf16[512,2048]{1,0:T(8,128)(2,1)S(1)} %bitcast.98), channel_id=1, source_target_pairs={{0,1},{1,0},{2,3},{3,2},{4,5},{5,4},{6,7},{7,6},{8,9},{9,8},{10,11... | collective-permute-start | bytes 6291464 | tf_op jit(solution)/shard_map/ppermute | solution.py:938
  259.1 21.3 %collective-permute-start.34 = (bf16[512,2048]{1,0:T(8,128)(2,1)}, bf16[512,2048]{1,0:T(8,128)(2,1)}, u32[]{:S(2)}, u32[]{:S(2)}) collective-permute-start(bf16[512,2048]{1,0:T(8,128)(2,1)} %get-tuple-element.364.refs_12_.refs_13_), channel_id=1, source_target_pairs={{0,1},{1,0},{2,3},{3,2},{4,5},{5,4},{6,7},{7,6},{8,9},{9,8},{10,11... | collective-permute-start | bytes 6291464 | tf_op jit(solution)/shard_map/ppermute | solution.py:938
  293.3 26.5 %collective-permute-start.37 = (bf16[256,4224]{1,0:T(8,128)(2,1)}, bf16[256,4224]{1,0:T(8,128)(2,1)}, u32[]{:S(2)}, u32[]{:S(2)}) collective-permute-start(bf16[256,4224]{1,0:T(8,128)(2,1)} %get-tuple-element.446.grad_ref.refs_4_), channel_id=1, source_target_pairs={{0,1},{1,0},{2,3},{3,2},{4,5},{5,4},{6,7},{7,6},{8,9},{9,8},{10,11... | collective-permute-start | bytes 6488072 | tf_op jit(solution)/shard_map/ppermute | solution.py:938
  293.3 26.5 %collective-permute-start.31 = (bf16[256,2048]{1,0:T(8,128)(2,1)}, bf16[256,2048]{1,0:T(8,128)(2,1)}, u32[]{:S(2)}, u32[]{:S(2)}) collective-permute-start(bf16[256,2048]{1,0:T(8,128)(2,1)} %get-tuple-element.401.refs_8_), channel_id=1, source_target_pairs={{0,1},{1,0},{2,3},{3,2},{4,5},{5,4},{6,7},{7,6},{8,9},{9,8},{10,11... | collective-permute-start | bytes 3145736 | tf_op jit(solution)/shard_map/ppermute | solution.py:938
  293.8 26.0 %collective-permute-start.32 = (bf16[256,2048]{1,0:T(8,128)(2,1)}, bf16[256,2048]{1,0:T(8,128)(2,1)}, u32[]{:S(2)}, u32[]{:S(2)}) collective-permute-start(bf16[256,2048]{1,0:T(8,128)(2,1)} %get-tuple-element.405.refs_12_), channel_id=1, source_target_pairs={{0,1},{1,0},{2,3},{3,2},{4,5},{5,4},{6,7},{7,6},{8,9},{9,8},{10,11... | collective-permute-start | bytes 3145736 | tf_op jit(solution)/shard_map/ppermute | solution.py:938
  425.8 21.1 %collective-permute-start.58 = (bf16[64,4224]{1,0:T(8,128)(2,1)S(1)}, bf16[64,4224]{1,0:T(8,128)(2,1)S(1)}, u32[]{:S(2)}, u32[]{:S(2)}) collective-permute-start(bf16[64,4224]{1,0:T(8,128)(2,1)S(1)} %get-tuple-element.503), channel_id=1, source_target_pairs={{0,4},{4,8},{8,12},{12,14},{14,10},{10,6},{6,2},{2,0},{1,5},{5,9},... | collective-permute-start | bytes 1622024 | tf_op jit(solution)/shard_map/ppermute | solution.py:954
  427.5 21.0 %collective-permute-start.59 = (bf16[64,4224]{1,0:T(8,128)(2,1)S(1)}, bf16[64,4224]{1,0:T(8,128)(2,1)S(1)}, u32[]{:S(2)}, u32[]{:S(2)}) collective-permute-start(bf16[64,4224]{1,0:T(8,128)(2,1)S(1)} %get-tuple-element.502), channel_id=1, source_target_pairs={{0,2},{4,0},{8,4},{12,8},{14,12},{10,14},{6,10},{2,6},{1,3},{5,1},... | collective-permute-start | bytes 1622024 | tf_op jit(solution)/shard_map/ppermute | solution.py:954
  428.1 29.6 %collective-permute-start.61 = (f32[16,1792]{1,0:T(8,128)S(1)}, f32[16,1792]{1,0:T(8,128)S(1)}, u32[]{:S(2)}, u32[]{:S(2)}) collective-permute-start(f32[16,1792]{1,0:T(8,128)S(1)} %add.284), channel_id=1, source_target_pairs={{0,2},{2,0},{4,6},{6,4},{8,10},{10,8},{12,14},{14,12},{1,3},{3,1},... | collective-permute-start | bytes 344072 | tf_op jit(solution)/shard_map/ppermute | solution.py:1055
  437.2 23.4 %collective-permute-start.74 = (bf16[64,4096]{1,0:T(8,128)(2,1)S(1)}, bf16[64,4096]{1,0:T(8,128)(2,1)S(1)}, u32[]{:S(2)}, u32[]{:S(2)}) collective-permute-start(bf16[64,4096]{1,0:T(8,128)(2,1)S(1)} %get-tuple-element.507), channel_id=1, source_target_pairs={{0,4},{4,8},{8,12},{12,14},{14,10},{10,6},{6,2},{2,0},{1,5},{5,9},... | collective-permute-start | bytes 1572872 | tf_op jit(solution)/shard_map/ppermute | solution.py:954
  438.7 21.9 %collective-permute-start.75 = (bf16[64,4096]{1,0:T(8,128)(2,1)S(1)}, bf16[64,4096]{1,0:T(8,128)(2,1)S(1)}, u32[]{:S(2)}, u32[]{:S(2)}) collective-permute-start(bf16[64,4096]{1,0:T(8,128)(2,1)S(1)} %get-tuple-element.506), channel_id=1, source_target_pairs={{0,2},{4,0},{8,4},{12,8},{14,12},{10,14},{6,10},{2,6},{1,3},{5,1},... | collective-permute-start | bytes 1572872 | tf_op jit(solution)/shard_map/ppermute | solution.py:954
  (133 other events, 2456.0 us)

commit v2 on v1

--- a/solution.py
+++ b/solution.py
@@ -26,8 +26,8 @@
 LANES = 128
 SIDE = D // 2
 MIB = 2**20
-FF_VMEM = 22
-FB_VMEM = 20
+FF_VMEM = 19
+FB_VMEM = 17
 
 AT_W = E
 AT_Q = E + CH
@@ -413,12 +413,15 @@
 
 def core_forward(row, projected, layout, params, held=()):
     operands = (*projected, *layout)
+    held = tuple(held)
+    if held:
+        held = (pltpu.with_memory_space_constraint(held[0], pltpu.HBM),) + held[1:]
 
     def block(array):
         return once((None,) + array.shape[1:], lambda step: (row, 0, 0))
 
     outs = [
-        jax.ShapeDtypeStruct((MB, TOK, MIXED), bf16),
+        pltpu.HBM((MB, TOK, MIXED), bf16),
         jax.ShapeDtypeStruct((MB, TOK, CH), bf16),
         jax.ShapeDtypeStruct((MB, TOK, E), f32),
     ]
@@ -562,6 +565,9 @@
     weight = pl.BlockSpec((SIDE, tile), lambda step: (0, step))
     at = row or 0
     total = count if row is None else MB * TOK
+    held = tuple(held)
+    if held:
+        held = (pltpu.with_memory_space_constraint(held[0], pltpu.HBM),) + held[1:]
     widths = ((D, bf16), (AT_Q, bf16), (AT_DT - AT_Q, bf16), (LANES, f32))
     return pl.pallas_call(
         project_kernel,
@@ -569,7 +575,8 @@
         in_specs=[whole_block((count, D)), whole_block((1, D)), weight, weight]
         + [pl.BlockSpec(memory_space=pl.ANY)] * len(held),
         out_specs=[pl.BlockSpec((count, width), lambda step: (at, 0)) for width, _ in widths],
-        out_shape=[jax.ShapeDtypeStruct((total, width), kind) for width, kind in widths],
+        out_shape=[pltpu.HBM((total, D), bf16)]
+        + [jax.ShapeDtypeStruct((total, width), kind) for width, kind in widths[1:]],
         input_output_aliases={4 + index: index for index in range(len(held))},
         compiler_params=pltpu.CompilerParams(vmem_limit_bytes=15 * MIB),
         cost_estimate=pl.CostEstimate(
@@ -634,7 +641,7 @@
 def pinned(own, other):
     return [
         pltpu.with_memory_space_constraint(own, pltpu.VMEM),
-        pltpu.with_memory_space_constraint(other, pltpu.HBM),
+        pltpu.with_memory_space_constraint(other, pltpu.VMEM),
     ]
 
 
@@ -668,7 +675,9 @@
         out_specs = [whole_block((TOK, D))]
         out_shape = [jax.ShapeDtypeStruct((TOK, D), bf16)]
         scratch = [pltpu.VMEM((TOK, D), f32), pltpu.VMEM((TOK, D), bf16)] + scratch
-    held = tuple(pltpu.with_memory_space_constraint(one, pltpu.HBM) for one in held or ())
+    mixed, *held = (
+        pltpu.with_memory_space_constraint(one, pltpu.HBM) for one in (mixed, *(held or ()))
+    )
     return pl.pallas_call(
         functools.partial(feed_forward_kernel, keep),
         grid=(8,),
@@ -755,8 +764,8 @@
             scratch_shapes=[pltpu.VMEM((TOK, D), f32)],
         ),
         out_shape=[
-            jax.ShapeDtypeStruct((TOK, FF), bf16),
-            jax.ShapeDtypeStruct((TOK, FF), bf16),
+            pltpu.HBM((TOK, FF), bf16),
+            pltpu.HBM((TOK, FF), bf16),
             jax.ShapeDtypeStruct((TOK, D), f32),
             jax.ShapeDtypeStruct((TOK, D), bf16),
             jax.ShapeDtypeStruct((TOK, MIXED), f32),

time: 499 us -> 505 us (1.012)
  local copies, waits for them, and re-layouts: 36.7 us -> 42 us
    unnamed x185 -> x177, local copies, waits for them, and re-layouts: 20.4 us -> 25.1 us
  transfers between devices with their start and end apart: 76 -> 76, of which waited for: 42 -> 43; matrix products, arithmetic and copies ran while one was open for 10% -> 9% of each run, Pallas kernels for 37% -> 37%
where the time goes in v2:
time: 505 us; the launch traced here: 496 us
  Pallas kernels  216 us (43%)
  waiting for transfers between devices  142 us (28%)
  starting transfers between devices  63.9 us (13%)
  local copies, waits for them, and re-layouts  42 us (8%)
  matrix products  16.9 us (3%)
  other arithmetic  13.2 us (3%)
    ppermute x44, waiting for transfers between devices, onward(): lax.ppermute(value, 'chip', [(order[at], order[(at + steps) % chips]) for...  119 us
    ppermute x44, starting transfers between devices, onward(): lax.ppermute(value, 'chip', [(order[at], order[(at + steps) % chips]) for...  46.8 us
    pallas_call x4, Pallas kernels, feed_forward(): pl.pallas_call(functools.partial(feed_forward_kernel, keep), grid=(8,), i...  42.3 us
    pallas_call x3, Pallas kernels, mixer_back(): pl.pallas_call(mixer_back_kernel, grid_spec=pltpu.PrefetchScalarGridSpec(...  36.6 us
    pallas_call x3, Pallas kernels, feed_back(): pl.pallas_call(feed_back_kernel, grid_spec=pltpu.PrefetchScalarGridSpec(n...  35.5 us
    pallas_call x4, Pallas kernels, core_forward(): pl.pallas_call(functools.partial(core_forward_kernel, bool(held)), grid=(...  31.5 us
    pallas_call x3, Pallas kernels, weight_grad(): pl.pallas_call(functools.partial(weight_grad_kernel, tuple(steps)), grid_...  26.6 us
    unnamed x177, local copies, waits for them, and re-layouts  25.1 us
  transfers between devices with their start and end apart: 76, of which 43 were waited for; matrix products, arithmetic and copies ran while one was open for 9% of the time, Pallas kernels for 37%

profile of v2, /device:TPU:0, one launch (start us, length us, event | category | flops | bytes accessed | tf_op | source)
XLA Modules:
  0.0 496.2 jit_solution(12354136264273661232)
XLA Ops:
  26.1 16.1 %collective-permute-done.6 = bf16[64,8192]{1,0:T(8,128)(2,1)} collective-permute-done((bf16[64,8192]{1,0:T(8,128)(2,1)}, bf16[64,8192]{1,0:T(8,128)(2,1)}, u32[]{:S(2)}, u32[]{:S(2)}) %collective-permute-start.6) | collective-permute-done | bytes 1048608 | tf_op jit(solution)/shard_map/ppermute | solution.py:963
  56.5 10.7 %collective-permute-done.4 = bf16[64,4224]{1,0:T(8,128)(2,1)S(1)} collective-permute-done((bf16[64,4224]{1,0:T(8,128)(2,1)S(1)}, bf16[64,4224]{1,0:T(8,128)(2,1)S(1)}, u32[]{:S(2)}, u32[]{:S(2)}) %collective-permute-start.4) | collective-permute-done | bytes 540704 | tf_op jit(solution)/shard_map/ppermute | solution.py:963
  79.5 17.4 %collective-permute-done.8 = bf16[64,8192]{1,0:T(8,128)(2,1)S(1)} collective-permute-done((bf16[64,8192]{1,0:T(8,128)(2,1)}, bf16[64,8192]{1,0:T(8,128)(2,1)S(1)}, u32[]{:S(2)}, u32[]{:S(2)}) %collective-permute-start.8) | collective-permute-done | bytes 1048608 | tf_op jit(solution)/shard_map/ppermute | solution.py:963
  104.3 7.9 %project.3 = (bf16[512,1024]{1,0:T(8,128)(2,1)}, bf16[512,3328]{1,0:T(8,128)(2,1)S(1)}, bf16[512,768]{1,0:T(8,128)(2,1)S(1)}, f32[512,128]{1,0:T(8,128)S(1)}) custom-call(bf16[512,1024]{1,0:T(8,128)(2,1)S(1)} %fusion.23.rows_ref, f32[1,1024]{1,0:T(1,128)S(1)} %fusion.4.gain_ref, bf16[512,4224]{1,0:T(8,128)(2,1)S(1)} %constant_dynamic-update-slice_fusion.own_ref, ...), custom_call_target="tpu_custom_call" | custom-call | flops 4429185024 | bytes 12976128 | tf_op jit(solution)/shard_map/project/pallas_call | solution.py:572
  112.3 7.9 %core_forward.4 = (bf16[2,256,2048]{2,1,0:T(8,128)(2,1)}, bf16[2,256,1792]{2,1,0:T(8,128)(2,1)S(1)}, f32[2,256,1536]{2,1,0:T(8,128)S(1)}) custom-call(bf16[2,256,3328]{2,1,0:T(8,128)(2,1)S(1)} %bitcast.106, bf16[2,256,768]{2,1,0:T(8,128)(2,1)S(1)} %bitcast.113, f32[2,256,128]{2,1,0:T(8,128)S(1)} %bitcast.115, f32[2,256,256]{2,1,0:T(8,128)S(1)} %concatenate.67.rope_ref, ...), custom_call_target="tpu_custom_call" | custom-call | flops 400000000 | bytes 12582912 | tf_op jit(solution)/shard_map/core_forward/pallas_call | solution.py:428
  120.2 6.9 %collective-permute-done.13 = bf16[64,8192]{1,0:T(8,128)(2,1)S(1)} collective-permute-done((bf16[64,8192]{1,0:T(8,128)(2,1)S(1)}, bf16[64,8192]{1,0:T(8,128)(2,1)S(1)}, u32[]{:S(2)}, u32[]{:S(2)}) %collective-permute-start.13) | collective-permute-done | bytes 1048608 | tf_op jit(solution)/shard_map/ppermute | solution.py:963
  131.9 7.9 %core_forward.5 = (bf16[2,256,2048]{2,1,0:T(8,128)(2,1)}, bf16[2,256,1792]{2,1,0:T(8,128)(2,1)S(1)}, f32[2,256,1536]{2,1,0:T(8,128)S(1)}) custom-call(bf16[2,256,3328]{2,1,0:T(8,128)(2,1)S(1)} %bitcast.107, bf16[2,256,768]{2,1,0:T(8,128)(2,1)S(1)} %bitcast.114, ...), custom_call_target="tpu_custom_call", output_to_operand_aliasing={{0}: (10, {}), {1}: (11, {}), {2}: (12, {})} | custom-call | flops 400000000 | bytes 12582912 | tf_op jit(solution)/shard_map/core_forward/pallas_call | solution.py:428
  146.7 9.9 %feed_forward.4 = bf16[256,1024]{1,0:T(8,128)(2,1)S(1)} custom-call(bf16[512,1024]{1,0:T(8,128)(2,1)S(1)} %fusion.23.rows_ref, bf16[512,2048]{1,0:T(8,128)(2,1)} %bitcast.117, f32[1,1024]{1,0:T(1,128)S(1)} %fusion.3.gain_ref, bf16[512,8192]{1,0:T(8,128)(2,1)S(1)} %constant_dynamic-update-slice_fusion.9.out_own.gate_own.up_own.down_own, ...), custom_call_target="tpu_custom_call" | custom-call | flops 4294967296 | bytes 16777216 | tf_op jit(solution)/shard_map/feed_forward/pallas_call | solution.py:681
  160.1 9.3 %feed_forward.6 = bf16[256,1024]{1,0:T(8,128)(2,1)S(1)} custom-call(bf16[512,1024]{1,0:T(8,128)(2,1)S(1)} %fusion.23.rows_ref, bf16[512,2048]{1,0:T(8,128)(2,1)} %bitcast.118, f32[1,1024]{1,0:T(1,128)S(1)} %fusion.3.gain_ref, bf16[512,8192]{1,0:T(8,128)(2,1)S(1)} %constant_dynamic-update-slice_fusion.9.out_own.gate_own.up_own.down_own, ...), custom_call_target="tpu_custom_call" | custom-call | flops 4294967296 | bytes 16777216 | tf_op jit(solution)/shard_map/feed_forward/pallas_call | solution.py:681
  176.9 7.9 %core_forward.6 = (bf16[2,256,2048]{2,1,0:T(8,128)(2,1)}, bf16[2,256,1792]{2,1,0:T(8,128)(2,1)S(1)}, f32[2,256,1536]{2,1,0:T(8,128)S(1)}) custom-call(bf16[2,256,3328]{2,1,0:T(8,128)(2,1)S(1)} %bitcast.83, bf16[2,256,768]{2,1,0:T(8,128)(2,1)S(1)} %bitcast.101, f32[2,256,128]{2,1,0:T(8,128)S(1)} %bitcast.108, f32[2,256,256]{2,1,0:T(8,128)S(1)} %concatenate.67.rope_ref, ...), custom_call_target="tpu_custom_call" | custom-call | flops 400000000 | bytes 12582912 | tf_op jit(solution)/shard_map/core_forward/pallas_call | solution.py:428
  184.8 11.2 %feed_forward.5 = (bf16[512,1024]{1,0:T(8,128)(2,1)}, f32[512,1024]{1,0:T(8,128)}, bf16[512,1024]{1,0:T(8,128)(2,1)}, bf16[512,2048]{1,0:T(8,128)(2,1)}, bf16[51...) custom-call(bf16[256,1024]{1,0:T(8,128)(2,1)S(1)} %slice_select_fusion.2.rows_ref, bf16[512,2048]{1,0:T(8,128)(2,1)} %bitcast.96, ...), custom_call_target="tpu_custom_call" | custom-call | flops 4294967296 | bytes 16777216 | tf_op jit(solution)/shard_map/feed_forward/pallas_call | solution.py:681
  196.0 11.8 %feed_back.3 = (bf16[256,2048]{1,0:T(8,128)(2,1)}, bf16[256,2048]{1,0:T(8,128)(2,1)}, f32[256,1024]{1,0:T(8,128)S(1)}, bf16[256,1024]{1,0:T(8,128)(2,1)}, f32[256,2048]{1,0:T(8,128)S(1)}, /*index=5*/f32[1,1024]{1,0:T(1,128)}) custom-call(s32[1]{0:T(128)} %constant.154.clone.1.pick_ref, bf16[256,1024]{1,0:T(8,128)(2,1)S(1)} %broadcast_select_fusion.3.cot_ref, ...), custom_call_target="tpu_custom_call" | custom-call | flops 4294967296 | bytes 16777216 | tf_op jit(solution)/shard_map/feed_back/pallas_call | solution.py:750
  210.5 11.9 %mixer_back.3 = (bf16[256,4224]{1,0:T(8,128)(2,1)S(1)}, f32[8,1792]{1,0:T(8,128)}) custom-call(s32[1]{0:T(128)} %constant.154.clone.1.pick_ref, bf16[2,256,3328]{2,1,0:T(8,128)(2,1)S(1)} %bitcast.84, f32[2,256,128]{2,1,0:T(8,128)S(1)} %bitcast.109, bf16[2,256,1792]{2,1,0:T(8,128)(2,1)S(1)} %get-tuple-element.337.pre_ref.refs_1_, ...), custom_call_target="tpu_custom_call" | custom-call | flops 700000000 | bytes 10485760 | tf_op jit(solution)/shard_map/mixer_back/pallas_call | solution.py:483
  237.1 7.9 %core_forward.7 = (bf16[2,256,2048]{2,1,0:T(8,128)(2,1)}, bf16[2,256,1792]{2,1,0:T(8,128)(2,1)S(1)}, f32[2,256,1536]{2,1,0:T(8,128)S(1)}) custom-call(bf16[2,256,3328]{2,1,0:T(8,128)(2,1)S(1)} %bitcast.85, bf16[2,256,768]{2,1,0:T(8,128)(2,1)S(1)} %bitcast.103, ...), custom_call_target="tpu_custom_call", output_to_operand_aliasing={{0}: (10, {}), {1}: (11, {}), {2}: (12, {})} | custom-call | flops 400000000 | bytes 12582912 | tf_op jit(solution)/shard_map/core_forward/pallas_call | solution.py:428
  245.0 11.9 %feed_forward.7 = (bf16[512,1024]{1,0:T(8,128)(2,1)}, f32[512,1024]{1,0:T(8,128)}, bf16[512,1024]{1,0:T(8,128)(2,1)}, bf16[512,2048]{1,0:T(8,128)(2,1)}, bf16[51...) custom-call(bf16[256,1024]{1,0:T(8,128)(2,1)S(1)} %slice_select_fusi, ...), custom_call_target="tpu_custom_call", output_to_operand_aliasing={{0}: (11, {}), {1}: (12, {}), {2}: (13, {}), {3}: (14, {}),... | custom-call | flops 4294967296 | bytes 16777216 | tf_op jit(solution)/shard_map/feed_forward/pallas_call | solution.py:681
  268.6 11.8 %feed_back.4 = (bf16[256,2048]{1,0:T(8,128)(2,1)}, bf16[256,2048]{1,0:T(8,128)(2,1)}, f32[256,1024]{1,0:T(8,128)S(1)}, bf16[256,1024]{1,0:T(8,128)(2,1)S(1)}, f3...) custom-call(s32[1]{0:T(128)} %bitcast.42.pick_ref, bf16[256,1024]{1,0:T(8,128)(2,1)S(1)} %copy-done.42, ...), custom_call_target="tpu_custom_call" | custom-call | flops 4294967296 | bytes 16777216 | tf_op jit(solution)/shard_map/feed_back/pallas_call | solution.py:750
  283.3 12.9 %mixer_back.4 = (bf16[256,4224]{1,0:T(8,128)(2,1)}, f32[8,1792]{1,0:T(8,128)S(1)}) custom-call(s32[1]{0:T(128)} %bitcast.42.pick_ref, bf16[2,256,3328]{2,1,0:T(8,128)(2,1)S(1)} %bitcast.86, f32[2,256,128]{2,1,0:T(8,128)S(1)} %bitcast.111, bf16[2,256,1792]{2,1,0:T(8,128)(2,1)S(1)} %copy-done.30, f32[2,256,1536]{2,1,0:T(8,128)S(1)} %copy-done.18, ...), custom_call_target="tpu_custom_call" | custom-call | flops 700000000 | bytes 10485760 | tf_op jit(solution)/shard_map/mixer_back/pallas_call | solution.py:483
  310.6 10.3 %collective-permute-done.38 = bf16[256,1024]{1,0:T(8,128)(2,1)} collective-permute-done((bf16[256,1024]{1,0:T(8,128)(2,1)}, bf16[256,1024]{1,0:T(8,128)(2,1)}, u32[]{:S(2)}, u32[]{:S(2)}) %collective-permute-start.38) | collective-permute-done | bytes 524320 | tf_op jit(solution)/shard_map/ppermute | solution.py:524
  329.6 12.0 %feed_back.5 = (bf16[256,2048]{1,0:T(8,128)(2,1)}, bf16[256,2048]{1,0:T(8,128)(2,1)}, f32[256,1024]{1,0:T(8,128)S(1)}, bf16[256,1024]{1,0:T(8,128)(2,1)S(1)}, f3...) custom-call(s32[1]{0:T(128)} %bitcast.pick_ref, bf16[256,1024]{1,0:T(8,128)(2,1)S(1)} %broadcast_select_fusion.2.cot_ref.refs_5_, ...), custom_call_target="tpu_custom_call" | custom-call | flops 4294967296 | bytes 16777216 | tf_op jit(solution)/shard_map/feed_back/pallas_call | solution.py:750
  343.1 8.8 %weight_grad.3 = bf16[512,4096]{1,0:T(8,128)(2,1)S(1)} custom-call(s32[2]{0:T(128)S(1)} %broadcast_select_fusion.4.pick_ref, bf16[256,1024]{1,0:T(8,128)(2,1)S(1)} %copy-done.48, bf16[256,1024]{1,0:T(8,128)(2,1)S(1)} %get-tuple-element.383.refs_1_, bf16[256,512]{1,0:T(8,128)(2,1)S(1)} %collective-permute-done.30.refs_2_, ...), custom_call_target="tpu_custom_call" | custom-call | flops 4294967296 | bytes 8388608 | tf_op jit(solution)/shard_map/weight_grad/pallas_call | solution.py:894
  362.9 9.4 %weight_grad.4 = bf16[512,4096]{1,0:T(8,128)(2,1)S(1)} custom-call(s32[2]{0:T(128)S(1)} %broadcast_select_fusion.4.pick_ref, bf16[512,1024]{1,0:T(8,128)(2,1)S(1)} %copy-done.26, bf16[512,1024]{1,0:T(8,128)(2,1)S(1)} %copy-done.26, bf16[512,512]{1,0:T(8,128)(2,1)} %collective-permute-done.36.refs_2_.refs_3_.refs_6_.refs_7_, ...), custom_call_target="tpu_custom_call" | custom-call | flops 4294967296 | bytes 8388608 | tf_op jit(solution)/shard_map/weight_grad/pallas_call | solution.py:894
  378.4 11.8 %mixer_back.5 = (bf16[256,4224]{1,0:T(8,128)(2,1)S(1)}, f32[8,1792]{1,0:T(8,128)S(1)}) custom-call(s32[1]{0:T(128)} %bitcast.pick_ref, bf16[2,256,3328]{2,1,0:T(8,128)(2,1)S(1)} %bitcast.87, f32[2,256,128]{2,1,0:T(8,128)S(1)} %bitcast.112, bf16[2,256,1792]{2,1,0:T(8,128)(2,1)S(1)} %copy-done.31, f32[2,256,1536]{2,1,0:T(8,128)S(1)} %copy-done.19, ...), custom_call_target="tpu_custom_call" | custom-call | flops 700000000 | bytes 10485760 | tf_op jit(solution)/shard_map/mixer_back/pallas_call | solution.py:483
  411.7 8.4 %weight_grad.5 = bf16[512,4224]{1,0:T(8,128)(2,1)S(1)} custom-call(s32[2]{0:T(128)S(1)} %broadcast_select_fusion.4.pick_ref, bf16[512,1024]{1,0:T(8,128)(2,1)S(1)} %copy-done.46, bf16[512,1024]{1,0:T(8,128)(2,1)S(1)} %copy-done.46, bf16[512,512]{1,0:T(8,128)(2,1)} %collective-permute-done.35.refs_2_.refs_3_, ...), custom_call_target="tpu_custom_call" | custom-call | flops 4429185024 | bytes 8650752 | tf_op jit(solution)/shard_map/weight_grad/pallas_call | solution.py:894
  445.4 7.6 %collective-permute-done.58 = bf16[64,4224]{1,0:T(8,128)(2,1)S(1)} collective-permute-done((bf16[64,4224]{1,0:T(8,128)(2,1)S(1)}, bf16[64,4224]{1,0:T(8,128)(2,1)S(1)}, u32[]{:S(2)}, u32[]{:S(2)}) %collective-permute-start.58) | collective-permute-done | bytes 540704 | tf_op jit(solution)/shard_map/ppermute | solution.py:963
  (438 shorter events, 244.3 us)
Async XLA Ops:
  9.3 32.8 %collective-permute-start.6 = (bf16[64,8192]{1,0:T(8,128)(2,1)}, bf16[64,8192]{1,0:T(8,128)(2,1)}, u32[]{:S(2)}, u32[]{:S(2)}) collective-permute-start(bf16[64,8192]{1,0:T(8,128)(2,1)} %get-tuple-element.525), channel_id=1, source_target_pairs={{0,4},{4,8},{8,12},{12,14},{14,10},{10,6},{6,2},{2,0},{1,5},{5,9},... | collective-permute-start | bytes 3145736 | tf_op jit(solution)/shard_map/ppermute | solution.py:963
  11.4 33.0 %collective-permute-start.7 = (bf16[64,8192]{1,0:T(8,128)(2,1)}, bf16[64,8192]{1,0:T(8,128)(2,1)}, u32[]{:S(2)}, u32[]{:S(2)}) collective-permute-start(bf16[64,8192]{1,0:T(8,128)(2,1)} %get-tuple-element.525), channel_id=1, source_target_pairs={{0,2},{4,0},{8,4},{12,8},{14,12},{10,14},{6,10},{2,6},{1,3},{5,1},... | collective-permute-start | bytes 3145736 | tf_op jit(solution)/shard_map/ppermute | solution.py:963
  11.4 38.1 %collective-permute-start.17 = (bf16[64,8192]{1,0:T(8,128)(2,1)}, bf16[64,8192]{1,0:T(8,128)(2,1)}, u32[]{:S(2)}, u32[]{:S(2)}) collective-permute-start(bf16[64,8192]{1,0:T(8,128)(2,1)} %get-tuple-element.525), channel_id=1, source_target_pairs={{0,1},{1,0},{2,3},{3,2},{4,5},{5,4},{6,7},{7,6},{8,9},{9,8},{10,11... | collective-permute-start | bytes 3145736 | tf_op jit(solution)/shard_map/ppermute | solution.py:947
  21.9 30.9 %collective-permute-start.2 = (bf16[64,4224]{1,0:T(8,128)(2,1)}, bf16[64,4224]{1,0:T(8,128)(2,1)S(1)}, u32[]{:S(2)}, u32[]{:S(2)}) collective-permute-start(bf16[64,4224]{1,0:T(8,128)(2,1)} %collective-permute-done), channel_id=1, source_target_pairs={{0,4},{4,8},{8,12},{12,14},{14,10},{10,6},{6,2},{2,0},{1,5},{5,9},... | collective-permute-start | bytes 1622024 | tf_op jit(solution)/shard_map/ppermute | solution.py:963
  23.8 30.5 %collective-permute-start.3 = (bf16[64,4224]{1,0:T(8,128)(2,1)}, bf16[64,4224]{1,0:T(8,128)(2,1)S(1)}, u32[]{:S(2)}, u32[]{:S(2)}) collective-permute-start(bf16[64,4224]{1,0:T(8,128)(2,1)} %collective-permute-done.1), channel_id=1, source_target_pairs={{0,2},{4,0},{8,4},{12,8},{14,12},{10,14},{6,10},{2,6},{1,3},{5,1},... | collective-permute-start | bytes 1622024 | tf_op jit(solution)/shard_map/ppermute | solution.py:963
  44.4 35.0 %collective-permute-start.18 = (bf16[64,8192]{1,0:T(8,128)(2,1)}, bf16[64,8192]{1,0:T(8,128)(2,1)S(1)}, u32[]{:S(2)}, u32[]{:S(2)}) collective-permute-start(bf16[64,8192]{1,0:T(8,128)(2,1)} %collective-permute-done.6), channel_id=1, source_target_pairs={{0,1},{1,0},{2,3},{3,2},{4,5},{5,4},{6,7},{7,6},{8,9},{9,8},{10,11... | collective-permute-start | bytes 3145736 | tf_op jit(solution)/shard_map/ppermute | solution.py:947
  44.4 35.1 %collective-permute-start.19 = (bf16[64,8192]{1,0:T(8,128)(2,1)}, bf16[64,8192]{1,0:T(8,128)(2,1)S(1)}, u32[]{:S(2)}, u32[]{:S(2)}) collective-permute-start(bf16[64,8192]{1,0:T(8,128)(2,1)} %collective-permute-done.7), channel_id=1, source_target_pairs={{0,1},{1,0},{2,3},{3,2},{4,5},{5,4},{6,7},{7,6},{8,9},{9,8},{10,11... | collective-permute-start | bytes 3145736 | tf_op jit(solution)/shard_map/ppermute | solution.py:947
  70.7 26.2 %collective-permute-start.8 = (bf16[64,8192]{1,0:T(8,128)(2,1)}, bf16[64,8192]{1,0:T(8,128)(2,1)S(1)}, u32[]{:S(2)}, u32[]{:S(2)}) collective-permute-start(bf16[64,8192]{1,0:T(8,128)(2,1)} %collective-permute-done.6), channel_id=1, source_target_pairs={{0,4},{4,8},{8,12},{12,14},{14,10},{10,6},{6,2},{2,0},{1,5},{5,9},... | collective-permute-start | bytes 3145736 | tf_op jit(solution)/shard_map/ppermute | solution.py:963
  78.0 21.1 %collective-permute-start.9 = (bf16[64,8192]{1,0:T(8,128)(2,1)}, bf16[64,8192]{1,0:T(8,128)(2,1)S(1)}, u32[]{:S(2)}, u32[]{:S(2)}) collective-permute-start(bf16[64,8192]{1,0:T(8,128)(2,1)} %collective-permute-done.7), channel_id=1, source_target_pairs={{0,2},{4,0},{8,4},{12,8},{14,12},{10,14},{6,10},{2,6},{1,3},{5,1},... | collective-permute-start | bytes 3145736 | tf_op jit(solution)/shard_map/ppermute | solution.py:963
  79.3 22.6 %collective-permute-start.12 = (bf16[512,4224]{1,0:T(8,128)(2,1)S(1)}, bf16[512,4224]{1,0:T(8,128)(2,1)S(1)}, u32[]{:S(2)}, u32[]{:S(2)}) collective-permute-start(bf16[512,4224]{1,0:T(8,128)(2,1)S(1)} %constant_dynamic-update-slice_fusion.own_ref), channel_id=1, source_target_pairs={{0,1},{1,0},{2,3},{3,2},{4,5},{5,4},{6,7},{7,6},{8,9},{9,8},{10,11... | collective-permute-start | bytes 12976136 | tf_op jit(solution)/shard_map/ppermute | solution.py:947
  101.9 25.3 %collective-permute-start.13 = (bf16[64,8192]{1,0:T(8,128)(2,1)S(1)}, bf16[64,8192]{1,0:T(8,128)(2,1)S(1)}, u32[]{:S(2)}, u32[]{:S(2)}) collective-permute-start(bf16[64,8192]{1,0:T(8,128)(2,1)S(1)} %collective-permute-done.8), channel_id=1, source_target_pairs={{0,4},{4,8},{8,12},{12,14},{14,10},{10,6},{6,2},{2,0},{1,5},{5,9},... | collective-permute-start | bytes 3145736 | tf_op jit(solution)/shard_map/ppermute | solution.py:963
  103.4 25.2 %collective-permute-start.14 = (bf16[64,8192]{1,0:T(8,128)(2,1)S(1)}, bf16[64,8192]{1,0:T(8,128)(2,1)S(1)}, u32[]{:S(2)}, u32[]{:S(2)}) collective-permute-start(bf16[64,8192]{1,0:T(8,128)(2,1)S(1)} %collective-permute-done.9), channel_id=1, source_target_pairs={{0,2},{4,0},{8,4},{12,8},{14,12},{10,14},{6,10},{2,6},{1,3},{5,1},... | collective-permute-start | bytes 3145736 | tf_op jit(solution)/shard_map/ppermute | solution.py:963
  169.4 60.0 %collective-permute-start.28 = (bf16[256,1024]{1,0:T(8,128)(2,1)S(1)}, bf16[256,1024]{1,0:T(8,128)(2,1)S(1)}, u32[]{:S(2)}, u32[]{:S(2)}) collective-permute-start(bf16[256,1024]{1,0:T(8,128)(2,1)S(1)} %feed_forward.6), channel_id=1, source_target_pairs={{0,16},{1,17},{2,18},{3,19},{4,20},{5,21},{6,22},{7,23},{8,24},{9,... | collective-permute-start | bytes 1572872 | tf_op jit(solution)/shard_map/ppermute | solution.py:524
  228.1 28.8 %collective-permute-start.27 = (bf16[256,1024]{1,0:T(8,128)(2,1)S(1)}, bf16[256,1024]{1,0:T(8,128)(2,1)S(1)}, u32[]{:S(2)}, u32[]{:S(2)}) collective-permute-start(bf16[256,1024]{1,0:T(8,128)(2,1)S(1)} %get-tuple-element.323), channel_id=1, source_target_pairs={{16,0},{17,1},{18,2},{19,3},{20,4},{21,5},{22,6},{23,7},{24,8},{25... | collective-permute-start | bytes 1572872 | tf_op jit(solution)/shard_map/ppermute | solution.py:524
  259.7 23.5 %collective-permute-start.33 = (bf16[512,2048]{1,0:T(8,128)(2,1)S(1)}, bf16[512,2048]{1,0:T(8,128)(2,1)}, u32[]{:S(2)}, u32[]{:S(2)}) collective-permute-start(bf16[512,2048]{1,0:T(8,128)(2,1)S(1)} %bitcast.98), channel_id=1, source_target_pairs={{0,1},{1,0},{2,3},{3,2},{4,5},{5,4},{6,7},{7,6},{8,9},{9,8},{10,11... | collective-permute-start | bytes 6291464 | tf_op jit(solution)/shard_map/ppermute | solution.py:947
  259.7 23.5 %collective-permute-start.34 = (bf16[512,2048]{1,0:T(8,128)(2,1)}, bf16[512,2048]{1,0:T(8,128)(2,1)}, u32[]{:S(2)}, u32[]{:S(2)}) collective-permute-start(bf16[512,2048]{1,0:T(8,128)(2,1)} %get-tuple-element.364.refs_12_.refs_13_), channel_id=1, source_target_pairs={{0,1},{1,0},{2,3},{3,2},{4,5},{5,4},{6,7},{7,6},{8,9},{9,8},{10,11... | collective-permute-start | bytes 6291464 | tf_op jit(solution)/shard_map/ppermute | solution.py:947
  260.2 23.0 %collective-permute-start.35 = (bf16[512,512]{1,0:T(8,128)(2,1)}, bf16[512,512]{1,0:T(8,128)(2,1)}, u32[]{:S(2)}, u32[]{:S(2)}) collective-permute-start(bf16[512,512]{1,0:T(8,128)(2,1)} %slice.262), channel_id=1, source_target_pairs={{0,1},{1,0},{2,3},{3,2},{4,5},{5,4},{6,7},{7,6},{8,9},{9,8},{10,11... | collective-permute-start | bytes 1572872 | tf_op jit(solution)/shard_map/ppermute | solution.py:947
  260.2 23.0 %collective-permute-start.36 = (bf16[512,512]{1,0:T(8,128)(2,1)}, bf16[512,512]{1,0:T(8,128)(2,1)}, u32[]{:S(2)}, u32[]{:S(2)}) collective-permute-start(bf16[512,512]{1,0:T(8,128)(2,1)} %slice.263), channel_id=1, source_target_pairs={{0,1},{1,0},{2,3},{3,2},{4,5},{5,4},{6,7},{7,6},{8,9},{9,8},{10,11... | collective-permute-start | bytes 1572872 | tf_op jit(solution)/shard_map/ppermute | solution.py:947
  296.2 26.5 %collective-permute-start.37 = (bf16[256,4224]{1,0:T(8,128)(2,1)}, bf16[256,4224]{1,0:T(8,128)(2,1)}, u32[]{:S(2)}, u32[]{:S(2)}) collective-permute-start(bf16[256,4224]{1,0:T(8,128)(2,1)} %get-tuple-element.446.grad_ref.refs_4_), channel_id=1, source_target_pairs={{0,1},{1,0},{2,3},{3,2},{4,5},{5,4},{6,7},{7,6},{8,9},{9,8},{10,11... | collective-permute-start | bytes 6488072 | tf_op jit(solution)/shard_map/ppermute | solution.py:947
  296.2 26.5 %collective-permute-start.31 = (bf16[256,2048]{1,0:T(8,128)(2,1)}, bf16[256,2048]{1,0:T(8,128)(2,1)}, u32[]{:S(2)}, u32[]{:S(2)}) collective-permute-start(bf16[256,2048]{1,0:T(8,128)(2,1)} %get-tuple-element.401.refs_8_), channel_id=1, source_target_pairs={{0,1},{1,0},{2,3},{3,2},{4,5},{5,4},{6,7},{7,6},{8,9},{9,8},{10,11... | collective-permute-start | bytes 3145736 | tf_op jit(solution)/shard_map/ppermute | solution.py:947
  296.7 26.0 %collective-permute-start.32 = (bf16[256,2048]{1,0:T(8,128)(2,1)}, bf16[256,2048]{1,0:T(8,128)(2,1)}, u32[]{:S(2)}, u32[]{:S(2)}) collective-permute-start(bf16[256,2048]{1,0:T(8,128)(2,1)} %get-tuple-element.405.refs_12_), channel_id=1, source_target_pairs={{0,1},{1,0},{2,3},{3,2},{4,5},{5,4},{6,7},{7,6},{8,9},{9,8},{10,11... | collective-permute-start | bytes 3145736 | tf_op jit(solution)/shard_map/ppermute | solution.py:947
  434.3 29.6 %collective-permute-start.61 = (f32[16,1792]{1,0:T(8,128)S(1)}, f32[16,1792]{1,0:T(8,128)S(1)}, u32[]{:S(2)}, u32[]{:S(2)}) collective-permute-start(f32[16,1792]{1,0:T(8,128)S(1)} %add.284), channel_id=1, source_target_pairs={{0,2},{2,0},{4,6},{6,4},{8,10},{10,8},{12,14},{14,12},{1,3},{3,1},... | collective-permute-start | bytes 344072 | tf_op jit(solution)/shard_map/ppermute | solution.py:1064
  443.3 23.4 %collective-permute-start.74 = (bf16[64,4096]{1,0:T(8,128)(2,1)S(1)}, bf16[64,4096]{1,0:T(8,128)(2,1)S(1)}, u32[]{:S(2)}, u32[]{:S(2)}) collective-permute-start(bf16[64,4096]{1,0:T(8,128)(2,1)S(1)} %get-tuple-element.507), channel_id=1, source_target_pairs={{0,4},{4,8},{8,12},{12,14},{14,10},{10,6},{6,2},{2,0},{1,5},{5,9},... | collective-permute-start | bytes 1572872 | tf_op jit(solution)/shard_map/ppermute | solution.py:963
  444.9 21.8 %collective-permute-start.75 = (bf16[64,4096]{1,0:T(8,128)(2,1)S(1)}, bf16[64,4096]{1,0:T(8,128)(2,1)S(1)}, u32[]{:S(2)}, u32[]{:S(2)}) collective-permute-start(bf16[64,4096]{1,0:T(8,128)(2,1)S(1)} %get-tuple-element.506), channel_id=1, source_target_pairs={{0,2},{4,0},{8,4},{12,8},{14,12},{10,14},{6,10},{2,6},{1,3},{5,1},... | collective-permute-start | bytes 1572872 | tf_op jit(solution)/shard_map/ppermute | solution.py:963
  (129 other events, 2444.4 us)

commit v3 on v1

--- a/solution.py
+++ b/solution.py
@@ -631,9 +631,9 @@
         low_ref[...] = total_s[...].astype(bf16)
 
 
-def pinned(own, other):
+def pinned(own, other, kept=True):
     return [
-        pltpu.with_memory_space_constraint(own, pltpu.VMEM),
+        pltpu.with_memory_space_constraint(own, pltpu.VMEM if kept else pltpu.HBM),
         pltpu.with_memory_space_constraint(other, pltpu.HBM),
     ]
 
@@ -732,7 +732,7 @@
         )
 
 
-def feed_back(row, cotangent, gate, up, middle, gain, own, other):
+def feed_back(row, cotangent, gate, up, middle, gain, own, other, kept):
     saved = pl.BlockSpec((TOK, 512), lambda step, pick: (pick[0], jnp.clip(step, 0, 3)))
     early = pl.BlockSpec((TOK, 512), lambda step, pick: (0, jnp.clip(step, 0, 3)))
     late = pl.BlockSpec((TOK, 512), lambda step, pick: (0, jnp.clip(step - 4, 0, 3)))
@@ -769,7 +769,8 @@
         name="feed_back",
     )(
         row, cotangent, *(pltpu.with_memory_space_constraint(one, pltpu.HBM) for one in (gate, up)),
-        pltpu.with_memory_space_constraint(middle, pltpu.HBM), gain, *(pinned(own, other) * 4),
+        pltpu.with_memory_space_constraint(middle, pltpu.HBM), gain,
+        *(pinned(own, other, kept) * 4),
     )
 
 
@@ -1107,7 +1108,8 @@
     def whole_order(values):
         if values.dtype == bf16:
             return dot_nt(values, turn).astype(bf16)
-        return dot_exact(values, turn.astype(f32).T)
+        high = values.astype(bf16)
+        return dot_nt(high, turn) + dot_nt((values - high.astype(f32)).astype(bf16), turn)
 
     pre_row = own_order(pre_gain)
     mlp_row = own_order(mlp_gain)
@@ -1195,6 +1197,7 @@
         if tick == 2:
             row, lefts[1], rights[1], rows[1] = tied(row, lefts[1], rights[1], rows[1])
             section_out = whole_order(result)
+            d_early = whole_order(rows[1][0])
             row, section_out = tied(row, section_out)
         loss_row = (1, 0, 1)[tick]
         cotangent = jnp.where(
@@ -1206,7 +1209,7 @@
             )
             their_mixed, their_act, their_normed, their_normed_two = map(swapped, swaps)
         d_gate, d_up, d_middle, middle_low, d_mixed, mlp_grad = feed_back(
-            row, cotangent, gate, up, middle, mlp_row, *pair_b
+            row, cotangent, gate, up, middle, mlp_row, *pair_b, kept=tick == 0
         )
         lefts.append(
             (cotangent, middle_low, swapped(cotangent[:, SIDE:]), swapped(middle_low[:, SIDE:]))
@@ -1265,17 +1268,17 @@
             d_rows, d_low, pre_grad = project_back(
                 row, proj_low, start_rows, d_middle, pre_row, *pair_a
             )
-            now_c, their_low, d_rows, pre_grad = tied(
-                ring_c.operands(), their_low, d_rows, pre_grad
-            )
-            ring_c.send(*now_c)
             small_two = (pre_grad, mlp_grad, small)
             pre_sum, mlp_sum, small_sum = (one + two for one, two in zip(rows[1][2:], small_two))
             gain_sums = whole_order(jnp.concatenate([pre_sum, mlp_sum], axis=0))
             small_sum = jnp.concatenate(
                 [small_sum, jnp.pad(gain_sums, ((0, 6), (0, CH - D)))], axis=0
             )
-            picks_now, now_c, small_sum = tied(picks, now_c, small_sum)
+            now_c, their_low, d_rows, small_sum = tied(
+                ring_c.operands(), their_low, d_rows, small_sum
+            )
+            ring_c.send(*now_c)
+            picks_now, now_c = tied(picks, now_c)
             (p_one, their_one), (p_two, their_two) = rows[1][1], (proj_low, their_low)
             sum_a = weight_grad(
                 picks_now,
@@ -1318,7 +1321,7 @@
     small = hop_beside(small, ring_a)
     while ring_a.left > 2:
         ring_a.step()
-    d_last = tied(rows[2][0], ring_a.ahead)[0]
+    d_last = whole_order(tied(rows[2][0], ring_a.ahead)[0])
     rings_a = [ring_a.columns(0, CUT_A), ring_a.columns(CUT_A, WIDE_A)]
     while rings_a[0].left:
         for ring in rings_a:
@@ -1332,8 +1335,8 @@
 
     start_grad = jnp.concatenate(
         [
-            jnp.where(is_first, d_last, rows[1][0]),
-            jnp.where(is_first, rows[1][0], d_last),
+            jnp.where(is_first, d_last, d_early),
+            jnp.where(is_first, d_early, d_last),
         ],
         axis=0,
     )
@@ -1341,7 +1344,7 @@
     mixer_in_grad = jnp.concatenate([share_a[:, :AT_Q], share_a[:, AT_DT : AT_DT + MH]], axis=1)
     return (
         section_out[None],
-        whole_order(start_grad)[None],
+        start_grad[None],
         small[8:9, :D],
         small[9:10, :D],
         small[5:6, :E],

time: 499 us -> 497 us (level)
  local copies, waits for them, and re-layouts: 36.7 us -> 30.7 us
    dot_general x4 -> x2, matrix products: 9.66 us -> 2.74 us  [dot_exact(): lax.dot_general(left, right, (((1,), (0,)), ((), ())), precision=highest,...]
    unnamed x185 -> x181, local copies, waits for them, and re-layouts: 20.4 us -> 14.4 us
    dot_general x1 -> x7, matrix products: 3.54 us -> 9.26 us  [dot_nt(): lax.dot_general(left, right, (((1,), (1,)), ((), ())), preferred_element_...]
  transfers between devices with their start and end apart: 76 -> 76, of which waited for: 42 -> 42; matrix products, arithmetic and copies ran while one was open for 10% -> 10% of each run, Pallas kernels for 37% -> 38%
where the time goes in v3:
time: 497 us; the launch traced here: 488 us
  Pallas kernels  217 us (44%)
  waiting for transfers between devices  143 us (29%)
  starting transfers between devices  64.1 us (13%)
  local copies, waits for them, and re-layouts  30.7 us (6%)
  matrix products  15.7 us (3%)
  other arithmetic  14.5 us (3%)
    ppermute x44, waiting for transfers between devices, onward(): lax.ppermute(value, 'chip', [(order[at], order[(at + steps) % chips]) for...  118 us
    ppermute x44, starting transfers between devices, onward(): lax.ppermute(value, 'chip', [(order[at], order[(at + steps) % chips]) for...  46.9 us
    pallas_call x4, Pallas kernels, feed_forward(): pl.pallas_call(functools.partial(feed_forward_kernel, keep), grid=(8,), i...  42.3 us
    pallas_call x3, Pallas kernels, feed_back(): pl.pallas_call(feed_back_kernel, grid_spec=pltpu.PrefetchScalarGridSpec(n...  41.8 us
    pallas_call x3, Pallas kernels, mixer_back(): pl.pallas_call(mixer_back_kernel, grid_spec=pltpu.PrefetchScalarGridSpec(...  36.9 us
    pallas_call x4, Pallas kernels, core_forward(): pl.pallas_call(functools.partial(core_forward_kernel, bool(held)), grid=(...  27.6 us
    pallas_call x3, Pallas kernels, weight_grad(): pl.pallas_call(functools.partial(weight_grad_kernel, tuple(steps)), grid_...  26.5 us
    pallas_call x3, Pallas kernels, project_back(): pl.pallas_call(project_back_kernel, grid_spec=pltpu.PrefetchScalarGridSpe...  17.1 us
  transfers between devices with their start and end apart: 76, of which 42 were waited for; matrix products, arithmetic and copies ran while one was open for 10% of the time, Pallas kernels for 38%

profile of v3, /device:TPU:0, one launch (start us, length us, event | category | flops | bytes accessed | tf_op | source)
XLA Modules:
  0.0 487.8 jit_solution(16430011183506852964)
XLA Ops:
  27.9 15.1 %collective-permute-done.6 = bf16[64,8192]{1,0:T(8,128)(2,1)} collective-permute-done((bf16[64,8192]{1,0:T(8,128)(2,1)}, bf16[64,8192]{1,0:T(8,128)(2,1)}, u32[]{:S(2)}, u32[]{:S(2)}) %collective-permute-start.6) | collective-permute-done | bytes 1048608 | tf_op jit(solution)/shard_map/ppermute | solution.py:955
  57.4 10.7 %collective-permute-done.4 = bf16[64,4224]{1,0:T(8,128)(2,1)S(1)} collective-permute-done((bf16[64,4224]{1,0:T(8,128)(2,1)S(1)}, bf16[64,4224]{1,0:T(8,128)(2,1)S(1)}, u32[]{:S(2)}, u32[]{:S(2)}) %collective-permute-start.4) | collective-permute-done | bytes 540704 | tf_op jit(solution)/shard_map/ppermute | solution.py:955
  80.4 17.4 %collective-permute-done.8 = bf16[64,8192]{1,0:T(8,128)(2,1)S(1)} collective-permute-done((bf16[64,8192]{1,0:T(8,128)(2,1)}, bf16[64,8192]{1,0:T(8,128)(2,1)S(1)}, u32[]{:S(2)}, u32[]{:S(2)}) %collective-permute-start.8) | collective-permute-done | bytes 1048608 | tf_op jit(solution)/shard_map/ppermute | solution.py:955
  105.1 7.9 %project.3 = (bf16[512,1024]{1,0:T(8,128)(2,1)}, bf16[512,3328]{1,0:T(8,128)(2,1)S(1)}, bf16[512,768]{1,0:T(8,128)(2,1)S(1)}, f32[512,128]{1,0:T(8,128)S(1)}) custom-call(bf16[512,1024]{1,0:T(8,128)(2,1)S(1)} %fusion.25.rows_ref, f32[1,1024]{1,0:T(1,128)S(1)} %fusion.8.gain_ref, bf16[512,4224]{1,0:T(8,128)(2,1)S(1)} %constant_dynamic-update-slice_fusion.own_ref, ...), custom_call_target="tpu_custom_call" | custom-call | flops 4429185024 | bytes 12976128 | tf_op jit(solution)/shard_map/project/pallas_call | solution.py:566
  113.2 6.9 %core_forward.4 = (bf16[2,256,2048]{2,1,0:T(8,128)(2,1)S(1)}, bf16[2,256,1792]{2,1,0:T(8,128)(2,1)S(1)}, f32[2,256,1536]{2,1,0:T(8,128)S(1)}) custom-call(bf16[2,256,3328]{2,1,0:T(8,128)(2,1)S(1)} %bitcast.108, bf16[2,256,768]{2,1,0:T(8,128)(2,1)S(1)} %bitcast.115, f32[2,256,128]{2,1,0:T(8,128)S(1)} %bitcast.117, f32[2,256,256]{2,1,0:T(8,128)S(1)} %concatenate.67.rope_ref, ...), custom_call_target="tpu_custom_call" | custom-call | flops 400000000 | bytes 12582912 | tf_op jit(solution)/shard_map/core_forward/pallas_call | solution.py:425
  120.1 7.9 %collective-permute-done.13 = bf16[64,8192]{1,0:T(8,128)(2,1)S(1)} collective-permute-done((bf16[64,8192]{1,0:T(8,128)(2,1)S(1)}, bf16[64,8192]{1,0:T(8,128)(2,1)S(1)}, u32[]{:S(2)}, u32[]{:S(2)}) %collective-permute-start.13) | collective-permute-done | bytes 1048608 | tf_op jit(solution)/shard_map/ppermute | solution.py:955
  132.8 6.9 %core_forward.5 = (bf16[2,256,2048]{2,1,0:T(8,128)(2,1)S(1)}, bf16[2,256,1792]{2,1,0:T(8,128)(2,1)S(1)}, f32[2,256,1536]{2,1,0:T(8,128)S(1)}) custom-call(bf16[2,256,3328]{2,1,0:T(8,128)(2,1)S(1)} %bitcast.109, bf16[2,256,768]{2,1,0:T(8,128)(2,1)S(1)} %bitcast.116, ...), custom_call_target="tpu_custom_call", output_to_operand_aliasing={{0}: (10, {}), {1}: (11, {}), {2}: (12, {})} | custom-call | flops 400000000 | bytes 12582912 | tf_op jit(solution)/shard_map/core_forward/pallas_call | solution.py:425
  147.6 8.6 %feed_forward.4 = bf16[256,1024]{1,0:T(8,128)(2,1)S(1)} custom-call(bf16[512,1024]{1,0:T(8,128)(2,1)S(1)} %fusion.25.rows_ref, bf16[512,2048]{1,0:T(8,128)(2,1)S(1)} %bitcast.106, f32[1,1024]{1,0:T(1,128)S(1)} %fusion.7.gain_ref, bf16[512,8192]{1,0:T(8,128)(2,1)S(1)} %constant_dynamic-update-slice_fusion.9.out_own.gate_own.up_own.down_own, ...), custom_call_target="tpu_custom_call" | custom-call | flops 4294967296 | bytes 16777216 | tf_op jit(solution)/shard_map/feed_forward/pallas_call | solution.py:672
  159.7 8.6 %feed_forward.6 = bf16[256,1024]{1,0:T(8,128)(2,1)S(1)} custom-call(bf16[512,1024]{1,0:T(8,128)(2,1)S(1)} %fusion.25.rows_ref, bf16[512,2048]{1,0:T(8,128)(2,1)S(1)} %bitcast.107, f32[1,1024]{1,0:T(1,128)S(1)} %fusion.7.gain_ref, bf16[512,8192]{1,0:T(8,128)(2,1)S(1)} %constant_dynamic-update-slice_fusion.9.out_own.gate_own.up_own.down_own, ...), custom_call_target="tpu_custom_call" | custom-call | flops 4294967296 | bytes 16777216 | tf_op jit(solution)/shard_map/feed_forward/pallas_call | solution.py:672
  176.0 6.9 %core_forward.6 = (bf16[2,256,2048]{2,1,0:T(8,128)(2,1)S(1)}, bf16[2,256,1792]{2,1,0:T(8,128)(2,1)S(1)}, f32[2,256,1536]{2,1,0:T(8,128)S(1)}) custom-call(bf16[2,256,3328]{2,1,0:T(8,128)(2,1)S(1)} %bitcast.83, bf16[2,256,768]{2,1,0:T(8,128)(2,1)S(1)} %bitcast.101, f32[2,256,128]{2,1,0:T(8,128)S(1)} %bitcast.110, f32[2,256,256]{2,1,0:T(8,128)S(1)} %copy-done.18, ...), custom_call_target="tpu_custom_call" | custom-call | flops 400000000 | bytes 12582912 | tf_op jit(solution)/shard_map/core_forward/pallas_call | solution.py:425
  183.0 11.8 %feed_forward.5 = (bf16[512,1024]{1,0:T(8,128)(2,1)}, f32[512,1024]{1,0:T(8,128)}, bf16[512,1024]{1,0:T(8,128)(2,1)}, bf16[512,2048]{1,0:T(8,128)(2,1)}, bf16[51...) custom-call(bf16[256,1024]{1,0:T(8,128)(2,1)S(1)} %slice_select_fusion.2.rows_ref, bf16[512,2048]{1,0:T(8,128)(2,1)S(1)} %bitcast.96, ...), custom_call_target="tpu_custom_call" | custom-call | flops 4294967296 | bytes 16777216 | tf_op jit(solution)/shard_map/feed_forward/pallas_call | solution.py:672
  194.8 12.9 %feed_back.3 = (bf16[256,2048]{1,0:T(8,128)(2,1)}, bf16[256,2048]{1,0:T(8,128)(2,1)}, f32[256,1024]{1,0:T(8,128)S(1)}, bf16[256,1024]{1,0:T(8,128)(2,1)}, f32[256,2048]{1,0:T(8,128)S(1)}, /*index=5*/f32[1,1024]{1,0:T(1,128)}) custom-call(s32[1]{0:T(128)} %constant.154.clone.1.pick_ref, bf16[256,1024]{1,0:T(8,128)(2,1)S(1)} %broadcast_select_fusion.3.cot_ref, ...), custom_call_target="tpu_custom_call" | custom-call | flops 4294967296 | bytes 16777216 | tf_op jit(solution)/shard_map/feed_back/pallas_call | solution.py:741
  211.3 12.1 %mixer_back.3 = (bf16[256,4224]{1,0:T(8,128)(2,1)S(1)}, f32[8,1792]{1,0:T(8,128)}) custom-call(s32[1]{0:T(128)} %constant.154.clone.1.pick_ref, bf16[2,256,3328]{2,1,0:T(8,128)(2,1)S(1)} %bitcast.84, f32[2,256,128]{2,1,0:T(8,128)S(1)} %bitcast.111, bf16[2,256,1792]{2,1,0:T(8,128)(2,1)S(1)} %get-tuple-element.336.pre_ref.refs_1_, ...), custom_call_target="tpu_custom_call" | custom-call | flops 700000000 | bytes 10485760 | tf_op jit(solution)/shard_map/mixer_back/pallas_call | solution.py:480
  235.9 6.9 %core_forward.7 = (bf16[2,256,2048]{2,1,0:T(8,128)(2,1)S(1)}, bf16[2,256,1792]{2,1,0:T(8,128)(2,1)S(1)}, f32[2,256,1536]{2,1,0:T(8,128)S(1)}) custom-call(bf16[2,256,3328]{2,1,0:T(8,128)(2,1)S(1)} %bitcast.85, bf16[2,256,768]{2,1,0:T(8,128)(2,1)S(1)} %bitcast.103, ...), custom_call_target="tpu_custom_call", output_to_operand_aliasing={{0}: (10, {}), {1}: (11, {}), {2}: (12, {})} | custom-call | flops 400000000 | bytes 12582912 | tf_op jit(solution)/shard_map/core_forward/pallas_call | solution.py:425
  242.9 13.4 %feed_forward.7 = (bf16[512,1024]{1,0:T(8,128)(2,1)}, f32[512,1024]{1,0:T(8,128)}, bf16[512,1024]{1,0:T(8,128)(2,1)}, bf16[512,2048]{1,0:T(8,128)(2,1)}, bf16[51...) custom-call(bf16[256,1024]{1,0:T(8,128)(2,1)S(1)} %slice_select_fusi, ...), custom_call_target="tpu_custom_call", output_to_operand_aliasing={{0}: (11, {}), {1}: (12, {}), {2}: (13, {}), {3}: (14, {}),... | custom-call | flops 4294967296 | bytes 16777216 | tf_op jit(solution)/shard_map/feed_forward/pallas_call | solution.py:672
  261.2 15.0 %feed_back.4 = (bf16[256,2048]{1,0:T(8,128)(2,1)}, bf16[256,2048]{1,0:T(8,128)(2,1)}, f32[256,1024]{1,0:T(8,128)S(1)}, bf16[256,1024]{1,0:T(8,128)(2,1)S(1)}, f3...) custom-call(s32[1]{0:T(128)} %bitcast.42.pick_ref, bf16[256,1024]{1,0:T(8,128)(2,1)S(1)} %copy-done.45, ...), custom_call_target="tpu_custom_call" | custom-call | flops 4294967296 | bytes 16777216 | tf_op jit(solution)/shard_map/feed_back/pallas_call | solution.py:741
  279.8 12.9 %mixer_back.4 = (bf16[256,4224]{1,0:T(8,128)(2,1)}, f32[8,1792]{1,0:T(8,128)S(1)}) custom-call(s32[1]{0:T(128)} %bitcast.42.pick_ref, bf16[2,256,3328]{2,1,0:T(8,128)(2,1)S(1)} %bitcast.86, f32[2,256,128]{2,1,0:T(8,128)S(1)} %bitcast.113, bf16[2,256,1792]{2,1,0:T(8,128)(2,1)S(1)} %copy-done.28, f32[2,256,1536]{2,1,0:T(8,128)S(1)} %copy-done.11, ...), custom_call_target="tpu_custom_call" | custom-call | flops 700000000 | bytes 10485760 | tf_op jit(solution)/shard_map/mixer_back/pallas_call | solution.py:480
  307.1 10.3 %collective-permute-done.38 = bf16[256,1024]{1,0:T(8,128)(2,1)} collective-permute-done((bf16[256,1024]{1,0:T(8,128)(2,1)}, bf16[256,1024]{1,0:T(8,128)(2,1)}, u32[]{:S(2)}, u32[]{:S(2)}) %collective-permute-start.38) | collective-permute-done | bytes 524320 | tf_op jit(solution)/shard_map/ppermute | solution.py:521
  319.2 14.0 %feed_back.5 = (bf16[256,2048]{1,0:T(8,128)(2,1)S(1)}, bf16[256,2048]{1,0:T(8,128)(2,1)S(1)}, f32[256,1024]{1,0:T(8,128)S(1)}, bf16[256,1024]{1,0:T(8,128)(2,1)S...) custom-call(s32[1]{0:T(128)} %bitcast.pick_ref, bf16[256,1024]{1,0:T(8,128)(2,1)S(1)} %broadcast_select_fusion.2.cot_ref.refs_5_, ...), custom_call_target="tpu_custom_call" | custom-call | flops 4294967296 | bytes 16777216 | tf_op jit(solution)/shard_map/feed_back/pallas_call | solution.py:741
  334.8 8.8 %weight_grad.3 = bf16[512,4096]{1,0:T(8,128)(2,1)S(1)} custom-call(s32[2]{0:T(128)S(1)} %broadcast_select_fusion.4.pick_ref, bf16[256,1024]{1,0:T(8,128)(2,1)S(1)} %copy-done.52, bf16[256,1024]{1,0:T(8,128)(2,1)S(1)} %get-tuple-element.382.refs_1_, bf16[256,512]{1,0:T(8,128)(2,1)S(1)} %collective-permute-done.30.refs_2_, ...), custom_call_target="tpu_custom_call" | custom-call | flops 4294967296 | bytes 8388608 | tf_op jit(solution)/shard_map/weight_grad/pallas_call | solution.py:886
  354.5 9.3 %weight_grad.4 = bf16[512,4096]{1,0:T(8,128)(2,1)S(1)} custom-call(s32[2]{0:T(128)S(1)} %broadcast_select_fusion.4.pick_ref, bf16[512,1024]{1,0:T(8,128)(2,1)S(1)} %copy-done.26, bf16[512,1024]{1,0:T(8,128)(2,1)S(1)} %copy-done.26, bf16[512,512]{1,0:T(8,128)(2,1)} %collective-permute-done.36.refs_2_.refs_3_.refs_6_.refs_7_, ...), custom_call_target="tpu_custom_call" | custom-call | flops 4294967296 | bytes 8388608 | tf_op jit(solution)/shard_map/weight_grad/pallas_call | solution.py:886
  370.0 11.9 %mixer_back.5 = (bf16[256,4224]{1,0:T(8,128)(2,1)S(1)}, f32[8,1792]{1,0:T(8,128)S(1)}) custom-call(s32[1]{0:T(128)} %bitcast.pick_ref, bf16[2,256,3328]{2,1,0:T(8,128)(2,1)S(1)} %bitcast.87, f32[2,256,128]{2,1,0:T(8,128)S(1)} %bitcast.114, bf16[2,256,1792]{2,1,0:T(8,128)(2,1)S(1)} %copy-done.29, f32[2,256,1536]{2,1,0:T(8,128)S(1)} %copy-done.12, ...), custom_call_target="tpu_custom_call" | custom-call | flops 700000000 | bytes 10485760 | tf_op jit(solution)/shard_map/mixer_back/pallas_call | solution.py:480
  401.4 8.4 %weight_grad.5 = bf16[512,4224]{1,0:T(8,128)(2,1)S(1)} custom-call(s32[2]{0:T(128)S(1)} %broadcast_select_fusion.4.pick_ref, bf16[512,1024]{1,0:T(8,128)(2,1)S(1)} %copy-done.49, bf16[512,1024]{1,0:T(8,128)(2,1)S(1)} %copy-done.49, bf16[512,512]{1,0:T(8,128)(2,1)} %collective-permute-done.35.refs_2_.refs_3_, ...), custom_call_target="tpu_custom_call" | custom-call | flops 4429185024 | bytes 8650752 | tf_op jit(solution)/shard_map/weight_grad/pallas_call | solution.py:886
  436.1 7.5 %collective-permute-done.58 = bf16[64,4224]{1,0:T(8,128)(2,1)S(1)} collective-permute-done((bf16[64,4224]{1,0:T(8,128)(2,1)S(1)}, bf16[64,4224]{1,0:T(8,128)(2,1)S(1)}, u32[]{:S(2)}, u32[]{:S(2)}) %collective-permute-start.58) | collective-permute-done | bytes 540704 | tf_op jit(solution)/shard_map/ppermute | solution.py:955
  (446 shorter events, 233.2 us)
Async XLA Ops:
  10.0 33.1 %collective-permute-start.6 = (bf16[64,8192]{1,0:T(8,128)(2,1)}, bf16[64,8192]{1,0:T(8,128)(2,1)}, u32[]{:S(2)}, u32[]{:S(2)}) collective-permute-start(bf16[64,8192]{1,0:T(8,128)(2,1)} %get-tuple-element.523), channel_id=1, source_target_pairs={{0,4},{4,8},{8,12},{12,14},{14,10},{10,6},{6,2},{2,0},{1,5},{5,9},... | collective-permute-start | bytes 3145736 | tf_op jit(solution)/shard_map/ppermute | solution.py:955
  12.0 33.2 %collective-permute-start.7 = (bf16[64,8192]{1,0:T(8,128)(2,1)}, bf16[64,8192]{1,0:T(8,128)(2,1)}, u32[]{:S(2)}, u32[]{:S(2)}) collective-permute-start(bf16[64,8192]{1,0:T(8,128)(2,1)} %get-tuple-element.523), channel_id=1, source_target_pairs={{0,2},{4,0},{8,4},{12,8},{14,12},{10,14},{6,10},{2,6},{1,3},{5,1},... | collective-permute-start | bytes 3145736 | tf_op jit(solution)/shard_map/ppermute | solution.py:955
  12.0 38.3 %collective-permute-start.17 = (bf16[64,8192]{1,0:T(8,128)(2,1)}, bf16[64,8192]{1,0:T(8,128)(2,1)}, u32[]{:S(2)}, u32[]{:S(2)}) collective-permute-start(bf16[64,8192]{1,0:T(8,128)(2,1)} %get-tuple-element.523), channel_id=1, source_target_pairs={{0,1},{1,0},{2,3},{3,2},{4,5},{5,4},{6,7},{7,6},{8,9},{9,8},{10,11... | collective-permute-start | bytes 3145736 | tf_op jit(solution)/shard_map/ppermute | solution.py:939
  23.6 30.1 %collective-permute-start.2 = (bf16[64,4224]{1,0:T(8,128)(2,1)}, bf16[64,4224]{1,0:T(8,128)(2,1)S(1)}, u32[]{:S(2)}, u32[]{:S(2)}) collective-permute-start(bf16[64,4224]{1,0:T(8,128)(2,1)} %collective-permute-done), channel_id=1, source_target_pairs={{0,4},{4,8},{8,12},{12,14},{14,10},{10,6},{6,2},{2,0},{1,5},{5,9},... | collective-permute-start | bytes 1622024 | tf_op jit(solution)/shard_map/ppermute | solution.py:955
  25.7 29.6 %collective-permute-start.3 = (bf16[64,4224]{1,0:T(8,128)(2,1)}, bf16[64,4224]{1,0:T(8,128)(2,1)S(1)}, u32[]{:S(2)}, u32[]{:S(2)}) collective-permute-start(bf16[64,4224]{1,0:T(8,128)(2,1)} %collective-permute-done.1), channel_id=1, source_target_pairs={{0,2},{4,0},{8,4},{12,8},{14,12},{10,14},{6,10},{2,6},{1,3},{5,1},... | collective-permute-start | bytes 1622024 | tf_op jit(solution)/shard_map/ppermute | solution.py:955
  45.2 35.0 %collective-permute-start.18 = (bf16[64,8192]{1,0:T(8,128)(2,1)}, bf16[64,8192]{1,0:T(8,128)(2,1)S(1)}, u32[]{:S(2)}, u32[]{:S(2)}) collective-permute-start(bf16[64,8192]{1,0:T(8,128)(2,1)} %collective-permute-done.6), channel_id=1, source_target_pairs={{0,1},{1,0},{2,3},{3,2},{4,5},{5,4},{6,7},{7,6},{8,9},{9,8},{10,11... | collective-permute-start | bytes 3145736 | tf_op jit(solution)/shard_map/ppermute | solution.py:939
  45.2 35.1 %collective-permute-start.19 = (bf16[64,8192]{1,0:T(8,128)(2,1)}, bf16[64,8192]{1,0:T(8,128)(2,1)S(1)}, u32[]{:S(2)}, u32[]{:S(2)}) collective-permute-start(bf16[64,8192]{1,0:T(8,128)(2,1)} %collective-permute-done.7), channel_id=1, source_target_pairs={{0,1},{1,0},{2,3},{3,2},{4,5},{5,4},{6,7},{7,6},{8,9},{9,8},{10,11... | collective-permute-start | bytes 3145736 | tf_op jit(solution)/shard_map/ppermute | solution.py:939
  71.6 26.2 %collective-permute-start.8 = (bf16[64,8192]{1,0:T(8,128)(2,1)}, bf16[64,8192]{1,0:T(8,128)(2,1)S(1)}, u32[]{:S(2)}, u32[]{:S(2)}) collective-permute-start(bf16[64,8192]{1,0:T(8,128)(2,1)} %collective-permute-done.6), channel_id=1, source_target_pairs={{0,4},{4,8},{8,12},{12,14},{14,10},{10,6},{6,2},{2,0},{1,5},{5,9},... | collective-permute-start | bytes 3145736 | tf_op jit(solution)/shard_map/ppermute | solution.py:955
  78.9 21.1 %collective-permute-start.9 = (bf16[64,8192]{1,0:T(8,128)(2,1)}, bf16[64,8192]{1,0:T(8,128)(2,1)S(1)}, u32[]{:S(2)}, u32[]{:S(2)}) collective-permute-start(bf16[64,8192]{1,0:T(8,128)(2,1)} %collective-permute-done.7), channel_id=1, source_target_pairs={{0,2},{4,0},{8,4},{12,8},{14,12},{10,14},{6,10},{2,6},{1,3},{5,1},... | collective-permute-start | bytes 3145736 | tf_op jit(solution)/shard_map/ppermute | solution.py:955
  80.1 22.6 %collective-permute-start.12 = (bf16[512,4224]{1,0:T(8,128)(2,1)S(1)}, bf16[512,4224]{1,0:T(8,128)(2,1)S(1)}, u32[]{:S(2)}, u32[]{:S(2)}) collective-permute-start(bf16[512,4224]{1,0:T(8,128)(2,1)S(1)} %constant_dynamic-update-slice_fusion.own_ref), channel_id=1, source_target_pairs={{0,1},{1,0},{2,3},{3,2},{4,5},{5,4},{6,7},{7,6},{8,9},{9,8},{10,11... | collective-permute-start | bytes 12976136 | tf_op jit(solution)/shard_map/ppermute | solution.py:939
  102.7 25.3 %collective-permute-start.13 = (bf16[64,8192]{1,0:T(8,128)(2,1)S(1)}, bf16[64,8192]{1,0:T(8,128)(2,1)S(1)}, u32[]{:S(2)}, u32[]{:S(2)}) collective-permute-start(bf16[64,8192]{1,0:T(8,128)(2,1)S(1)} %collective-permute-done.8), channel_id=1, source_target_pairs={{0,4},{4,8},{8,12},{12,14},{14,10},{10,6},{6,2},{2,0},{1,5},{5,9},... | collective-permute-start | bytes 3145736 | tf_op jit(solution)/shard_map/ppermute | solution.py:955
  104.3 25.2 %collective-permute-start.14 = (bf16[64,8192]{1,0:T(8,128)(2,1)S(1)}, bf16[64,8192]{1,0:T(8,128)(2,1)S(1)}, u32[]{:S(2)}, u32[]{:S(2)}) collective-permute-start(bf16[64,8192]{1,0:T(8,128)(2,1)S(1)} %collective-permute-done.9), channel_id=1, source_target_pairs={{0,2},{4,0},{8,4},{12,8},{14,12},{10,14},{6,10},{2,6},{1,3},{5,1},... | collective-permute-start | bytes 3145736 | tf_op jit(solution)/shard_map/ppermute | solution.py:955
  168.2 62.1 %collective-permute-start.28 = (bf16[256,1024]{1,0:T(8,128)(2,1)S(1)}, bf16[256,1024]{1,0:T(8,128)(2,1)S(1)}, u32[]{:S(2)}, u32[]{:S(2)}) collective-permute-start(bf16[256,1024]{1,0:T(8,128)(2,1)S(1)} %feed_forward.6), channel_id=1, source_target_pairs={{0,16},{1,17},{2,18},{3,19},{4,20},{5,21},{6,22},{7,23},{8,24},{9,... | collective-permute-start | bytes 1572872 | tf_op jit(solution)/shard_map/ppermute | solution.py:521
  229.0 27.3 %collective-permute-start.27 = (bf16[256,1024]{1,0:T(8,128)(2,1)S(1)}, bf16[256,1024]{1,0:T(8,128)(2,1)S(1)}, u32[]{:S(2)}, u32[]{:S(2)}) collective-permute-start(bf16[256,1024]{1,0:T(8,128)(2,1)S(1)} %get-tuple-element.322), channel_id=1, source_target_pairs={{16,0},{17,1},{18,2},{19,3},{20,4},{21,5},{22,6},{23,7},{24,8},{25... | collective-permute-start | bytes 1572872 | tf_op jit(solution)/shard_map/ppermute | solution.py:521
  259.1 20.6 %collective-permute-start.33 = (bf16[512,2048]{1,0:T(8,128)(2,1)S(1)}, bf16[512,2048]{1,0:T(8,128)(2,1)}, u32[]{:S(2)}, u32[]{:S(2)}) collective-permute-start(bf16[512,2048]{1,0:T(8,128)(2,1)S(1)} %bitcast.98), channel_id=1, source_target_pairs={{0,1},{1,0},{2,3},{3,2},{4,5},{5,4},{6,7},{7,6},{8,9},{9,8},{10,11... | collective-permute-start | bytes 6291464 | tf_op jit(solution)/shard_map/ppermute | solution.py:939
  259.1 20.6 %collective-permute-start.34 = (bf16[512,2048]{1,0:T(8,128)(2,1)}, bf16[512,2048]{1,0:T(8,128)(2,1)}, u32[]{:S(2)}, u32[]{:S(2)}) collective-permute-start(bf16[512,2048]{1,0:T(8,128)(2,1)} %get-tuple-element.363.refs_12_.refs_13_), channel_id=1, source_target_pairs={{0,1},{1,0},{2,3},{3,2},{4,5},{5,4},{6,7},{7,6},{8,9},{9,8},{10,11... | collective-permute-start | bytes 6291464 | tf_op jit(solution)/shard_map/ppermute | solution.py:939
  292.6 26.5 %collective-permute-start.37 = (bf16[256,4224]{1,0:T(8,128)(2,1)}, bf16[256,4224]{1,0:T(8,128)(2,1)}, u32[]{:S(2)}, u32[]{:S(2)}) collective-permute-start(bf16[256,4224]{1,0:T(8,128)(2,1)} %get-tuple-element.444.grad_ref.refs_4_), channel_id=1, source_target_pairs={{0,1},{1,0},{2,3},{3,2},{4,5},{5,4},{6,7},{7,6},{8,9},{9,8},{10,11... | collective-permute-start | bytes 6488072 | tf_op jit(solution)/shard_map/ppermute | solution.py:939
  292.6 26.5 %collective-permute-start.31 = (bf16[256,2048]{1,0:T(8,128)(2,1)}, bf16[256,2048]{1,0:T(8,128)(2,1)}, u32[]{:S(2)}, u32[]{:S(2)}) collective-permute-start(bf16[256,2048]{1,0:T(8,128)(2,1)} %get-tuple-element.400.refs_8_), channel_id=1, source_target_pairs={{0,1},{1,0},{2,3},{3,2},{4,5},{5,4},{6,7},{7,6},{8,9},{9,8},{10,11... | collective-permute-start | bytes 3145736 | tf_op jit(solution)/shard_map/ppermute | solution.py:939
  293.1 26.0 %collective-permute-start.32 = (bf16[256,2048]{1,0:T(8,128)(2,1)}, bf16[256,2048]{1,0:T(8,128)(2,1)}, u32[]{:S(2)}, u32[]{:S(2)}) collective-permute-start(bf16[256,2048]{1,0:T(8,128)(2,1)} %get-tuple-element.404.refs_12_), channel_id=1, source_target_pairs={{0,1},{1,0},{2,3},{3,2},{4,5},{5,4},{6,7},{7,6},{8,9},{9,8},{10,11... | collective-permute-start | bytes 3145736 | tf_op jit(solution)/shard_map/ppermute | solution.py:939
  422.7 20.9 %collective-permute-start.58 = (bf16[64,4224]{1,0:T(8,128)(2,1)S(1)}, bf16[64,4224]{1,0:T(8,128)(2,1)S(1)}, u32[]{:S(2)}, u32[]{:S(2)}) collective-permute-start(bf16[64,4224]{1,0:T(8,128)(2,1)S(1)} %get-tuple-element.501), channel_id=1, source_target_pairs={{0,4},{4,8},{8,12},{12,14},{14,10},{10,6},{6,2},{2,0},{1,5},{5,9},... | collective-permute-start | bytes 1622024 | tf_op jit(solution)/shard_map/ppermute | solution.py:955
  424.2 21.1 %collective-permute-start.59 = (bf16[64,4224]{1,0:T(8,128)(2,1)S(1)}, bf16[64,4224]{1,0:T(8,128)(2,1)S(1)}, u32[]{:S(2)}, u32[]{:S(2)}) collective-permute-start(bf16[64,4224]{1,0:T(8,128)(2,1)S(1)} %get-tuple-element.500), channel_id=1, source_target_pairs={{0,2},{4,0},{8,4},{12,8},{14,12},{10,14},{6,10},{2,6},{1,3},{5,1},... | collective-permute-start | bytes 1622024 | tf_op jit(solution)/shard_map/ppermute | solution.py:955
  424.8 29.3 %collective-permute-start.61 = (f32[16,1792]{1,0:T(8,128)S(1)}, f32[16,1792]{1,0:T(8,128)S(1)}, u32[]{:S(2)}, u32[]{:S(2)}) collective-permute-start(f32[16,1792]{1,0:T(8,128)S(1)} %add.296), channel_id=1, source_target_pairs={{0,2},{2,0},{4,6},{6,4},{8,10},{10,8},{12,14},{14,12},{1,3},{3,1},... | collective-permute-start | bytes 344072 | tf_op jit(solution)/shard_map/ppermute | solution.py:1056
  434.1 23.3 %collective-permute-start.74 = (bf16[64,4096]{1,0:T(8,128)(2,1)S(1)}, bf16[64,4096]{1,0:T(8,128)(2,1)S(1)}, u32[]{:S(2)}, u32[]{:S(2)}) collective-permute-start(bf16[64,4096]{1,0:T(8,128)(2,1)S(1)} %get-tuple-element.505), channel_id=1, source_target_pairs={{0,4},{4,8},{8,12},{12,14},{14,10},{10,6},{6,2},{2,0},{1,5},{5,9},... | collective-permute-start | bytes 1572872 | tf_op jit(solution)/shard_map/ppermute | solution.py:955
  435.6 21.8 %collective-permute-start.75 = (bf16[64,4096]{1,0:T(8,128)(2,1)S(1)}, bf16[64,4096]{1,0:T(8,128)(2,1)S(1)}, u32[]{:S(2)}, u32[]{:S(2)}) collective-permute-start(bf16[64,4096]{1,0:T(8,128)(2,1)S(1)} %get-tuple-element.504), channel_id=1, source_target_pairs={{0,2},{4,0},{8,4},{12,8},{14,12},{10,14},{6,10},{2,6},{1,3},{5,1},... | collective-permute-start | bytes 1572872 | tf_op jit(solution)/shard_map/ppermute | solution.py:955
  (131 other events, 2423.4 us)
